TPU v7x, 128 devices: a whole 4x4x4 slice. The times are simulated.
128 devices in a mesh: row: 32 (over z, y, x_hi), col: 4 (over x_lo, core).
Axes of the slice: x: 4 (x_hi: 2, x_lo: 2; x = x_hi * 2 + x_lo), y: 4, z: 4, core: 2. Of those that a mesh axis runs over, the one named last changes fastest.
Arguments:
- pair_block: bfloat16 [2048, 2048, 128], P('row', 'col'), may hold values from -6 to 6
- left_panel: bfloat16 [2048, 64, 128], P('row', 'col'), may hold values from -6 to 6
- right_panel: bfloat16 [2048, 64, 128], P('row', 'col'), may hold values from -6 to 6
- ln_gain: float32 [128], replicated, may hold values from 0.1 to 1.9
- ln_bias: float32 [128], replicated, may hold values from -3 to 3
- w_left: bfloat16 [128, 256], replicated, may hold values from -0.5 to 0.5
- w_right: bfloat16 [128, 256], replicated, may hold values from -0.5 to 0.5
- w_gate: bfloat16 [128, 128], replicated, may hold values from -0.5 to 0.5
- out_gain: float32 [128], replicated, may hold values from 0.1 to 1.9
- out_bias: float32 [128], replicated, may hold values from -3 to 3
- w_out: bfloat16 [128, 128], replicated, may hold values from -0.5 to 0.5
Outputs:
- update: bfloat16 [2048, 2048, 128], P('row', 'col')
All inputs are finite; a program needn't handle non-finite values.
Results may differ from a plain program's by a relative error of at most 0.0065.
Values may be sent and summed in bfloat16 or wider, within the bound.
No kernel may reach another device: no remote copies, remote signals or barrier semaphores. Data moves between devices by JAX's collectives and lax.ppermute only.
A program may use at most 192 MiB of HBM per device.

v0:
```python
import jax
import jax.numpy as jnp
from jax import lax
from jax.sharding import PartitionSpec as P


def layer_norm(values, gain, bias):
    values = values.astype(jnp.float32)
    mean = jnp.mean(values, axis=-1, keepdims=True)
    centered = values - mean
    var = jnp.mean(centered * centered, axis=-1, keepdims=True)
    return centered / jnp.sqrt(var + 1e-05) * gain + bias


def project_panel(panel, weight, ln_gain, ln_bias):
    normed = layer_norm(panel, ln_gain, ln_bias).astype(jnp.bfloat16)
    proj = jnp.einsum("rkc,ch->rkh", normed, weight, preferred_element_type=jnp.float32)
    half = weight.shape[1] // 2
    return (jax.nn.sigmoid(proj[..., :half]) * proj[..., half:]).astype(jnp.bfloat16)


def per_device(
    pair_block,
    left_panel,
    right_panel,
    ln_gain,
    ln_bias,
    w_left,
    w_right,
    w_gate,
    out_gain,
    out_bias,
    w_out,
):
    left = project_panel(left_panel, w_left, ln_gain, ln_bias)
    right = project_panel(right_panel, w_right, ln_gain, ln_bias)
    left_all, right_rows = (
        lax.all_gather(left, "col", axis=1, tiled=True),
        lax.all_gather(right, "col", axis=1, tiled=True),
    )
    per_block = lax.axis_size("row") // lax.axis_size("col")
    column = lax.axis_index("col")
    every = lax.all_gather(right_rows, "row", axis=0, tiled=True)
    width = right_rows.shape[0] * per_block
    needed = lax.dynamic_slice_in_dim(every, column * width, width, 0)
    product = jnp.einsum("ikh,jkh->ijh", left_all, needed, preferred_element_type=jnp.float32)
    normed = layer_norm(product, out_gain, out_bias).astype(jnp.bfloat16)
    norm_pair = layer_norm(pair_block, ln_gain, ln_bias).astype(jnp.bfloat16)
    gate = jax.nn.sigmoid(
        jnp.einsum("ijc,cd->ijd", norm_pair, w_gate, preferred_element_type=jnp.float32)
    )
    output = jnp.einsum("ijh,hc->ijc", normed, w_out, preferred_element_type=jnp.float32)
    return (gate * output).astype(jnp.bfloat16)


def solution(mesh):
    in_specs = (
        P("row", "col", None),
        P("row", "col", None),
        P("row", "col", None),
        P(),
        P(),
        P(),
        P(),
        P(),
        P(),
        P(),
        P(),
    )
    out_specs = P("row", "col", None)
    return jax.shard_map(
        per_device, mesh=mesh, in_specs=in_specs, out_specs=out_specs, check_vma=False
    )
```

profile of v0, /device:TPU:0, one launch (start us, length us, event | category | flops | bytes accessed | tf_op | source)
XLA Modules:
  0.0 399.0 jit_solution(17797707447988023090)
XLA Ops:
  6.5 0.0 all-gather.4.cloned.1.call-start
  6.6 1.2 convert_reduce_fusion.2
  7.8 1.3 fusion.21
  9.1 1.4 fusion.33
  10.6 0.8 fusion.29
  11.4 0.0 all-gather.4.cloned.1.call-update
  11.4 0.0 all-gather.8.cloned.1.call-start
  11.5 1.2 convert_reduce_fusion.1
  12.7 1.3 fusion.17
  14.0 1.4 fusion.35
  15.5 0.8 fusion.25
  16.3 0.0 all-gather.6.cloned.1.call-start
  16.4 17.9 %all-gather.4.cloned.1.call-done = bf16[64,64,128]{2,1,0:T(8,128)(2,1)} async-done(((bf16[64,16,128]{2,1,0:T(8,128)(2,1)}), bf16[64,64,128]{2,1,0:T(8,128)(2,1)}) %all-gather.4.cloned.1.call-update) | async-done | bytes 1048592 | tf_op jit(solution)/shard_map/all_gather | solution.py:39
  34.3 5.7 %convert_reduce_fusion = f32[64,512]{1,0:T(8,128)S(1)} fusion(bf16[64,512,128]{2,1,0:T(8,128)(2,1)} %param.11), kind=kLoop, calls=%fused_computation.1 | loop fusion | flops 8355840 | bytes 8519680 | tf_op jit(solution)/shard_map/reduce_sum | solution.py:9
  40.0 10.9 %fusion.2 = f32[64,512]{1,0:T(8,128)S(1)} fusion(bf16[64,512,128]{2,1,0:T(8,128)(2,1)} %param.11, f32[64,512]{1,0:T(8,128)S(1)} %broadcast_multiply_fusion.1), kind=kLoop, calls=%fused_computation.4 | loop fusion | flops 16744448 | bytes 8650752 | tf_op jit(solution)/shard_map/reduce_sum | solution.py:11
  51.0 15.2 %fusion.6 = f32[64,512,128]{2,1,0:T(8,128)} fusion(bf16[64,512,128]{2,1,0:T(8,128)(2,1)} %param.11, f32[128]{0:T(128)S(1)} %copy-done.6, f32[128]{0:T(128)S(1)} %copy-done.7, f32[64,512]{1,0:T(8,128)S(1)} %add_sqrt_fusion.1, f32[64,512]{1,0:T(8,128)S(1)} %broadcast_multiply_fusion.1, bf16[128,128]{1,0:T(8,128)(2,1)S(1)} %copy-done.4), kind=kOutput, calls=%fused_computation.13 | convolution fusion | flops 1098907648 | bytes 25461760 | tf_op jit(solution)/shard_map/ijc,cd->ijd/dot_general | solution.py:50
  66.2 4.7 %copy.16 = bf16[64,64,128]{0,1,2:T(8,128)(2,1)S(1)} copy(bf16[64,64,128]{2,1,0:T(8,128)(2,1)} %all-gather.8.cloned.1.call-done) | data formatting | bytes 2097152 | tf_op jit(solution)/shard_map/all_gather | solution.py:38
  70.9 254.7 %all-gather.6.cloned.1.call-done = bf16[2048,64,128]{2,1,0:T(8,128)(2,1)} async-done(((bf16[64,64,128]{2,1,0:T(8,128)(2,1)}), bf16[2048,64,128]{2,1,0:T(8,128)(2,1)}) %all-gather.6.cloned.1.call-update) | async-done | bytes 33554448 | tf_op jit(solution)/shard_map/all_gather | solution.py:43
  325.6 8.8 %constant_dynamic-slice_fusion = bf16[512,64,128]{2,1,0:T(8,128)(2,1)} fusion(bf16[2048,64,128]{2,1,0:T(8,128)(2,1)} %all-gather.6.cloned.1.call-done, s32[]{:T(128)S(6)} %select_n.3), kind=kLoop, calls=%fused_computation.69 | loop fusion | bytes 16777220 | tf_op jit(solution)/shard_map/dynamic_slice | solution.py:45
  334.5 13.4 %copy.18 = bf16[512,64,128]{0,1,2:T(8,128)(2,1)} copy(bf16[512,64,128]{2,1,0:T(8,128)(2,1)} %constant_dynamic-slice_fusion) | data formatting | bytes 16777216
  347.9 11.5 %bitcast_reduce_fusion = (f32[64,512]{1,0:T(8,128)S(1)}, f32[128,512,64]{1,2,0:T(8,128)}) fusion(bf16[512,64,128]{0,1,2:T(8,128)(2,1)} %copy.18, bf16[64,64,128]{0,1,2:T(8,128)(2,1)S(1)} %copy.16), kind=kOutput, calls=%fused_computation.9 | convolution fusion | flops 541032448 | bytes 26345472 | tf_op jit(solution)/shard_map/ikh,jkh->ijh/dot_general | solution.py:46
  359.4 7.9 %multiply_reduce_fusion = f32[64,512]{1,0:T(8,128)S(1)} fusion(f32[128,512,64]{1,2,0:T(8,128)} %get-tuple-element.6, f32[64,512]{1,0:T(8,128)S(1)} %broadcast_multiply_fusion), kind=kLoop, calls=%fused_computation.12 | loop fusion | flops 12550144 | bytes 17039360 | tf_op jit(solution)/shard_map/reduce_sum | solution.py:11
  367.4 8.4 %add_convert_fusion = bf16[64,512,128]{1,0,2:T(8,128)(2,1)S(1)} fusion(f32[128,512,64]{1,2,0:T(8,128)} %get-tuple-element.6, f32[128]{0:T(128)S(1)} %copy-done.2, f32[128]{0:T(128)S(1)} %copy-done.3, f32[64,512]{1,0:T(8,128)S(1)} %add_sqrt_fusion, f32[64,512]{1,0:T(8,128)S(1)} %broadcast_multiply_fusion), kind=kLoop, calls=%fused_computation.11 | loop fusion | flops 20971520 | bytes 25428992 | tf_op jit(solution)/shard_map/convert_element_type | solution.py:47
  375.8 16.7 %multiply_convert_fusion = bf16[64,512,128]{2,1,0:T(8,128)(2,1)} fusion(f32[64,512,128]{2,1,0:T(8,128)} %fusion.6, bf16[64,512,128]{1,0,2:T(8,128)(2,1)S(1)} %add_convert_fusion, bf16[128,128]{1,0:T(8,128)(2,1)S(1)} %copy-done.5), kind=kOutput, calls=%fused_computation.10 | convolution fusion | flops 1094713344 | bytes 33587200 | tf_op jit(solution)/shard_map/ijh,hc->ijc/dot_general | solution.py:52
  (27 shorter events, 0.2 us)
Async XLA Ops:
  6.5 2.6 copy-start
  6.5 44.4 %copy-start.7 = (f32[128]{0:T(128)S(1)}, f32[128]{0:T(128)}, u32[]{:S(2)}) copy-start(f32[128]{0:T(128)} %param.14) | copy-start | bytes 1540
  6.5 44.4 %copy-start.6 = (f32[128]{0:T(128)S(1)}, f32[128]{0:T(128)}, u32[]{:S(2)}) copy-start(f32[128]{0:T(128)} %param.15) | copy-start | bytes 1540
  6.5 44.4 %copy-start.4 = (bf16[128,128]{1,0:T(8,128)(2,1)S(1)}, bf16[128,128]{1,0:T(8,128)(2,1)}, u32[]{:S(2)}) copy-start(bf16[128,128]{1,0:T(8,128)(2,1)} %param.18) | copy-start | bytes 98308
  6.5 27.7 %all-gather.4.cloned.1.call-start = ((), (), s32[]{:S(2)}) async-start(), calls=%async_computation | async-start | bytes 1310720 | tf_op jit(solution)/shard_map/all_gather | solution.py:39
  11.4 54.8 %all-gather.8.cloned.1.call-start = ((), (), s32[]{:S(2)}) async-start(), calls=%async_computation.2 | async-start | bytes 1310720 | tf_op jit(solution)/shard_map/all_gather | solution.py:38
  16.3 309.3 %all-gather.6.cloned.1.call-start = ((), (), s32[]{:S(2)}) async-start(), calls=%async_computation.1 | async-start | bytes 34603008 | tf_op jit(solution)/shard_map/all_gather | solution.py:43
  347.9 19.5 %copy-start.2 = (f32[128]{0:T(128)S(1)}, f32[128]{0:T(128)}, u32[]{:S(2)}) copy-start(f32[128]{0:T(128)} %param.20) | copy-start | bytes 1540
  347.9 19.5 %copy-start.3 = (f32[128]{0:T(128)S(1)}, f32[128]{0:T(128)}, u32[]{:S(2)}) copy-start(f32[128]{0:T(128)} %param.19) | copy-start | bytes 1540
  367.3 8.5 %copy-start.5 = (bf16[128,128]{1,0:T(8,128)(2,1)S(1)}, bf16[128,128]{1,0:T(8,128)(2,1)}, u32[]{:S(2)}) copy-start(bf16[128,128]{1,0:T(8,128)(2,1)} %param.21) | copy-start | bytes 98308
  375.8 16.7 %copy-start.1 = (bf16[128,256]{1,0:T(8,128)(2,1)S(1)}, bf16[128,256]{1,0:T(8,128)(2,1)}, u32[]{:S(2)}) copy-start(bf16[128,256]{1,0:T(8,128)(2,1)} %param.17) | copy-start | bytes 196612
Sparse Core Ops, SparseCore 0:
  11.6 22.6 all-gather.3
  35.9 22.0 all-gather.7
  61.2 264.4 all-gather.5
where the time goes:
time: 400 us; the launch traced here: 399 us
  waiting for transfers between devices  273 us (68%)
  matrix products  46.3 us (12%)
  other arithmetic  39.7 us (10%)
  local copies, waits for them, and re-layouts  27 us (7%)
  between operations  13.3 us (3%)
    all_gather x1, waiting for transfers between devices, per_device(): every = lax.all_gather(right_rows, 'row', axis=0, tiled=True)  255 us
    reduce_sum x4, other arithmetic, layer_norm(): var = jnp.mean(centered * centered, axis=-1, keepdims=True)  21.5 us
    all_gather x1, waiting for transfers between devices, per_device(): lax.all_gather(right, 'col', axis=1, tiled=True)  17.9 us
    dot_general x1, matrix products, per_device(): jnp.einsum('ijh,hc->ijc', normed, w_out, preferred_element_type=jnp.float32)  16.7 us
    dot_general x1, matrix products, per_device(): jnp.einsum('ijc,cd->ijd', norm_pair, w_gate, preferred_element_type=jnp.f...  15.2 us
    unnamed x17, local copies, waits for them, and re-layouts  13.5 us
    dot_general x1, matrix products, per_device(): jnp.einsum('ikh,jkh->ijh', left_all, needed, preferred_element_type=jnp.f...  11.5 us
    dynamic_slice x1, local copies, waits for them, and re-layouts, per_device(): needed = lax.dynamic_slice_in_dim(every, column * width, width, 0)  8.81 us
  transfers between devices with their start and end apart: 3, of which 2 were waited for; matrix products, arithmetic and copies ran while one was open for 10% of the time, Pallas kernels for 0%

commit v1 on v0

v1 whole, which is shorter than its diff:
```python
import functools

import jax
import jax.numpy as jnp
import numpy as np
from jax import lax
from jax.experimental import pallas as pl
from jax.experimental.pallas import tpu as pltpu
from jax.sharding import PartitionSpec as P

AXES = ("row", "col")
BF16, F32 = jnp.bfloat16, jnp.float32
DEVICES = [(z, y, x, c) for z in range(4) for y in range(4) for x in range(2) for c in range(4)]
MIB = 1 << 20


def device_id(z, y, x, c):
    return (((z % 4) * 4 + y % 4) * 2 + x % 2) * 4 + c


def move(value, dz=0, dy=0, dx=0):
    pairs = [(device_id(z, y, x, c), device_id(z + dz, y + dy, x + dx, c)) for z, y, x, c in DEVICES]
    return lax.ppermute(value, AXES, pairs)


def layer_norm(values, gain, bias):
    mean = jnp.mean(values, axis=-1, keepdims=True)
    centered = values - mean
    var = jnp.mean(centered * centered, axis=-1, keepdims=True)
    return centered * lax.rsqrt(var + 1e-05) * gain + bias


def sigmoid(values):
    return 0.5 * jnp.tanh(0.5 * values) + 0.5


def hidden_order():
    order = []
    for group in range(32):
        first = 2 * group
        order += [first, first + 64, first + 1, first + 65]
    return np.array(order)


def project_16(normed, weight, swap, store):
    proj = lax.dot_general(
        weight, normed.reshape(16 * 64, 128), (((0,), (1,)), ((), ())), preferred_element_type=F32
    )
    value = (sigmoid(proj[:128]) * proj[128:]).astype(BF16).astype(F32)
    low, high = value[:64], value[64:]
    lane = lax.broadcasted_iota(jnp.int32, (64, 128), 1)
    for pair in range(8):
        lo = low[:, pair * 128 : (pair + 1) * 128]
        hi = high[:, pair * 128 : (pair + 1) * 128]
        swap[:, 2 * pair, :] = jnp.where(lane < 64, lo, pltpu.roll(hi, 64, 1))
        swap[:, 2 * pair + 1, :] = jnp.where(lane < 64, pltpu.roll(lo, 64, 1), hi)
    for h in range(64):
        store(h, swap[h].astype(BF16))


def right_kernel(z_ref, p0, p1, p2, p3, gain, bias, weight, a_ref, b_ref, normed, swap):
    z = z_ref[0]
    for s, piece in enumerate((p0, p1, p2, p3)):
        start = pl.multiple_of(lax.rem(z - s + 4, 4) * 16, 16)
        normed[:, pl.ds(start, 16), :] = layer_norm(
            piece[...].astype(F32), gain[...], bias[...]
        ).astype(BF16)

    def store(h, tile):
        ref = a_ref if h < 32 else b_ref
        ref[:, (h % 32) * 128 : (h % 32 + 1) * 128] = tile

    project_16(normed[...], weight[...], swap, store)


def left_kernel(left, gain, bias, weight, spread, out, normed, swap, rows):
    for quarter in range(4):
        at = slice(quarter * 16, quarter * 16 + 16)
        for c in range(4):
            normed[:, c * 16 : (c + 1) * 16, :] = layer_norm(
                left[c, at].astype(F32), gain[...], bias[...]
            ).astype(BF16)

        def store(h, tile, at=at):
            rows[at, h * 128 : (h + 1) * 128] = tile

        project_16(normed[...], weight[...], swap, store)
    row = lax.broadcasted_iota(jnp.int32, (256, 256), 0)
    lane = lax.broadcasted_iota(jnp.int32, (256, 256), 1)
    keep = lax.rem(row, 4) == lane // 64

    def body(g, carry):
        tile = rows[:, pl.ds(pl.multiple_of(g * 256, 256), 256)]
        wide = jnp.dot(spread[...], tile, preferred_element_type=F32)
        out[g] = jnp.where(keep, wide, 0.0).astype(BF16)
        return carry

    lax.fori_loop(0, 32, body, 0)


def gate_kernel(pair, gain, bias, weight, out):
    def body(n, carry):
        i, j = n // 2, pl.multiple_of(lax.rem(n, 2) * 256, 256)
        values = pair[i, pl.ds(j, 256), :].astype(F32)
        normed = layer_norm(values, gain[...], bias[...]).astype(BF16)
        proj = jnp.dot(normed, weight[...], preferred_element_type=F32)
        out[i, pl.ds(j, 256), :] = sigmoid(proj).astype(BF16)
        return carry

    lax.fori_loop(0, pair.shape[0] * 2, body, 0)


def update_kernel(tiles, n_src, has_out, *refs):
    joff = refs[0]
    sources = refs[1 : 1 + n_src]
    gate, lbd, wide_out, gain, bias = refs[1 + n_src : 6 + n_src]
    refs = refs[6 + n_src + has_out :]
    out, right, product, gates, results, gate_sem, out_sem = refs

    def gate_copy(t, b):
        start = pl.multiple_of(joff[t * 8 + b], 16)
        return pltpu.make_async_copy(
            gate.at[:, pl.ds(start, 16), :], gates.at[t, :, pl.ds(b * 16, 16), :], gate_sem.at[t, b]
        )

    def out_copy(t, b):
        start = pl.multiple_of(joff[t * 8 + b], 16)
        return pltpu.make_async_copy(
            results.at[t, :, pl.ds(b * 16, 16), :], out.at[:, pl.ds(start, 16), :], out_sem.at[t, b]
        )

    for t, tile in enumerate(tiles):
        for b in range(len(tile)):
            gate_copy(t, b).start()
    member = lax.broadcasted_iota(jnp.int32, (8, 128), 0)

    def over_four(total):
        swapped = jnp.where(lax.rem(member, 2) == 0, pltpu.roll(total, 7, 0), pltpu.roll(total, 1, 0))
        total = total + swapped
        swapped = jnp.where(lax.rem(member, 4) < 2, pltpu.roll(total, 6, 0), pltpu.roll(total, 2, 0))
        return total + swapped

    for t, tile in enumerate(tiles):
        for b in range(8):
            for half, (src, row, lane) in enumerate(tile[min(b, len(tile) - 1)]):
                right[b * 16 : b * 16 + 16, half * 4096 : half * 4096 + 4096] = sources[src][
                    row : row + 16, lane : lane + 4096
                ]

        def multiply(g, carry):
            panel = right[:, pl.ds(pl.multiple_of(g * 256, 256), 256)]
            made = lax.dot_general(
                lbd[g], panel, (((1,), (1,)), ((), ())), preferred_element_type=F32
            )
            product[:, g] = made.reshape(32, 8, 128)
            return carry

        lax.fori_loop(0, 32, multiply, 0, unroll=2)
        for b in range(len(tile)):
            gate_copy(t, b).wait()

        def finish(ip, carry):
            values = product[ip]
            mean = over_four(jnp.sum(values, axis=0)) * (1.0 / 128)
            centered = values - mean[None]
            var = over_four(jnp.sum(centered * centered, axis=0)) * (1.0 / 128)
            normed = centered * lax.rsqrt(var + 1e-05)[None] * gain[...] + bias[...]
            normed = normed.reshape(256, 128).astype(BF16)
            both = lax.dot_general(
                normed, wide_out[...], (((0,), (0,)), ((), ())), preferred_element_type=F32
            )
            for i2 in range(2):
                row = 2 * ip + i2
                results[t, row] = (
                    both[:, i2 * 128 : (i2 + 1) * 128] * gates[t, row].astype(F32)
                ).astype(BF16)
            return carry

        lax.fori_loop(0, 32, finish, 0, unroll=2)
        for b in range(len(tile)):
            out_copy(t, b).start()
    for t, tile in enumerate(tiles):
        for b in range(len(tile)):
            out_copy(t, b).wait()


VMEM = pl.BlockSpec(memory_space=pltpu.VMEM)
SMEM = pl.BlockSpec(memory_space=pltpu.SMEM)
ANY = pl.BlockSpec(memory_space=pl.ANY)


def run_update(tiles, joff, sources, gate, lbd, wide_out, gain, bias, before):
    n = len(tiles)
    has_out = before is not None
    args = [joff, *sources, gate, lbd, wide_out, gain, bias] + ([before] if has_out else [])
    specs = [SMEM] + [VMEM] * len(sources) + [ANY, VMEM, VMEM, VMEM, VMEM] + [ANY] * has_out
    shape = gate.shape
    return pl.pallas_call(
        functools.partial(update_kernel, tiles, len(sources), has_out),
        out_shape=jax.ShapeDtypeStruct(shape, BF16),
        in_specs=specs,
        out_specs=ANY,
        scratch_shapes=[
            pltpu.VMEM((128, 8192), BF16),
            pltpu.VMEM((32, 32, 8, 128), F32),
            pltpu.VMEM((n, 64, 128, 128), BF16),
            pltpu.VMEM((n, 64, 128, 128), BF16),
            pltpu.SemaphoreType.DMA((n, 8)),
            pltpu.SemaphoreType.DMA((n, 8)),
        ],
        input_output_aliases={len(args) - 1: 0} if has_out else {},
        compiler_params=pltpu.CompilerParams(vmem_limit_bytes=48 * MIB),
        cost_estimate=pl.CostEstimate(
            flops=n * 3 * 10**9, bytes_accessed=n * 6 * MIB, transcendentals=0
        ),
    )(*args)


def run_right(z, pieces, gain, bias, weight):
    return pl.pallas_call(
        right_kernel,
        out_shape=[jax.ShapeDtypeStruct((16, 4096), BF16)] * 2,
        in_specs=[SMEM] + [VMEM] * 7,
        out_specs=[VMEM] * 2,
        scratch_shapes=[pltpu.VMEM((16, 64, 128), BF16), pltpu.VMEM((64, 16, 128), F32)],
        compiler_params=pltpu.CompilerParams(vmem_limit_bytes=16 * MIB),
    )(z.reshape(1), *pieces, gain, bias, weight)


def run_left(left, gain, bias, weight):
    spread = np.zeros((256, 64), np.float32)
    spread[np.arange(256), np.arange(256) // 4] = 1
    return pl.pallas_call(
        left_kernel,
        out_shape=jax.ShapeDtypeStruct((32, 256, 256), BF16),
        in_specs=[VMEM] * 5,
        out_specs=VMEM,
        scratch_shapes=[
            pltpu.VMEM((16, 64, 128), BF16),
            pltpu.VMEM((64, 16, 128), F32),
            pltpu.VMEM((64, 8192), BF16),
        ],
        compiler_params=pltpu.CompilerParams(vmem_limit_bytes=24 * MIB),
        cost_estimate=pl.CostEstimate(flops=4 * 10**9, bytes_accessed=5 * MIB, transcendentals=0),
    )(left, gain, bias, weight, jnp.asarray(spread, BF16))


def run_gate(pair, gain, bias, weight):
    rows = 8
    block = pl.BlockSpec((rows, 512, 128), lambda n: (n, 0, 0))
    whole = pl.BlockSpec((1, 128), lambda n: (0, 0))
    return pl.pallas_call(
        gate_kernel,
        out_shape=jax.ShapeDtypeStruct(pair.shape, BF16),
        grid=(pair.shape[0] // rows,),
        in_specs=[block, whole, whole, pl.BlockSpec((128, 128), lambda n: (0, 0))],
        out_specs=block,
        compiler_params=pltpu.CompilerParams(vmem_limit_bytes=16 * MIB),
        cost_estimate=pl.CostEstimate(flops=10**10, bytes_accessed=16 * MIB, transcendentals=0),
    )(pair, gain, bias, weight)


def place_a(z, y, x):
    if z == 0:
        if x == 0:
            return "GA", y * 16, 0
        return ("GA", 64, 0) if y == 0 else ("X", (y - 1) * 16, 0)
    if z in (1, 3):
        if x == 0 or y == 0:
            return f"A{z}", 64 if x else y * 16, 0
        return f"PA{z}", (y - 1) * 16, 0
    if x == 0:
        return ("PA1", 48 + y * 16, 0) if y < 3 else ("PA3", 48, 0)
    if y == 0:
        return "PA3", 64, 0
    return ("QA1", (y - 1) * 16, 0) if y < 3 else ("QA3", 0, 0)


def place_b(z, y, x):
    if y == 0:
        if x == 0:
            return "GB", z * 16, 0
        return ("GB", 64, 0) if z == 0 else ("X", (z - 1) * 16, 4096)
    if y in (1, 3):
        if x == 0 or z == 0:
            return f"B{y}", 64 if x else z * 16, 0
        return f"PB{y}", (z - 1) * 16, 0
    if x == 0:
        return ("PB1", 48 + z * 16, 0) if z < 3 else ("PB3", 48, 0)
    if z == 0:
        return "PB3", 64, 0
    return ("QB1", 0, 0) if z == 1 else ("QB3", (z - 2) * 16, 0)


LATE = [(2, 1, 1), (2, 2, 1), (2, 3, 1), (1, 2, 1), (3, 2, 1)]
EARLY = [(z, y, 0) for z in (0, 1, 3) for y in (0, 1, 3)][:8]
OTHERS = [
    (z, y, x)
    for x in range(2)
    for z in range(4)
    for y in range(4)
    if (z, y, x) not in LATE and (z, y, x) not in EARLY
]


def per_device(
    pair_block, left_panel, right_panel, ln_gain, ln_bias, w_left, w_right, w_gate, out_gain, out_bias, w_out
):
    row = lax.axis_index("row")
    z, y, x = row // 8, (row // 2) % 4, row % 2
    c = lax.axis_index("col")
    gain, bias = ln_gain.reshape(1, 128), ln_bias.reshape(1, 128)

    pieces = []
    for s in range(4):
        pairs = [(device_id(z_, y_, x_, c_), device_id(c_ + s, y_, x_, z_)) for z_, y_, x_, c_ in DEVICES]
        part = lax.dynamic_slice_in_dim(right_panel, ((c + s) % 4) * 16, 16, 0)
        pieces.append(lax.ppermute(part, AXES, pairs))
    left_all = lax.all_gather(left_panel, "col", axis=0, tiled=False)
    a, b = run_right(z.astype(jnp.int32), pieces, gain, bias, w_right)

    def cat(*parts):
        return jnp.concatenate(parts, 0)

    got = {}
    xab = move(jnp.concatenate([a, b], 1), dx=1)
    got["GA"] = cat(a, move(a, dy=-1), move(a, dy=2), move(a, dy=1), xab[:, :4096])
    got["GB"] = cat(b, move(b, dz=-1), move(b, dz=2), move(b, dz=1), xab[:, 4096:])
    got["A1"], got["A3"] = move(got["GA"], dz=-1), move(got["GA"], dz=1)
    got["B1"], got["B3"] = move(got["GB"], dy=-1), move(got["GB"], dy=1)
    other = move(jnp.concatenate([got["GA"][16:64], got["GB"][16:64]], 1), dx=1)
    got["X"] = other
    got["PA1"] = move(cat(other[:, :4096], got["A1"][:48]), dz=-1)
    got["PA3"] = move(cat(other[:, :4096], got["A3"][48:]), dz=1)
    got["PB1"] = move(cat(other[:, 4096:], got["B1"][:48]), dy=-1)
    got["PB3"] = move(cat(other[:, 4096:], got["B3"][48:]), dy=1)
    got["QA1"], got["QA3"] = move(got["PA1"][:32], dz=-1), move(got["PA3"][32:48], dz=1)
    got["QB1"], got["QB3"] = move(got["PB1"][:16], dy=-1), move(got["PB3"][16:48], dy=1)

    lbd = run_left(left_all, gain, bias, w_left)
    gate = run_gate(pair_block, gain, bias, w_gate)

    order = hidden_order()
    perm_out = w_out[order].reshape(32, 1, 4, 128)
    eye = jnp.eye(2, dtype=BF16)
    wide_out = (perm_out[:, :, :, None, :] * eye[None, :, None, :, None]).reshape(256, 256)

    def spread(vector):
        rows = jnp.broadcast_to(vector[order].reshape(32, 1, 4), (32, 2, 4)).reshape(32, 8, 1)
        return jnp.broadcast_to(rows, (32, 8, 128))

    gain_out, bias_out = spread(out_gain), spread(out_bias)

    def call(blocks, before):
        names = sorted({p(*d)[0] for d in blocks for p in (place_a, place_b)})
        tiles, joff = [], []
        for at in range(0, len(blocks), 8):
            tile = blocks[at : at + 8]
            tiles.append(
                [
                    tuple((names.index(p(*d)[0]), p(*d)[1], p(*d)[2]) for p in (place_a, place_b))
                    for d in tile
                ]
            )
            for dz, dy, dx in tile + [tile[0]] * (8 - len(tile)):
                joff.append((((y + dy) % 4) * 2 + (x + dx) % 2) * 64 + ((z + dz) % 4) * 16)
        return run_update(
            tiles,
            jnp.stack(joff).astype(jnp.int32),
            [got[n] for n in names],
            gate,
            lbd,
            wide_out,
            gain_out,
            bias_out,
            before,
        )

    out = call(EARLY, None)
    out = call(OTHERS[:16], out)
    return call(LATE + OTHERS[16:], out)


def solution(mesh):
    part = P("row", "col", None)
    in_specs = (part, part, part) + (P(),) * 8
    return jax.shard_map(per_device, mesh=mesh, in_specs=in_specs, out_specs=part, check_vma=False)
```

time: 400 us -> 209 us (0.52)
  waiting for transfers between devices: 273 us -> 18.9 us
  Pallas kernels: 0 us -> 104 us
  matrix products: 46.3 us -> 0 us
  starting transfers between devices: 0.12 us -> 42.7 us
  other arithmetic: 39.7 us -> 4.64 us
    all_gather x3 -> x1, waiting for transfers between devices: 273 us -> 0.01 us  [per_device(): left_all = lax.all_gather(left_panel, 'col', axis=0, tiled=False)]
    pallas_call x0 -> x6, Pallas kernels: none -> 104 us  [the longest x3 50.3 us: run_update(): pl.pallas_call(functools.partial(update_kernel, tiles, len(sources), has_...]
    dot_general x5 -> x0, matrix products: 46.3 us -> none  [the longest x1 16.7 us: per_device(): jnp.einsum('ijh,hc->ijc', normed, w_out, preferred_element_type=jnp.float32)]
    ppermute x0 -> x24, starting transfers between devices: none -> 42.7 us  [the longest x20 32.1 us: move(): return lax.ppermute(value, AXES, pairs)]
    reduce_sum x7 -> x0, other arithmetic: 29.5 us -> none  [the longest x4 21.5 us: layer_norm(): var = jnp.mean(centered * centered, axis=-1, keepdims=True)]
    ppermute x0 -> x24, waiting for transfers between devices: none -> 18.9 us  [the longest x20 18.9 us: move(): return lax.ppermute(value, AXES, pairs)]
    convert_element_type x3 -> x1, other arithmetic: 10.1 us -> 0.01 us  [per_device(): eye = jnp.eye(2, dtype=BF16)]
    dynamic_slice x1, local copies, waits for them, and re-layouts: 8.81 us -> 0.96 us  [per_device(): part = lax.dynamic_slice_in_dim(right_panel, (c + s) % 4 * 16, 16, 0)]
  transfers between devices with their start and end apart: 3 -> 25, of which waited for: 2 -> 6; matrix products, arithmetic and copies ran while one was open for 10% -> 6% of each run, Pallas kernels for 0% -> 44%
where the time goes in v1:
time: 209 us; the launch traced here: 208 us
  Pallas kernels  104 us (50%)
  starting transfers between devices  42.7 us (20%)
  local copies, waits for them, and re-layouts  23.5 us (11%)
  waiting for transfers between devices  18.9 us (9%)
  between operations  14.1 us (7%)
  other arithmetic  4.64 us (2%)
    pallas_call x3, Pallas kernels, run_update(): pl.pallas_call(functools.partial(update_kernel, tiles, len(sources), has_...  50.3 us
    pallas_call x1, Pallas kernels, run_gate(): pl.pallas_call(gate_kernel, out_shape=jax.ShapeDtypeStruct(pair.shape, BF...  42.9 us
    ppermute x20, starting transfers between devices, move(): return lax.ppermute(value, AXES, pairs)  32.1 us
    ppermute x20, waiting for transfers between devices, move(): return lax.ppermute(value, AXES, pairs)  18.9 us
    unnamed x58, local copies, waits for them, and re-layouts  14.8 us
    ppermute x4, starting transfers between devices, per_device(): pieces.append(lax.ppermute(part, AXES, pairs))  10.7 us
    pallas_call x1, Pallas kernels, run_left(): pl.pallas_call(left_kernel, out_shape=jax.ShapeDtypeStruct((32, 256, 256)...  9.92 us
  transfers between devices with their start and end apart: 25, of which 6 were waited for; matrix products, arithmetic and copies ran while one was open for 6% of the time, Pallas kernels for 44%

profile of v1, /device:TPU:0, one launch (start us, length us, event | category | flops | bytes accessed | tf_op | source)
XLA Modules:
  0.0 208.1 jit_solution(15183355925932922435)
XLA Ops:
  8.2 3.3 %collective-permute-start.1 = (bf16[16,16,128]{2,1,0:T(8,128)(2,1)S(1)}, bf16[16,16,128]{2,1,0:T(8,128)(2,1)S(1)}, u32[]{:S(2)}, u32[]{:S(2)}) collective-permute-start(bf16[16,16,128]{2,1,0:T(8,128)(2,1)S(1)} %get-tuple-element.14), channel_id=1, source_target_pairs={{0,32},{1,64},{2,96},{3,0},{4,36},{5,68},{6,100},{7,4},{8,40},{9,7... | collective-permute-start | bytes 196616 | tf_op jit(solution)/shard_map/ppermute | solution.py:318
  11.5 4.3 %collective-permute-start.2 = (bf16[16,16,128]{2,1,0:T(8,128)(2,1)S(1)}, bf16[16,16,128]{2,1,0:T(8,128)(2,1)S(1)}, u32[]{:S(2)}, u32[]{:S(2)}) collective-permute-start(bf16[16,16,128]{2,1,0:T(8,128)(2,1)S(1)} %get-tuple-element.16), channel_id=1, source_target_pairs={{0,64},{1,96},{2,0},{3,32},{4,68},{5,100},{6,4},{7,36},{8,72},{9,1... | collective-permute-start | bytes 196616 | tf_op jit(solution)/shard_map/ppermute | solution.py:318
  15.8 2.3 %collective-permute-start.3 = (bf16[16,16,128]{2,1,0:T(8,128)(2,1)S(1)}, bf16[16,16,128]{2,1,0:T(8,128)(2,1)S(1)}, u32[]{:S(2)}, u32[]{:S(2)}) collective-permute-start(bf16[16,16,128]{2,1,0:T(8,128)(2,1)S(1)} %get-tuple-element.13), channel_id=1, source_target_pairs={{0,96},{1,0},{2,32},{3,64},{4,100},{5,4},{6,36},{7,68},{8,104},{9,... | collective-permute-start | bytes 196616 | tf_op jit(solution)/shard_map/ppermute | solution.py:318
  20.9 3.4 %copy-done.17 = bf16[64,512,128]{2,1,0:T(8,128)(2,1)S(1)} copy-done((bf16[64,512,128]{2,1,0:T(8,128)(2,1)S(1)}, bf16[64,512,128]{2,1,0:T(8,128)(2,1)}, u32[]{:S(2)}) %copy-start.17) | copy-done | bytes 8388632
  25.0 42.9 %shard_map.155.refs_7_.refs_12_.refs_11_ = bf16[64,512,128]{2,1,0:T(8,128)(2,1)S(1)} custom-call(bf16[64,512,128]{2,1,0:T(8,128)(2,1)S(1)} %copy-done.17, f32[1,128]{1,0:T(1,128)S(1)} %bitcast.47, f32[1,128]{1,0:T(1,128)S(1)} %bitcast.50, bf16[128,128]{1,0:T(8,128)(2,1)S(1)} %copy-done.20), custom_call_target="tpu_custom_call" | custom-call | flops 10000000000 | bytes 16777216 | tf_op jit(solution)/shard_map/pallas_call | solution.py:252
  68.0 3.3 %copy-done.1 = bf16[64,512,128]{2,1,0:T(8,128)(2,1)} copy-done((bf16[64,512,128]{2,1,0:T(8,128)(2,1)}, bf16[64,512,128]{2,1,0:T(8,128)(2,1)S(1)}, u32[]{:S(2)}) %copy-start.1) | copy-done | bytes 8388632
  77.4 3.1 %collective-permute-start.4 = (bf16[16,4096]{1,0:T(8,128)(2,1)S(1)}, bf16[16,4096]{1,0:T(8,128)(2,1)S(1)}, u32[]{:S(2)}, u32[]{:S(2)}) collective-permute-start(bf16[16,4096]{1,0:T(8,128)(2,1)S(1)} %get-tuple-element.7), channel_id=1, source_target_pairs={{0,24},{1,25},{2,26},{3,27},{4,28},{5,29},{6,30},{7,31},{8,0},{9,1... | collective-permute-start | bytes 393224 | tf_op jit(solution)/shard_map/ppermute | solution.py:23
  82.1 2.2 %collective-permute-start.10 = (bf16[16,4096]{1,0:T(8,128)(2,1)S(1)}, bf16[16,4096]{1,0:T(8,128)(2,1)S(1)}, u32[]{:S(2)}, u32[]{:S(2)}) collective-permute-start(bf16[16,4096]{1,0:T(8,128)(2,1)S(1)} %get-tuple-element.8), channel_id=1, source_target_pairs={{0,64},{1,65},{2,66},{3,67},{4,68},{5,69},{6,70},{7,71},{8,72},{9,... | collective-permute-start | bytes 393224 | tf_op jit(solution)/shard_map/ppermute | solution.py:23
  85.4 1.7 collective-permute-start.11
  87.7 3.0 %collective-permute-start.7 = (bf16[16,8192]{1,0:T(8,128)(2,1)S(1)}, bf16[16,8192]{1,0:T(8,128)(2,1)S(1)}, u32[]{:S(2)}, u32[]{:S(2)}) collective-permute-start(bf16[16,8192]{1,0:T(8,128)(2,1)S(1)} %pad_maximum_fusion.4), channel_id=1, source_target_pairs={{0,4},{1,5},{2,6},{3,7},{4,0},{5,1},{6,2},{7,3},{8,12},{9,13},{10,... | collective-permute-start | bytes 786440 | tf_op jit(solution)/shard_map/ppermute | solution.py:23
  91.6 3.1 %collective-permute-start.12 = (bf16[48,8192]{1,0:T(8,128)(2,1)S(1)}, bf16[48,8192]{1,0:T(8,128)(2,1)S(1)}, u32[]{:S(2)}, u32[]{:S(2)}) collective-permute-start(bf16[48,8192]{1,0:T(8,128)(2,1)S(1)} %maximum_maximum_fusion), channel_id=1, source_target_pairs={{0,4},{1,5},{2,6},{3,7},{4,0},{5,1},{6,2},{7,3},{8,12},{9,13},{10,... | collective-permute-start | bytes 2359304 | tf_op jit(solution)/shard_map/ppermute | solution.py:23
  94.8 3.6 %collective-permute-done.7 = bf16[16,8192]{1,0:T(8,128)(2,1)S(1)} collective-permute-done((bf16[16,8192]{1,0:T(8,128)(2,1)S(1)}, bf16[16,8192]{1,0:T(8,128)(2,1)S(1)}, u32[]{:S(2)}, u32[]{:S(2)}) %collective-permute-start.7) | collective-permute-done | bytes 262176 | tf_op jit(solution)/shard_map/ppermute | solution.py:23
  98.5 3.2 %collective-permute-start.16 = (bf16[80,4096]{1,0:T(8,128)(2,1)S(1)}, bf16[80,4096]{1,0:T(8,128)(2,1)S(1)}, u32[]{:S(2)}, u32[]{:S(2)}) collective-permute-start(bf16[80,4096]{1,0:T(8,128)(2,1)S(1)} %get-tuple-element.11.refs_6_), channel_id=1, source_target_pairs={{0,24},{1,25},{2,26},{3,27},{4,28},{5,29},{6,30},{7,31},{8,0},{9,1... | collective-permute-start | bytes 1966088 | tf_op jit(solution)/shard_map/ppermute | solution.py:23
  103.8 9.5 %collective-permute-done.12.refs_11_.refs_10_ = bf16[48,8192]{1,0:T(8,128)(2,1)S(1)} collective-permute-done((bf16[48,8192]{1,0:T(8,128)(2,1)S(1)}, bf16[48,8192]{1,0:T(8,128)(2,1)S(1)}, u32[]{:S(2)}, u32[]{:S(2)}) %collective-permute-start.12) | collective-permute-done | bytes 786464 | tf_op jit(solution)/shard_map/ppermute | solution.py:23
  113.3 3.3 %collective-permute-done.18.refs_4_ = bf16[80,4096]{1,0:T(8,128)(2,1)S(1)} collective-permute-done((bf16[80,4096]{1,0:T(8,128)(2,1)S(1)}, bf16[80,4096]{1,0:T(8,128)(2,1)S(1)}, u32[]{:S(2)}, u32[]{:S(2)}) %collective-permute-start.18) | collective-permute-done | bytes 655392 | tf_op jit(solution)/shard_map/ppermute | solution.py:23
  118.6 3.2 %collective-permute-start.17 = (bf16[96,4096]{1,0:T(8,128)(2,1)}, bf16[96,4096]{1,0:T(8,128)(2,1)}, u32[]{:S(2)}, u32[]{:S(2)}) collective-permute-start(bf16[96,4096]{1,0:T(8,128)(2,1)} %pad_maximum_fusion.1), channel_id=1, source_target_pairs={{0,24},{1,25},{2,26},{3,27},{4,28},{5,29},{6,30},{7,31},{8,0},{9,1... | collective-permute-start | bytes 2359304 | tf_op jit(solution)/shard_map/ppermute | solution.py:23
  123.7 2.0 collective-permute-start.15
  127.8 9.9 %shard_map.156.refs_8_.refs_13_.refs_12_ = bf16[32,256,256]{2,1,0:T(8,128)(2,1)S(1)} custom-call(bf16[4,64,16,128]{3,2,1,0:T(8,128)(2,1)S(1)} %bitcast.53, f32[1,128]{1,0:T(1,128)S(1)} %bitcast.49, f32[1,128]{1,0:T(1,128)S(1)} %bitcast.52, bf16[128,256]{1,0:T(8,128)(2,1)S(1)} %copy-done.19, bf16[256,64]{1,0:T(8,128)(2,1)S(1)} %copy-done.21), custom_call_target="tpu_custom_call" | custom-call | flops 4000000000 | bytes 5242880 | tf_op jit(solution)/shard_map/pallas_call | solution.py:233
  137.8 2.1 copy-done.2
  140.1 13.0 %shard_map.157.refs_17_ = bf16[64,512,128]{2,1,0:T(8,128)(2,1)} custom-call(s32[8]{0:T(128)S(1)} %stack.139.refs_0_, bf16[80,4096]{1,0:T(8,128)(2,1)S(1)} %collective-permute-done.13.refs_1_, bf16[80,4096]{1,0:T(8,128)(2,1)S(1)} %collective-permute-done.8.refs_2_.refs_1_, bf16[80,4096]{1,0:T(8,128)(2,1)S(1)} %collective-permute-done.16.refs_3_, ...), custom_call_target="tpu_custom_call" | custom-call | flops 3000000000 | bytes 6291456 | tf_op jit(solution)/shard_map/pallas_call | solution.py:198
  156.7 3.3 %collective-permute-start.22 = (bf16[16,4096]{1,0:T(8,128)(2,1)S(1)}, bf16[16,4096]{1,0:T(8,128)(2,1)S(1)}, u32[]{:S(2)}, u32[]{:S(2)}) collective-permute-start(bf16[16,4096]{1,0:T(8,128)(2,1)S(1)} %slice.70), channel_id=1, source_target_pairs={{0,24},{1,25},{2,26},{3,27},{4,28},{5,29},{6,30},{7,31},{8,0},{9,1... | collective-permute-start | bytes 393224 | tf_op jit(solution)/shard_map/ppermute | solution.py:23
  160.0 2.7 %collective-permute-start.20 = (bf16[32,4096]{1,0:T(8,128)(2,1)S(1)}, bf16[32,4096]{1,0:T(8,128)(2,1)S(1)}, u32[]{:S(2)}, u32[]{:S(2)}) collective-permute-start(bf16[32,4096]{1,0:T(8,128)(2,1)S(1)} %slice.68), channel_id=1, source_target_pairs={{0,96},{1,97},{2,98},{3,99},{4,100},{5,101},{6,102},{7,103},{8,104... | collective-permute-start | bytes 786440 | tf_op jit(solution)/shard_map/ppermute | solution.py:23
  162.7 23.6 %shard_map.158.refs_16_ = bf16[64,512,128]{2,1,0:T(8,128)(2,1)} custom-call(s32[16]{0:T(128)S(1)} %stack.130.refs_0_, bf16[80,4096]{1,0:T(8,128)(2,1)S(1)} %collective-permute-done.13.refs_1_, bf16[80,4096]{1,0:T(8,128)(2,1)S(1)} %collective-permute-done.8.refs_2_.refs_1_, ...), custom_call_target="tpu_custom_call", output_to_operand_aliasing={{}: (17, {})} | custom-call | flops 6000000000 | bytes 12582912 | tf_op jit(solution)/shard_map/pallas_call | solution.py:198
  187.5 13.7 %shard_map.159 = bf16[64,512,128]{2,1,0:T(8,128)(2,1)} custom-call(s32[8]{0:T(128)S(1)} %stack.113.refs_0_, bf16[80,4096]{1,0:T(8,128)(2,1)S(1)} %collective-permute-done.8.refs_2_.refs_1_, bf16[96,4096]{1,0:T(8,128)(2,1)S(1)} %copy-done.6, bf16[80,4096]{1,0:T(8,128)(2,1)} %collective-permute-done.15.refs_8_.refs_3_, ...), custom_call_target="tpu_custom_call", output_to_operand_aliasing={{}: (16, {})} | custom-call | flops 3000000000 | bytes 6291456 | tf_op jit(solution)/shard_map/pallas_call | solution.py:198
  (127 shorter events, 28.1 us)
Async XLA Ops:
  6.5 119.2 %all-gather.3.cloned.1.call-start = ((), (), s32[]{:S(2)}) async-start(), calls=%async_computation | async-start | bytes 1310720 | tf_op jit(solution)/shard_map/all_gather | solution.py:319
  7.5 68.8 %collective-permute-start = (bf16[16,16,128]{2,1,0:T(8,128)(2,1)S(1)}, bf16[16,16,128]{2,1,0:T(8,128)(2,1)S(1)}, u32[]{:S(2)}, u32[]{:S(2)}) collective-permute-start(bf16[16,16,128]{2,1,0:T(8,128)(2,1)S(1)} %get-tuple-element.15), channel_id=1, source_target_pairs={{0,0},{1,32},{2,64},{3,96},{4,4},{5,36},{6,68},{7,100},{8,8},{9,40... | collective-permute-start | bytes 196616 | tf_op jit(solution)/shard_map/ppermute | solution.py:318
  8.2 68.1 %collective-permute-start.1 = (bf16[16,16,128]{2,1,0:T(8,128)(2,1)S(1)}, bf16[16,16,128]{2,1,0:T(8,128)(2,1)S(1)}, u32[]{:S(2)}, u32[]{:S(2)}) collective-permute-start(bf16[16,16,128]{2,1,0:T(8,128)(2,1)S(1)} %get-tuple-element.14), channel_id=1, source_target_pairs={{0,32},{1,64},{2,96},{3,0},{4,36},{5,68},{6,100},{7,4},{8,40},{9,7... | collective-permute-start | bytes 196616 | tf_op jit(solution)/shard_map/ppermute | solution.py:318
  11.5 64.8 %collective-permute-start.2 = (bf16[16,16,128]{2,1,0:T(8,128)(2,1)S(1)}, bf16[16,16,128]{2,1,0:T(8,128)(2,1)S(1)}, u32[]{:S(2)}, u32[]{:S(2)}) collective-permute-start(bf16[16,16,128]{2,1,0:T(8,128)(2,1)S(1)} %get-tuple-element.16), channel_id=1, source_target_pairs={{0,64},{1,96},{2,0},{3,32},{4,68},{5,100},{6,4},{7,36},{8,72},{9,1... | collective-permute-start | bytes 196616 | tf_op jit(solution)/shard_map/ppermute | solution.py:318
  15.8 60.5 %collective-permute-start.3 = (bf16[16,16,128]{2,1,0:T(8,128)(2,1)S(1)}, bf16[16,16,128]{2,1,0:T(8,128)(2,1)S(1)}, u32[]{:S(2)}, u32[]{:S(2)}) collective-permute-start(bf16[16,16,128]{2,1,0:T(8,128)(2,1)S(1)} %get-tuple-element.13), channel_id=1, source_target_pairs={{0,96},{1,0},{2,32},{3,64},{4,100},{5,4},{6,36},{7,68},{8,104},{9,... | collective-permute-start | bytes 196616 | tf_op jit(solution)/shard_map/ppermute | solution.py:318
  77.4 8.0 %collective-permute-start.4 = (bf16[16,4096]{1,0:T(8,128)(2,1)S(1)}, bf16[16,4096]{1,0:T(8,128)(2,1)S(1)}, u32[]{:S(2)}, u32[]{:S(2)}) collective-permute-start(bf16[16,4096]{1,0:T(8,128)(2,1)S(1)} %get-tuple-element.7), channel_id=1, source_target_pairs={{0,24},{1,25},{2,26},{3,27},{4,28},{5,29},{6,30},{7,31},{8,0},{9,1... | collective-permute-start | bytes 393224 | tf_op jit(solution)/shard_map/ppermute | solution.py:23
  80.4 7.2 %collective-permute-start.5 = (bf16[16,4096]{1,0:T(8,128)(2,1)S(1)}, bf16[16,4096]{1,0:T(8,128)(2,1)S(1)}, u32[]{:S(2)}, u32[]{:S(2)}) collective-permute-start(bf16[16,4096]{1,0:T(8,128)(2,1)S(1)} %get-tuple-element.7), channel_id=1, source_target_pairs={{0,16},{1,17},{2,18},{3,19},{4,20},{5,21},{6,22},{7,23},{8,24},{9,... | collective-permute-start | bytes 393224 | tf_op jit(solution)/shard_map/ppermute | solution.py:23
  81.1 9.6 %collective-permute-start.6 = (bf16[16,4096]{1,0:T(8,128)(2,1)S(1)}, bf16[16,4096]{1,0:T(8,128)(2,1)S(1)}, u32[]{:S(2)}, u32[]{:S(2)}) collective-permute-start(bf16[16,4096]{1,0:T(8,128)(2,1)S(1)} %get-tuple-element.7), channel_id=1, source_target_pairs={{0,8},{1,9},{2,10},{3,11},{4,12},{5,13},{6,14},{7,15},{8,16},{9,17... | collective-permute-start | bytes 393224 | tf_op jit(solution)/shard_map/ppermute | solution.py:23
  82.0 8.7 %collective-permute-start.9 = (bf16[16,4096]{1,0:T(8,128)(2,1)S(1)}, bf16[16,4096]{1,0:T(8,128)(2,1)S(1)}, u32[]{:S(2)}, u32[]{:S(2)}) collective-permute-start(bf16[16,4096]{1,0:T(8,128)(2,1)S(1)} %get-tuple-element.8), channel_id=1, source_target_pairs={{0,96},{1,97},{2,98},{3,99},{4,100},{5,101},{6,102},{7,103},{8,104... | collective-permute-start | bytes 393224 | tf_op jit(solution)/shard_map/ppermute | solution.py:23
  82.1 8.7 %collective-permute-start.10 = (bf16[16,4096]{1,0:T(8,128)(2,1)S(1)}, bf16[16,4096]{1,0:T(8,128)(2,1)S(1)}, u32[]{:S(2)}, u32[]{:S(2)}) collective-permute-start(bf16[16,4096]{1,0:T(8,128)(2,1)S(1)} %get-tuple-element.8), channel_id=1, source_target_pairs={{0,64},{1,65},{2,66},{3,67},{4,68},{5,69},{6,70},{7,71},{8,72},{9,... | collective-permute-start | bytes 393224 | tf_op jit(solution)/shard_map/ppermute | solution.py:23
  87.7 10.8 %collective-permute-start.7 = (bf16[16,8192]{1,0:T(8,128)(2,1)S(1)}, bf16[16,8192]{1,0:T(8,128)(2,1)S(1)}, u32[]{:S(2)}, u32[]{:S(2)}) collective-permute-start(bf16[16,8192]{1,0:T(8,128)(2,1)S(1)} %pad_maximum_fusion.4), channel_id=1, source_target_pairs={{0,4},{1,5},{2,6},{3,7},{4,0},{5,1},{6,2},{7,3},{8,12},{9,13},{10,... | collective-permute-start | bytes 786440 | tf_op jit(solution)/shard_map/ppermute | solution.py:23
  91.6 21.6 %collective-permute-start.12 = (bf16[48,8192]{1,0:T(8,128)(2,1)S(1)}, bf16[48,8192]{1,0:T(8,128)(2,1)S(1)}, u32[]{:S(2)}, u32[]{:S(2)}) collective-permute-start(bf16[48,8192]{1,0:T(8,128)(2,1)S(1)} %maximum_maximum_fusion), channel_id=1, source_target_pairs={{0,4},{1,5},{2,6},{3,7},{4,0},{5,1},{6,2},{7,3},{8,12},{9,13},{10,... | collective-permute-start | bytes 2359304 | tf_op jit(solution)/shard_map/ppermute | solution.py:23
  98.5 19.1 %collective-permute-start.16 = (bf16[80,4096]{1,0:T(8,128)(2,1)S(1)}, bf16[80,4096]{1,0:T(8,128)(2,1)S(1)}, u32[]{:S(2)}, u32[]{:S(2)}) collective-permute-start(bf16[80,4096]{1,0:T(8,128)(2,1)S(1)} %get-tuple-element.11.refs_6_), channel_id=1, source_target_pairs={{0,24},{1,25},{2,26},{3,27},{4,28},{5,29},{6,30},{7,31},{8,0},{9,1... | collective-permute-start | bytes 1966088 | tf_op jit(solution)/shard_map/ppermute | solution.py:23
  101.7 14.8 %collective-permute-start.18 = (bf16[80,4096]{1,0:T(8,128)(2,1)S(1)}, bf16[80,4096]{1,0:T(8,128)(2,1)S(1)}, u32[]{:S(2)}, u32[]{:S(2)}) collective-permute-start(bf16[80,4096]{1,0:T(8,128)(2,1)S(1)} %get-tuple-element.11.refs_6_), channel_id=1, source_target_pairs={{0,8},{1,9},{2,10},{3,11},{4,12},{5,13},{6,14},{7,15},{8,16},{9,17... | collective-permute-start | bytes 1966088 | tf_op jit(solution)/shard_map/ppermute | solution.py:23
  101.7 20.1 %collective-permute-start.13 = (bf16[80,4096]{1,0:T(8,128)(2,1)S(1)}, bf16[80,4096]{1,0:T(8,128)(2,1)S(1)}, u32[]{:S(2)}, u32[]{:S(2)}) collective-permute-start(bf16[80,4096]{1,0:T(8,128)(2,1)S(1)} %get-tuple-element.12.refs_5_), channel_id=1, source_target_pairs={{0,96},{1,97},{2,98},{3,99},{4,100},{5,101},{6,102},{7,103},{8,104... | collective-permute-start | bytes 1966088 | tf_op jit(solution)/shard_map/ppermute | solution.py:23
  103.2 19.6 %collective-permute-start.8 = (bf16[80,4096]{1,0:T(8,128)(2,1)S(1)}, bf16[80,4096]{1,0:T(8,128)(2,1)S(1)}, u32[]{:S(2)}, u32[]{:S(2)}) collective-permute-start(bf16[80,4096]{1,0:T(8,128)(2,1)S(1)} %get-tuple-element.12.refs_5_), channel_id=1, source_target_pairs={{0,32},{1,33},{2,34},{3,35},{4,36},{5,37},{6,38},{7,39},{8,40},{9,... | collective-permute-start | bytes 1966088 | tf_op jit(solution)/shard_map/ppermute | solution.py:23
  117.5 35.6 %collective-permute-start.19 = (bf16[80,4096]{1,0:T(8,128)(2,1)}, bf16[80,4096]{1,0:T(8,128)(2,1)}, u32[]{:S(2)}, u32[]{:S(2)}) collective-permute-start(bf16[80,4096]{1,0:T(8,128)(2,1)} %pad_maximum_fusion.3), channel_id=1, source_target_pairs={{0,8},{1,9},{2,10},{3,11},{4,12},{5,13},{6,14},{7,15},{8,16},{9,17... | collective-permute-start | bytes 1966088 | tf_op jit(solution)/shard_map/ppermute | solution.py:23
  118.6 37.2 %collective-permute-start.17 = (bf16[96,4096]{1,0:T(8,128)(2,1)}, bf16[96,4096]{1,0:T(8,128)(2,1)}, u32[]{:S(2)}, u32[]{:S(2)}) collective-permute-start(bf16[96,4096]{1,0:T(8,128)(2,1)} %pad_maximum_fusion.1), channel_id=1, source_target_pairs={{0,24},{1,25},{2,26},{3,27},{4,28},{5,29},{6,30},{7,31},{8,0},{9,1... | collective-permute-start | bytes 2359304 | tf_op jit(solution)/shard_map/ppermute | solution.py:23
  122.8 37.2 %collective-permute-start.14 = (bf16[96,4096]{1,0:T(8,128)(2,1)}, bf16[96,4096]{1,0:T(8,128)(2,1)S(1)}, u32[]{:S(2)}, u32[]{:S(2)}) collective-permute-start(bf16[96,4096]{1,0:T(8,128)(2,1)} %pad_maximum_fusion), channel_id=1, source_target_pairs={{0,96},{1,97},{2,98},{3,99},{4,100},{5,101},{6,102},{7,103},{8,104... | collective-permute-start | bytes 2359304 | tf_op jit(solution)/shard_map/ppermute | solution.py:23
  123.7 30.4 %collective-permute-start.15 = (bf16[80,4096]{1,0:T(8,128)(2,1)}, bf16[80,4096]{1,0:T(8,128)(2,1)}, u32[]{:S(2)}, u32[]{:S(2)}) collective-permute-start(bf16[80,4096]{1,0:T(8,128)(2,1)} %pad_maximum_fusion.2), channel_id=1, source_target_pairs={{0,32},{1,33},{2,34},{3,35},{4,36},{5,37},{6,38},{7,39},{8,40},{9,... | collective-permute-start | bytes 1966088 | tf_op jit(solution)/shard_map/ppermute | solution.py:23
  154.1 32.3 %collective-permute-start.23 = (bf16[32,4096]{1,0:T(8,128)(2,1)S(1)}, bf16[32,4096]{1,0:T(8,128)(2,1)S(1)}, u32[]{:S(2)}, u32[]{:S(2)}) collective-permute-start(bf16[32,4096]{1,0:T(8,128)(2,1)S(1)} %slice.71), channel_id=1, source_target_pairs={{0,8},{1,9},{2,10},{3,11},{4,12},{5,13},{6,14},{7,15},{8,16},{9,17... | collective-permute-start | bytes 786440 | tf_op jit(solution)/shard_map/ppermute | solution.py:23
  155.1 31.3 %collective-permute-start.21 = (bf16[16,4096]{1,0:T(8,128)(2,1)S(1)}, bf16[16,4096]{1,0:T(8,128)(2,1)S(1)}, u32[]{:S(2)}, u32[]{:S(2)}) collective-permute-start(bf16[16,4096]{1,0:T(8,128)(2,1)S(1)} %slice.69), channel_id=1, source_target_pairs={{0,32},{1,33},{2,34},{3,35},{4,36},{5,37},{6,38},{7,39},{8,40},{9,... | collective-permute-start | bytes 393224 | tf_op jit(solution)/shard_map/ppermute | solution.py:23
  156.7 29.7 %collective-permute-start.22 = (bf16[16,4096]{1,0:T(8,128)(2,1)S(1)}, bf16[16,4096]{1,0:T(8,128)(2,1)S(1)}, u32[]{:S(2)}, u32[]{:S(2)}) collective-permute-start(bf16[16,4096]{1,0:T(8,128)(2,1)S(1)} %slice.70), channel_id=1, source_target_pairs={{0,24},{1,25},{2,26},{3,27},{4,28},{5,29},{6,30},{7,31},{8,0},{9,1... | collective-permute-start | bytes 393224 | tf_op jit(solution)/shard_map/ppermute | solution.py:23
  160.0 26.4 %collective-permute-start.20 = (bf16[32,4096]{1,0:T(8,128)(2,1)S(1)}, bf16[32,4096]{1,0:T(8,128)(2,1)S(1)}, u32[]{:S(2)}, u32[]{:S(2)}) collective-permute-start(bf16[32,4096]{1,0:T(8,128)(2,1)S(1)} %slice.68), channel_id=1, source_target_pairs={{0,96},{1,97},{2,98},{3,99},{4,100},{5,101},{6,102},{7,103},{8,104... | collective-permute-start | bytes 786440 | tf_op jit(solution)/shard_map/ppermute | solution.py:23
  (26 other events, 221.6 us)
Sparse Core Ops, SparseCore 0:
  18.3 19.8 all-gather.2

commit v2 on v0

v2 whole, which is shorter than its diff:
```python
import functools

import jax
import jax.numpy as jnp
import numpy as np
from jax import lax
from jax.experimental import pallas as pl
from jax.experimental.pallas import tpu as pltpu
from jax.sharding import PartitionSpec as P

AXES = ("row", "col")
BF16, F32 = jnp.bfloat16, jnp.float32
DEVICES = [(z, y, x, c) for z in range(4) for y in range(4) for x in range(2) for c in range(4)]
MIB = 1 << 20


def device_id(z, y, x, c):
    return (((z % 4) * 4 + y % 4) * 2 + x % 2) * 4 + c


def move(value, dz=0, dy=0, dx=0, dc=0):
    pairs = [
        (device_id(z, y, x, c), device_id(z + dz, y + dy, x + dx, c ^ dc)) for z, y, x, c in DEVICES
    ]
    return lax.ppermute(value, AXES, pairs)


def sigmoid(values):
    return 0.5 * jnp.tanh(0.5 * values) + 0.5


def hidden_order():
    order = []
    for group in range(32):
        first = 2 * group
        order += [first, first + 64, first + 1, first + 65]
    return np.array(order)


def norm_rows(values, average, gain, bias):
    mean = jnp.dot(values, average, preferred_element_type=F32)
    centered = values.astype(F32) - mean
    var = jnp.dot((centered * centered).astype(BF16), average, preferred_element_type=F32)
    return (centered * lax.rsqrt(var + 1e-05) * gain.reshape(1, 128) + bias.reshape(1, 128)).astype(BF16)


def project_16(normed, weight, swap, store):
    proj = lax.dot_general(
        weight, normed.reshape(16 * 64, 128), (((0,), (1,)), ((), ())), preferred_element_type=F32
    )
    value = (sigmoid(proj[:128]) * proj[128:]).astype(BF16).astype(F32)
    low, high = value[:64], value[64:]
    lane = lax.broadcasted_iota(jnp.int32, (64, 128), 1)
    for pair in range(8):
        lo = low[:, pair * 128 : (pair + 1) * 128]
        hi = high[:, pair * 128 : (pair + 1) * 128]
        swap[:, 2 * pair, :] = jnp.where(lane < 64, lo, pltpu.roll(hi, 64, 1))
        swap[:, 2 * pair + 1, :] = jnp.where(lane < 64, pltpu.roll(lo, 64, 1), hi)
    for h in range(64):
        store(h, swap[h].astype(BF16))


def right_kernel(here, p0, p1, p2, p3, gain_in, bias_in, weight_in, out, normed, swap, gain, bias, weight, sem):
    fetches = [
        pltpu.make_async_copy(source, target, sem.at[n])
        for n, (source, target) in enumerate(((gain_in, gain), (bias_in, bias), (weight_in, weight)))
    ]
    for fetch in fetches:
        fetch.start()
    for fetch in fetches:
        fetch.wait()
    average = jnp.full((128, 128), 1 / 128, BF16)
    for s, piece in enumerate((p0, p1, p2, p3)):
        start = pl.multiple_of(lax.rem(here[0] - s + 4, 4) * 16, 16)
        made = norm_rows(piece[...].reshape(256, 128), average, gain[...], bias[...])
        normed[:, pl.ds(start, 16), :] = made.reshape(16, 16, 128)

    def store(h, tile):
        out[:, h * 128 : (h + 1) * 128] = tile

    project_16(normed[...], weight[...], swap, store)


def left_kernel(
    here, left_0, left_1, average, gain, bias, weight, spread, order, w_out, out_gain, out_bias,
    out, wide_out, wide_gain, wide_bias, normed, swap, rows,
):
    for quarter in range(4):
        at = slice(quarter * 16, quarter * 16 + 16)
        mine = normed.at[quarter]
        for flip in range(4):
            piece = (left_0, left_1)[flip % 2][flip // 2, at].reshape(256, 128)
            start = pl.multiple_of((here[3] ^ flip) * 16, 16)
            made = norm_rows(piece, average[...], gain[...], bias[...])
            mine[:, pl.ds(start, 16), :] = made.reshape(16, 16, 128)

        def store(h, tile, at=at):
            rows[at, h * 128 : (h + 1) * 128] = tile

        project_16(mine[...], weight[...], swap.at[quarter], store)
    row = lax.broadcasted_iota(jnp.int32, (256, 256), 0)
    lane = lax.broadcasted_iota(jnp.int32, (256, 256), 1)
    keep = lax.rem(row, 4) == lane // 64

    def body(g, carry):
        tile = rows[:, pl.ds(pl.multiple_of(g * 256, 256), 256)]
        wide = jnp.dot(spread[...], tile, preferred_element_type=F32)
        out[g] = jnp.where(keep, wide, 0.0).astype(BF16)
        return carry

    lax.fori_loop(0, 32, body, 0, unroll=32)
    made = jnp.dot(order[...], w_out[...].astype(F32), preferred_element_type=F32)
    second = lax.rem(lax.broadcasted_iota(jnp.int32, (256, 128), 0), 8) // 4
    wide_out[:, :128] = jnp.where(second == 0, made, 0.0).astype(BF16)
    wide_out[:, 128:] = jnp.where(second == 1, made, 0.0).astype(BF16)
    for source, target in ((out_gain, wide_gain), (out_bias, wide_bias)):
        columns = jnp.broadcast_to(source[...], (128, 128)).T
        made = jnp.dot(
            order[...], columns, preferred_element_type=F32, precision=lax.Precision.HIGHEST
        )
        target[...] = made.reshape(32, 8, 128)


def gate_block(average, weight, bias, pair, out):
    for i in range(0, pair.shape[0], 2):
        both = jnp.concatenate([pair[i], pair[i + 1]], 1)
        mean = jnp.dot(both, average[...], preferred_element_type=F32)
        centered = (both.astype(F32) - mean).astype(BF16)
        var = jnp.dot(centered * centered, average[...], preferred_element_type=F32)
        proj = jnp.dot(centered, weight[...], preferred_element_type=F32)
        proj = proj * lax.rsqrt(var + 1e-05) + bias[...]
        gate = (0.5 * jnp.tanh(proj) + 0.5).astype(BF16)
        out[i], out[i + 1] = gate[:, :128], gate[:, 128:]


def gate_kernel(half, pair, average, weight, bias, out):
    rows, first = 8, half * 4
    pltpu.emit_pipeline(
        functools.partial(gate_block, average, weight, bias),
        grid=(4,),
        in_specs=[pl.BlockSpec((rows, 512, 128), lambda n: (n + first, 0, 0))],
        out_specs=[pl.BlockSpec((rows, 512, 128), lambda n: (n, 0, 0))],
    )(pair, out)


def update_kernel(blocks, n_src, has_out, *refs):
    here = refs[0]
    sources = refs[1 : 1 + n_src]
    gate_0, gate_1, lbd, wide_out, gain, bias = refs[1 + n_src : 7 + n_src]
    refs = refs[7 + n_src + has_out :]
    out, right, product, gates, results, gate_sem, out_sem = refs
    z, y, x = here[0], here[1], here[2]
    columns = 16 * len(blocks)

    def column(b):
        dz, dy, dx = blocks[b][0]
        start = (lax.rem(y + dy, 4) * 2 + lax.rem(x + dx, 2)) * 64 + lax.rem(z + dz, 4) * 16
        return pl.ds(pl.multiple_of(start, 16), 16)

    def gate_copy(b, half):
        return pltpu.make_async_copy(
            (gate_0, gate_1)[half].at[:, column(b), :],
            gates.at[pl.ds(half * 32, 32), pl.ds(b * 16, 16), :],
            gate_sem.at[b, half],
        )

    def out_copy(b, q):
        rows = pl.ds(q * 16, 16)
        return pltpu.make_async_copy(
            results.at[rows, pl.ds(b * 16, 16), :], out.at[rows, column(b), :], out_sem.at[b, q]
        )

    for b in range(len(blocks)):
        gate_copy(b, 0).start()
        gate_copy(b, 1).start()
    member = lax.broadcasted_iota(jnp.int32, (8, 128), 0)

    def over_four(total):
        swapped = jnp.where(lax.rem(member, 2) == 0, pltpu.roll(total, 7, 0), pltpu.roll(total, 1, 0))
        total = total + swapped
        swapped = jnp.where(lax.rem(member, 4) < 2, pltpu.roll(total, 6, 0), pltpu.roll(total, 2, 0))
        return total + swapped

    for b, (_, halves) in enumerate(blocks):
        for half, (src, row, lane) in enumerate(halves):
            right[b * 16 : b * 16 + 16, half * 4096 : half * 4096 + 4096] = sources[src][
                row : row + 16, lane : lane + 4096
            ]

    def multiply(g, carry):
        panel = right[:, pl.ds(pl.multiple_of(g * 256, 256), 256)]
        made = lax.dot_general(lbd[g], panel, (((1,), (1,)), ((), ())), preferred_element_type=F32)
        product[:, g] = made.reshape(32, 8, columns)
        return carry

    lax.fori_loop(0, 32, multiply, 0, unroll=16)
    for b in range(len(blocks)):
        gate_copy(b, 0).wait()
        gate_copy(b, 1).wait()

    def finish(ip, carry):
        for part in range(columns // 128):
            lanes = slice(part * 128, part * 128 + 128)
            values = product[ip, :, :, lanes]
            mean = over_four(jnp.sum(values, axis=0)) * (1.0 / 128)
            centered = values - mean[None]
            var = over_four(jnp.sum(centered * centered, axis=0)) * (1.0 / 128)
            normed = centered * lax.rsqrt(var + 1e-05)[None] * gain[...] + bias[...]
            normed = normed.reshape(256, 128).astype(BF16)
            both = lax.dot_general(
                normed, wide_out[...], (((0,), (0,)), ((), ())), preferred_element_type=F32
            )
            for i2 in range(2):
                row = 2 * ip + i2
                gate = gates[row, lanes].astype(F32)
                results[row, lanes] = (both[:, i2 * 128 : (i2 + 1) * 128] * gate).astype(BF16)
        return carry

    for q in range(4):
        lax.fori_loop(q * 8, q * 8 + 8, finish, 0, unroll=8 * 128 // columns)
        for b in range(len(blocks)):
            out_copy(b, q).start()
    for b in range(len(blocks)):
        for q in range(4):
            out_copy(b, q).wait()


VMEM = pl.BlockSpec(memory_space=pltpu.VMEM)
SMEM = pl.BlockSpec(memory_space=pltpu.SMEM)
HBM = pl.BlockSpec(memory_space=pltpu.HBM)


def run_update(blocks, here, sources, gates, lbd, wide_out, gain, bias, before):
    n = len(blocks)
    has_out = before is not None
    args = [here, *sources, *gates, lbd, wide_out, gain, bias] + ([before] if has_out else [])
    return pl.pallas_call(
        functools.partial(update_kernel, blocks, len(sources), has_out),
        out_shape=pltpu.HBM((64, 512, 128), BF16),
        in_specs=[SMEM] + [VMEM] * len(sources) + [HBM] * 2 + [VMEM] * 4 + [HBM] * has_out,
        out_specs=HBM,
        scratch_shapes=[
            pltpu.VMEM((n * 16, 8192), BF16),
            pltpu.VMEM((32, 32, 8, n * 16), F32),
            pltpu.VMEM((64, n * 16, 128), BF16),
            pltpu.VMEM((64, n * 16, 128), BF16),
            pltpu.SemaphoreType.DMA((n, 2)),
            pltpu.SemaphoreType.DMA((n, 4)),
        ],
        input_output_aliases={len(args) - 1: 0} if has_out else {},
        compiler_params=pltpu.CompilerParams(vmem_limit_bytes=(8 + 3 * n // 2) * MIB),
        cost_estimate=pl.CostEstimate(flops=n * 4 * 10**8, bytes_accessed=n * MIB, transcendentals=0),
    )(*args)


def run_right(here, pieces, *weights):
    weights = [pltpu.with_memory_space_constraint(w, pltpu.HBM) for w in weights]
    return pl.pallas_call(
        right_kernel,
        out_shape=jax.ShapeDtypeStruct((16, 8192), BF16),
        in_specs=[SMEM] + [VMEM] * 4 + [HBM] * 3,
        out_specs=VMEM,
        scratch_shapes=[
            pltpu.VMEM((16, 64, 128), BF16),
            pltpu.VMEM((64, 16, 128), F32),
            pltpu.VMEM((128,), F32),
            pltpu.VMEM((128,), F32),
            pltpu.VMEM((128, 256), BF16),
            pltpu.SemaphoreType.DMA((3,)),
        ],
        compiler_params=pltpu.CompilerParams(vmem_limit_bytes=16 * MIB),
    )(here, *pieces, *weights)


def run_left(here, left_0, left_1, gain, bias, weight, w_out, out_gain, out_bias):
    spread = np.zeros((256, 64), np.float32)
    spread[np.arange(256), np.arange(256) // 4] = 1
    order = np.zeros((32, 2, 4, 128), np.float32)
    for n, h in enumerate(hidden_order()):
        order[n // 4, :, n % 4, h] = 1
    return pl.pallas_call(
        left_kernel,
        out_shape=[
            jax.ShapeDtypeStruct((32, 256, 256), BF16),
            jax.ShapeDtypeStruct((256, 256), BF16),
            jax.ShapeDtypeStruct((32, 8, 128), F32),
            jax.ShapeDtypeStruct((32, 8, 128), F32),
        ],
        in_specs=[SMEM] + [VMEM] * 11,
        out_specs=[VMEM] * 4,
        scratch_shapes=[
            pltpu.VMEM((4, 16, 64, 128), BF16),
            pltpu.VMEM((4, 64, 16, 128), F32),
            pltpu.VMEM((64, 8192), BF16),
        ],
        compiler_params=pltpu.CompilerParams(vmem_limit_bytes=20 * MIB),
        cost_estimate=pl.CostEstimate(flops=4 * 10**9, bytes_accessed=12 * MIB, transcendentals=0),
    )(
        here, left_0, left_1, jnp.full((128, 128), 1 / 128, BF16), gain, bias, weight, jnp.asarray(spread, BF16), jnp.asarray(order.reshape(256, 128)),
        w_out, out_gain.reshape(1, 128), out_bias.reshape(1, 128),
    )


def gate_weights(gain, bias, weight):
    eye = jnp.eye(2, dtype=F32)
    weight = weight.astype(F32)
    wide = jnp.kron(eye, gain.reshape(128, 1) * weight * 0.5).astype(BF16)
    shift = 0.5 * jnp.dot(bias, weight, precision=lax.Precision.HIGHEST)
    return wide, jnp.tile(shift, (1, 2))


def run_gate(half, pair, wide, shift):
    average = jnp.kron(jnp.eye(2, dtype=BF16), jnp.full((128, 128), 1 / 128, BF16))
    return pl.pallas_call(
        functools.partial(gate_kernel, half),
        out_shape=pltpu.HBM((32, 512, 128), BF16),
        in_specs=[HBM, VMEM, VMEM, VMEM],
        out_specs=HBM,
        compiler_params=pltpu.CompilerParams(vmem_limit_bytes=20 * MIB),
        cost_estimate=pl.CostEstimate(flops=8 * 10**9, bytes_accessed=1 * MIB, transcendentals=0),
    )(pltpu.with_memory_space_constraint(pair, pltpu.HBM), average, wide, shift)


def place(near, far, x, own, first, other):
    if x == 0:
        if near == 0 or far == 0:
            return own(near, far), 0
        if far != 2:
            return f"{first}{far}", (near - 1) * 16
        return (f"P{first}1", 16 + near * 16) if near < 3 else (f"P{first}3", 32)
    if far == 0:
        if near == 0:
            return "X0", 0
        return (f"{other}1", 64) if near == 1 else ("X2", (near - 2) * 16)
    if far != 2:
        if near == 0:
            return f"{first}{far}", 48
        if near == 2:
            return "X3", 0 if far == 1 else 16
        return f"P{first}{far}", 0 if near == 1 else 16
    if near == 0:
        return f"P{first}3", 48
    return (f"Q{first}1", (near - 1) * 16) if near < 3 else (f"Q{first}3", 0)


def place_a(z, y, x):
    own = lambda near, far: f"Z{far}" if near == 0 and far else f"Y{near}"
    name, row = place(y, z, x, own, "A", "B")
    return name, row, 0


def place_b(z, y, x):
    own = lambda near, far: f"Y{far}" if near == 0 and far else (f"Z{near}" if near else "Y0")
    name, row = place(z, y, x, own, "B", "A")
    return name, row, 4096 if name[0] in "XYZ" else 0


EARLY = [(z, y, 0) for z in (0, 1, 3) for y in (0, 1, 3)] + [(2, 0, 0), (0, 2, 0)]
EARLY += [(0, 0, 1), (1, 0, 1), (3, 0, 1), (0, 1, 1), (0, 3, 1)]
LATE = [(2, 1, 1), (2, 2, 1), (2, 3, 1), (1, 2, 1), (3, 2, 1)]
OTHERS = [
    (z, y, x)
    for x in range(2)
    for z in range(4)
    for y in range(4)
    if (z, y, x) not in LATE and (z, y, x) not in EARLY
]


def per_device(
    pair_block, left_panel, right_panel, ln_gain, ln_bias, w_left, w_right, w_gate, out_gain, out_bias, w_out
):
    row = lax.axis_index("row")
    z, y, x = row // 8, (row // 2) % 4, row % 2
    c = lax.axis_index("col")
    gain, bias = ln_gain.reshape(1, 128), ln_bias.reshape(1, 128)

    here = jnp.stack([z, y, x, c]).astype(jnp.int32)

    pieces = []
    for s in range(4):
        pairs = [(device_id(z_, y_, x_, c_), device_id(c_ + s, y_, x_, z_)) for z_, y_, x_, c_ in DEVICES]
        part = lax.dynamic_slice_in_dim(right_panel, ((c + s) % 4) * 16, 16, 0)
        pieces.append(lax.ppermute(part, AXES, pairs))
    rows = run_right(here, pieces, ln_gain, ln_bias, w_right)
    left_2 = move(left_panel, dc=2)
    rows, left_2, wide_gate = lax.optimization_barrier(
        (rows, left_2, gate_weights(ln_gain, ln_bias, w_gate))
    )

    def cat(*parts):
        return jnp.concatenate(parts, 0)

    got = {}
    def together(*names, more=()):
        held = lax.optimization_barrier([got[n] for n in names] + list(more))
        got.update(zip(names, held))
        return held[len(names) :]

    def call(blocks, before):
        names = sorted({p(*d)[0] for d in blocks for p in (place_a, place_b)})
        found = []
        for d in blocks:
            places = [p(*d) for p in (place_a, place_b)]
            found.append((d, [(names.index(name), row, lane) for name, row, lane in places]))
        sources = [got[n] for n in names]
        return run_update(found, here, sources, gates, lbd, wide_out, gain_out, bias_out, before)

    def halves(a, b):
        return jnp.concatenate([a, b], 1)

    got["Y0"] = rows
    got["X0"] = move(rows, dx=1)
    for step in (1, 3):
        got[f"Y{step}"], got[f"Z{step}"] = move(rows, dy=-step), move(rows, dz=-step)
    got["X0"], again = lax.optimization_barrier((got["X0"], rows))
    got["Y2"] = move(again, dy=2)
    got["Y1"], again = lax.optimization_barrier((got["Y1"], again))
    got["Z2"] = move(again, dz=2)
    gate_0 = run_gate(0, pair_block, *wide_gate)
    ones = ("Y1", "Y2", "Y3", "Z1", "Z2", "Z3", "X0")
    gate_0, left_2 = together(*ones, more=[gate_0, left_2])
    half_a = [got[n][:, :4096] for n in ones]
    half_b = [got[n][:, 4096:] for n in ones]
    to_z, to_y = cat(*half_a[:3], half_a[6]), cat(*half_b[3:])
    got["A1"], got["A3"] = move(cat(to_z, half_b[6]), dz=-1), move(to_z, dz=1)
    got["B1"], got["B3"] = move(cat(to_y, half_a[6]), dy=-1), move(to_y, dy=1)
    got["X2"] = move(halves(cat(*half_a[1:3]), cat(*half_b[4:6])), dx=1)
    left_0 = jnp.stack([left_panel, left_2])
    left_1 = move(left_0, dc=1)
    gate_1 = run_gate(1, pair_block, *wide_gate)
    lbd, wide_out, gain_out, bias_out = run_left(
        here, left_0, left_1, gain, bias, w_left, w_out, out_gain, out_bias
    )
    gate_1, lbd = together("A1", "A3", "B1", "B3", "X2", more=[gate_1, lbd])
    gates = (gate_0, gate_1)
    a1, a3, b1, b3, x2 = (got[n] for n in ("A1", "A3", "B1", "B3", "X2"))
    xa, xb = cat(b1[64:], x2[16:, :4096]), cat(a1[64:], x2[16:, 4096:])
    got["PA1"], got["PA3"] = move(cat(xa, a1[:32]), dz=-1), move(cat(xa, a3[32:]), dz=1)
    got["PB1"], got["PB3"] = move(cat(xb, b1[:32]), dy=-1), move(cat(xb, b3[32:]), dy=1)
    got["X3"] = move(halves(cat(a1[16:32], a3[16:32]), cat(b1[16:32], b3[16:32])), dx=1)
    out = call(EARLY, None)
    (out,) = together("PA1", "PA3", "PB1", "PB3", "X3", more=[out])
    x3 = got["X3"]
    got["QA1"], got["QA3"] = move(cat(got["PA1"][:16], x3[:16, :4096]), dz=-1), move(got["PA3"][16:32], dz=1)
    got["QB1"], got["QB3"] = move(cat(got["PB1"][:16], x3[:16, 4096:]), dy=-1), move(got["PB3"][16:32], dy=1)
    out = call(OTHERS[:8], out)
    (out,) = together("QA1", "QA3", "QB1", "QB3", more=[out])
    return call(LATE + OTHERS[8:], out)


def solution(mesh):
    part = P("row", "col", None)
    in_specs = (part, part, part) + (P(),) * 8
    return jax.shard_map(per_device, mesh=mesh, in_specs=in_specs, out_specs=part, check_vma=False)
```

time: 400 us -> 105 us (0.26)
  waiting for transfers between devices: 273 us -> 4.92 us
  starting transfers between devices: 0.12 us -> 49.5 us
  Pallas kernels: 0 us -> 45.7 us
  matrix products: 46.3 us -> 0.9 us
  other arithmetic: 39.7 us -> 1.53 us
  local copies, waits for them, and re-layouts: 27 us -> 1.59 us
  between operations: 13.3 us -> 0.83 us
    all_gather x3 -> x0, waiting for transfers between devices: 273 us -> none  [the longest x1 255 us: per_device(): every = lax.all_gather(right_rows, 'row', axis=0, tiled=True)]
    ppermute x0 -> x27, starting transfers between devices: none -> 49.5 us  [the longest x23 37.9 us: move(): return lax.ppermute(value, AXES, pairs)]
    pallas_call x0 -> x7, Pallas kernels: none -> 45.7 us  [the longest x3 22.1 us: run_update(): pl.pallas_call(functools.partial(update_kernel, blocks, len(sources), has...]
    dot_general x5 -> x1, matrix products: 46.3 us -> 0.9 us  [gate_weights(): shift = 0.5 * jnp.dot(bias, weight, precision=lax.Precision.HIGHEST)]
    reduce_sum x7 -> x0, other arithmetic: 29.5 us -> none  [the longest x4 21.5 us: layer_norm(): var = jnp.mean(centered * centered, axis=-1, keepdims=True)]
    unnamed x17 -> x25, local copies, waits for them, and re-layouts: 13.5 us -> 0.11 us
    convert_element_type x3 -> x2, other arithmetic: 10.1 us -> 0.16 us  [the longest x1 0.16 us: gate_weights(): wide = jnp.kron(eye, gain.reshape(128, 1) * weight * 0.5).astype(BF16)]
    dynamic_slice x1, local copies, waits for them, and re-layouts: 8.81 us -> 0.95 us  [per_device(): part = lax.dynamic_slice_in_dim(right_panel, (c + s) % 4 * 16, 16, 0)]
  transfers between devices with their start and end apart: 3 -> 27, of which waited for: 2 -> 2; matrix products, arithmetic and copies ran while one was open for 10% -> 3% of each run, Pallas kernels for 0% -> 38%
where the time goes in v2:
time: 105 us
  starting transfers between devices  49.5 us (47%)
  Pallas kernels  45.7 us (44%)
  waiting for transfers between devices  4.92 us (5%)
  local copies, waits for them, and re-layouts  1.59 us (2%)
  other arithmetic  1.53 us (1%)
    ppermute x23, starting transfers between devices, move(): return lax.ppermute(value, AXES, pairs)  37.9 us
    pallas_call x3, Pallas kernels, run_update(): pl.pallas_call(functools.partial(update_kernel, blocks, len(sources), has...  22.1 us
    pallas_call x2, Pallas kernels, run_gate(): pl.pallas_call(functools.partial(gate_kernel, half), out_shape=pltpu.HBM(...  15.2 us
    ppermute x4, starting transfers between devices, per_device(): pieces.append(lax.ppermute(part, AXES, pairs))  11.5 us
    pallas_call x1, Pallas kernels, run_left(): pl.pallas_call(left_kernel, out_shape=[jax.ShapeDtypeStruct((32, 256, 256...  5.76 us
    ppermute x23, waiting for transfers between devices, move(): return lax.ppermute(value, AXES, pairs)  4.9 us
    pallas_call x1, Pallas kernels, run_right(): pl.pallas_call(right_kernel, out_shape=jax.ShapeDtypeStruct((16, 8192), B...  2.51 us
  transfers between devices with their start and end apart: 27, of which 2 were waited for; matrix products, arithmetic and copies ran while one was open for 3% of the time, Pallas kernels for 38%

profile of v2, /device:TPU:0, one launch (start us, length us, event | category | flops | bytes accessed | tf_op | source)
XLA Modules:
  0.0 104.9 jit_solution(16574457199537671443)
XLA Ops:
  1.0 4.2 %collective-permute-start.3 = (bf16[16,16,128]{2,1,0:T(8,128)(2,1)S(1)}, bf16[16,16,128]{2,1,0:T(8,128)(2,1)S(1)}, u32[]{:S(2)}, u32[]{:S(2)}) collective-permute-start(bf16[16,16,128]{2,1,0:T(8,128)(2,1)S(1)} %get-tuple-element.111), channel_id=1, source_target_pairs={{0,96},{1,0},{2,32},{3,64},{4,100},{5,4},{6,36},{7,68},{8,104},{9,... | collective-permute-start | bytes 196616 | tf_op jit(solution)/shard_map/ppermute | solution.py:384
  6.1 6.4 %collective-permute-start.2 = (bf16[16,16,128]{2,1,0:T(8,128)(2,1)S(1)}, bf16[16,16,128]{2,1,0:T(8,128)(2,1)S(1)}, u32[]{:S(2)}, u32[]{:S(2)}) collective-permute-start(bf16[16,16,128]{2,1,0:T(8,128)(2,1)S(1)} %get-tuple-element.114), channel_id=1, source_target_pairs={{0,64},{1,96},{2,0},{3,32},{4,68},{5,100},{6,4},{7,36},{8,72},{9,1... | collective-permute-start | bytes 196616 | tf_op jit(solution)/shard_map/ppermute | solution.py:384
  14.6 2.5 %shard_map.127.refs_7_ = bf16[16,8192]{1,0:T(8,128)(2,1)S(1)} custom-call(s32[4]{0:T(128)S(1)} %pad_add_fusion.here.refs_0_, bf16[16,16,128]{2,1,0:T(8,128)(2,1)S(1)} %collective-permute-done.p0, bf16[16,16,128]{2,1,0:T(8,128)(2,1)S(1)} %collective-permute-done.1.p1, bf16[16,16,128]{2,1,0:T(8,128)(2,1)S(1)} %collective-permute-done.2.p2, ...), custom_call_target="tpu_custom_call" | custom-call | tf_op jit(solution)/shard_map/pallas_call | solution.py:258
  17.1 3.3 %collective-permute-done.4 = bf16[64,16,128]{2,1,0:T(8,128)(2,1)S(1)} collective-permute-done((bf16[64,16,128]{2,1,0:T(8,128)(2,1)}, bf16[64,16,128]{2,1,0:T(8,128)(2,1)S(1)}, u32[]{:S(2)}, u32[]{:S(2)}) %collective-permute-start.4) | collective-permute-done | bytes 262176 | tf_op jit(solution)/shard_map/ppermute | solution.py:25
  20.4 3.0 %collective-permute-start.6 = (bf16[16,8192]{1,0:T(8,128)(2,1)S(1)}, bf16[16,8192]{1,0:T(8,128)(2,1)S(1)}, u32[]{:S(2)}, u32[]{:S(2)}) collective-permute-start(bf16[16,8192]{1,0:T(8,128)(2,1)S(1)} %shard_map.127.refs_7_), channel_id=1, source_target_pairs={{0,4},{1,5},{2,6},{3,7},{4,0},{5,1},{6,2},{7,3},{8,12},{9,13},{10,... | collective-permute-start | bytes 786440 | tf_op jit(solution)/shard_map/ppermute | solution.py:25
  23.4 3.0 %collective-permute-start.5 = (bf16[16,8192]{1,0:T(8,128)(2,1)S(1)}, bf16[16,8192]{1,0:T(8,128)(2,1)S(1)}, u32[]{:S(2)}, u32[]{:S(2)}) collective-permute-start(bf16[16,8192]{1,0:T(8,128)(2,1)S(1)} %shard_map.127.refs_7_), channel_id=1, source_target_pairs={{0,24},{1,25},{2,26},{3,27},{4,28},{5,29},{6,30},{7,31},{8,0},{9,1... | collective-permute-start | bytes 786440 | tf_op jit(solution)/shard_map/ppermute | solution.py:25
  26.7 3.2 %collective-permute-start.9 = (bf16[16,8192]{1,0:T(8,128)(2,1)S(1)}, bf16[16,8192]{1,0:T(8,128)(2,1)S(1)}, u32[]{:S(2)}, u32[]{:S(2)}) collective-permute-start(bf16[16,8192]{1,0:T(8,128)(2,1)S(1)} %shard_map.127.refs_7_), channel_id=1, source_target_pairs={{0,96},{1,97},{2,98},{3,99},{4,100},{5,101},{6,102},{7,103},{8,104... | collective-permute-start | bytes 786440 | tf_op jit(solution)/shard_map/ppermute | solution.py:25
  30.0 2.2 %collective-permute-start.7 = (bf16[16,8192]{1,0:T(8,128)(2,1)S(1)}, bf16[16,8192]{1,0:T(8,128)(2,1)S(1)}, u32[]{:S(2)}, u32[]{:S(2)}) collective-permute-start(bf16[16,8192]{1,0:T(8,128)(2,1)S(1)} %shard_map.127.refs_7_), channel_id=1, source_target_pairs={{0,16},{1,17},{2,18},{3,19},{4,20},{5,21},{6,22},{7,23},{8,24},{9,... | collective-permute-start | bytes 786440 | tf_op jit(solution)/shard_map/ppermute | solution.py:25
  32.2 1.4 %collective-permute-start.10 = (bf16[16,8192]{1,0:T(8,128)(2,1)S(1)}, bf16[16,8192]{1,0:T(8,128)(2,1)S(1)}, u32[]{:S(2)}, u32[]{:S(2)}) collective-permute-start(bf16[16,8192]{1,0:T(8,128)(2,1)S(1)} %shard_map.127.refs_7_), channel_id=1, source_target_pairs={{0,64},{1,65},{2,66},{3,67},{4,68},{5,69},{6,70},{7,71},{8,72},{9,... | collective-permute-start | bytes 786440 | tf_op jit(solution)/shard_map/ppermute | solution.py:25
  33.6 7.6 %shard_map.128.refs_14_.refs_10_ = bf16[32,512,128]{2,1,0:T(8,128)(2,1)} custom-call(bf16[64,512,128]{2,1,0:T(8,128)(2,1)} %pair.3, bf16[256,256]{1,0:T(8,128)(2,1)S(1)} %bitcast.31, bf16[256,256]{1,0:T(8,128)(2,1)S(1)} %bitcast.29, f32[1,256]{1,0:T(1,128)S(1)} %bitcast.37), custom_call_target="tpu_custom_call" | custom-call | flops 8000000000 | bytes 1048576 | tf_op jit(solution)/shard_map/pallas_call | solution.py:314
  41.2 1.5 %collective-permute-done.8.refs_10_ = bf16[16,8192]{1,0:T(8,128)(2,1)S(1)} collective-permute-done((bf16[16,8192]{1,0:T(8,128)(2,1)S(1)}, bf16[16,8192]{1,0:T(8,128)(2,1)S(1)}, u32[]{:S(2)}, u32[]{:S(2)}) %collective-permute-start.8) | collective-permute-done | bytes 262176 | tf_op jit(solution)/shard_map/ppermute | solution.py:25
  44.5 3.3 %collective-permute-start.12 = (bf16[80,4096]{1,0:T(8,128)(2,1)S(1)}, bf16[80,4096]{1,0:T(8,128)(2,1)S(1)}, u32[]{:S(2)}, u32[]{:S(2)}) collective-permute-start(bf16[80,4096]{1,0:T(8,128)(2,1)S(1)} %constant_dynamic-update-slice_fusion), channel_id=1, source_target_pairs={{0,96},{1,97},{2,98},{3,99},{4,100},{5,101},{6,102},{7,103},{8,104... | collective-permute-start | bytes 1966088 | tf_op jit(solution)/shard_map/ppermute | solution.py:25
  47.9 2.8 %collective-permute-start.14 = (bf16[80,4096]{1,0:T(8,128)(2,1)S(1)}, bf16[80,4096]{1,0:T(8,128)(2,1)S(1)}, u32[]{:S(2)}, u32[]{:S(2)}) collective-permute-start(bf16[80,4096]{1,0:T(8,128)(2,1)S(1)} %get-tuple-element.103), channel_id=1, source_target_pairs={{0,24},{1,25},{2,26},{3,27},{4,28},{5,29},{6,30},{7,31},{8,0},{9,1... | collective-permute-start | bytes 1966088 | tf_op jit(solution)/shard_map/ppermute | solution.py:25
  50.7 7.6 %shard_map.129.refs_15_.refs_11_ = bf16[32,512,128]{2,1,0:T(8,128)(2,1)} custom-call(bf16[64,512,128]{2,1,0:T(8,128)(2,1)} %pair.3, bf16[256,256]{1,0:T(8,128)(2,1)S(1)} %bitcast.32, bf16[256,256]{1,0:T(8,128)(2,1)S(1)} %bitcast.30, f32[1,256]{1,0:T(1,128)S(1)} %bitcast.38), custom_call_target="tpu_custom_call" | custom-call | flops 8000000000 | bytes 1048576 | tf_op jit(solution)/shard_map/pallas_call | solution.py:314
  58.4 5.8 %shard_map.130 = (bf16[32,256,256]{2,1,0:T(8,128)(2,1)S(1)}, bf16[256,256]{1,0:T(8,128)(2,1)S(1)}, f32[32,8,128]{2,1,0:T(8,128)S(1)}, f32[32,8,128]{2,1,0:T(8,128)S(1)}) custom-call(s32[4]{0:T(128)S(1)} %pad_add_fusion.here.refs_0_, bf16[2,64,16,128]{3,2,1,0:T(8,128)(2,1)S(1)} %pad_maximum_fusion.2.left_0, ...), custom_call_target="tpu_custom_call" | custom-call | flops 4000000000 | bytes 12582912 | tf_op jit(solution)/shard_map/pallas_call | solution.py:281
  65.0 2.9 %collective-permute-start.18 = (bf16[64,4096]{1,0:T(8,128)(2,1)S(1)}, bf16[64,4096]{1,0:T(8,128)(2,1)S(1)}, u32[]{:S(2)}, u32[]{:S(2)}) collective-permute-start(bf16[64,4096]{1,0:T(8,128)(2,1)S(1)} %get-tuple-element.94), channel_id=1, source_target_pairs={{0,96},{1,97},{2,98},{3,99},{4,100},{5,101},{6,102},{7,103},{8,104... | collective-permute-start | bytes 1572872 | tf_op jit(solution)/shard_map/ppermute | solution.py:25
  68.0 1.6 %collective-permute-start.21 = (bf16[64,4096]{1,0:T(8,128)(2,1)S(1)}, bf16[64,4096]{1,0:T(8,128)(2,1)S(1)}, u32[]{:S(2)}, u32[]{:S(2)}) collective-permute-start(bf16[64,4096]{1,0:T(8,128)(2,1)S(1)} %get-tuple-element.91), channel_id=1, source_target_pairs={{0,8},{1,9},{2,10},{3,11},{4,12},{5,13},{6,14},{7,15},{8,16},{9,17... | collective-permute-start | bytes 1572872 | tf_op jit(solution)/shard_map/ppermute | solution.py:25
  69.5 2.3 %collective-permute-start.20 = (bf16[64,4096]{1,0:T(8,128)(2,1)S(1)}, bf16[64,4096]{1,0:T(8,128)(2,1)S(1)}, u32[]{:S(2)}, u32[]{:S(2)}) collective-permute-start(bf16[64,4096]{1,0:T(8,128)(2,1)S(1)} %get-tuple-element.92), channel_id=1, source_target_pairs={{0,24},{1,25},{2,26},{3,27},{4,28},{5,29},{6,30},{7,31},{8,0},{9,1... | collective-permute-start | bytes 1572872 | tf_op jit(solution)/shard_map/ppermute | solution.py:25
  71.9 3.5 %collective-permute-start.22 = (bf16[32,8192]{1,0:T(8,128)(2,1)S(1)}, bf16[32,8192]{1,0:T(8,128)(2,1)S(1)}, u32[]{:S(2)}, u32[]{:S(2)}) collective-permute-start(bf16[32,8192]{1,0:T(8,128)(2,1)S(1)} %maximum_maximum_fusion.1), channel_id=1, source_target_pairs={{0,4},{1,5},{2,6},{3,7},{4,0},{5,1},{6,2},{7,3},{8,12},{9,13},{10,... | collective-permute-start | bytes 1572872 | tf_op jit(solution)/shard_map/ppermute | solution.py:25
  75.3 10.2 %shard_map.131.refs_16_ = bf16[64,512,128]{2,1,0:T(8,128)(2,1)} custom-call(s32[4]{0:T(128)S(1)} %pad_add_fusion.here.refs_0_, bf16[80,4096]{1,0:T(8,128)(2,1)S(1)} %collective-permute-done.12.refs_1_, bf16[64,4096]{1,0:T(8,128)(2,1)S(1)} %collective-permute-done.13.refs_2_, bf16[80,4096]{1,0:T(8,128)(2,1)S(1)} %collective-permute-done.14.refs_3_, ...), custom_call_target="tpu_custom_call" | custom-call | flops 6400000000 | bytes 16777216 | tf_op jit(solution)/shard_map/pallas_call | solution.py:237
  85.8 3.3 %collective-permute-start.23 = (bf16[32,4096]{1,0:T(8,128)(2,1)S(1)}, bf16[32,4096]{1,0:T(8,128)(2,1)S(1)}, u32[]{:S(2)}, u32[]{:S(2)}) collective-permute-start(bf16[32,4096]{1,0:T(8,128)(2,1)S(1)} %pad_maximum_fusion.9), channel_id=1, source_target_pairs={{0,96},{1,97},{2,98},{3,99},{4,100},{5,101},{6,102},{7,103},{8,104... | collective-permute-start | bytes 786440 | tf_op jit(solution)/shard_map/ppermute | solution.py:25
  89.1 3.5 %collective-permute-start.25 = (bf16[32,4096]{1,0:T(8,128)(2,1)S(1)}, bf16[32,4096]{1,0:T(8,128)(2,1)S(1)}, u32[]{:S(2)}, u32[]{:S(2)}) collective-permute-start(bf16[32,4096]{1,0:T(8,128)(2,1)S(1)} %pad_maximum_fusion.10), channel_id=1, source_target_pairs={{0,24},{1,25},{2,26},{3,27},{4,28},{5,29},{6,30},{7,31},{8,0},{9,1... | collective-permute-start | bytes 786440 | tf_op jit(solution)/shard_map/ppermute | solution.py:25
  92.6 6.0 %shard_map.132.refs_16_ = bf16[64,512,128]{2,1,0:T(8,128)(2,1)} custom-call(s32[4]{0:T(128)S(1)} %pad_add_fusion.here.refs_0_, bf16[80,4096]{1,0:T(8,128)(2,1)S(1)} %collective-permute-done.12.refs_1_, bf16[64,4096]{1,0:T(8,128)(2,1)S(1)} %collective-permute-done.13.refs_2_, ...), custom_call_target="tpu_custom_call", output_to_operand_aliasing={{}: (16, {})} | custom-call | flops 3200000000 | bytes 8388608 | tf_op jit(solution)/shard_map/pallas_call | solution.py:237
  98.7 6.0 %shard_map.133 = bf16[64,512,128]{2,1,0:T(8,128)(2,1)} custom-call(s32[4]{0:T(128)S(1)} %pad_add_fusion.here.refs_0_, bf16[64,4096]{1,0:T(8,128)(2,1)S(1)} %collective-permute-done.19.refs_6_.refs_1_, bf16[64,4096]{1,0:T(8,128)(2,1)S(1)} %collective-permute-done.20.refs_7_.refs_2_, ...), custom_call_target="tpu_custom_call", output_to_operand_aliasing={{}: (16, {})} | custom-call | flops 3200000000 | bytes 8388608 | tf_op jit(solution)/shard_map/pallas_call | solution.py:237
  (102 shorter events, 7.1 us)
Async XLA Ops:
  1.0 13.6 %collective-permute-start.3 = (bf16[16,16,128]{2,1,0:T(8,128)(2,1)S(1)}, bf16[16,16,128]{2,1,0:T(8,128)(2,1)S(1)}, u32[]{:S(2)}, u32[]{:S(2)}) collective-permute-start(bf16[16,16,128]{2,1,0:T(8,128)(2,1)S(1)} %get-tuple-element.111), channel_id=1, source_target_pairs={{0,96},{1,0},{2,32},{3,64},{4,100},{5,4},{6,36},{7,68},{8,104},{9,... | collective-permute-start | bytes 196616 | tf_op jit(solution)/shard_map/ppermute | solution.py:384
  5.2 9.4 %collective-permute-start.1 = (bf16[16,16,128]{2,1,0:T(8,128)(2,1)S(1)}, bf16[16,16,128]{2,1,0:T(8,128)(2,1)S(1)}, u32[]{:S(2)}, u32[]{:S(2)}) collective-permute-start(bf16[16,16,128]{2,1,0:T(8,128)(2,1)S(1)} %get-tuple-element.112), channel_id=1, source_target_pairs={{0,32},{1,64},{2,96},{3,0},{4,36},{5,68},{6,100},{7,4},{8,40},{9,7... | collective-permute-start | bytes 196616 | tf_op jit(solution)/shard_map/ppermute | solution.py:384
  5.5 9.1 %collective-permute-start = (bf16[16,16,128]{2,1,0:T(8,128)(2,1)S(1)}, bf16[16,16,128]{2,1,0:T(8,128)(2,1)S(1)}, u32[]{:S(2)}, u32[]{:S(2)}) collective-permute-start(bf16[16,16,128]{2,1,0:T(8,128)(2,1)S(1)} %get-tuple-element.113), channel_id=1, source_target_pairs={{0,0},{1,32},{2,64},{3,96},{4,4},{5,36},{6,68},{7,100},{8,8},{9,40... | collective-permute-start | bytes 196616 | tf_op jit(solution)/shard_map/ppermute | solution.py:384
  20.4 9.5 %collective-permute-start.6 = (bf16[16,8192]{1,0:T(8,128)(2,1)S(1)}, bf16[16,8192]{1,0:T(8,128)(2,1)S(1)}, u32[]{:S(2)}, u32[]{:S(2)}) collective-permute-start(bf16[16,8192]{1,0:T(8,128)(2,1)S(1)} %shard_map.127.refs_7_), channel_id=1, source_target_pairs={{0,4},{1,5},{2,6},{3,7},{4,0},{5,1},{6,2},{7,3},{8,12},{9,13},{10,... | collective-permute-start | bytes 786440 | tf_op jit(solution)/shard_map/ppermute | solution.py:25
  23.4 8.7 %collective-permute-start.5 = (bf16[16,8192]{1,0:T(8,128)(2,1)S(1)}, bf16[16,8192]{1,0:T(8,128)(2,1)S(1)}, u32[]{:S(2)}, u32[]{:S(2)}) collective-permute-start(bf16[16,8192]{1,0:T(8,128)(2,1)S(1)} %shard_map.127.refs_7_), channel_id=1, source_target_pairs={{0,24},{1,25},{2,26},{3,27},{4,28},{5,29},{6,30},{7,31},{8,0},{9,1... | collective-permute-start | bytes 786440 | tf_op jit(solution)/shard_map/ppermute | solution.py:25
  26.6 14.6 %collective-permute-start.11 = (bf16[16,8192]{1,0:T(8,128)(2,1)S(1)}, bf16[16,8192]{1,0:T(8,128)(2,1)S(1)}, u32[]{:S(2)}, u32[]{:S(2)}) collective-permute-start(bf16[16,8192]{1,0:T(8,128)(2,1)S(1)} %shard_map.127.refs_7_), channel_id=1, source_target_pairs={{0,32},{1,33},{2,34},{3,35},{4,36},{5,37},{6,38},{7,39},{8,40},{9,... | collective-permute-start | bytes 786440 | tf_op jit(solution)/shard_map/ppermute | solution.py:25
  26.7 14.5 %collective-permute-start.9 = (bf16[16,8192]{1,0:T(8,128)(2,1)S(1)}, bf16[16,8192]{1,0:T(8,128)(2,1)S(1)}, u32[]{:S(2)}, u32[]{:S(2)}) collective-permute-start(bf16[16,8192]{1,0:T(8,128)(2,1)S(1)} %shard_map.127.refs_7_), channel_id=1, source_target_pairs={{0,96},{1,97},{2,98},{3,99},{4,100},{5,101},{6,102},{7,103},{8,104... | collective-permute-start | bytes 786440 | tf_op jit(solution)/shard_map/ppermute | solution.py:25
  29.9 12.8 %collective-permute-start.8 = (bf16[16,8192]{1,0:T(8,128)(2,1)S(1)}, bf16[16,8192]{1,0:T(8,128)(2,1)S(1)}, u32[]{:S(2)}, u32[]{:S(2)}) collective-permute-start(bf16[16,8192]{1,0:T(8,128)(2,1)S(1)} %shard_map.127.refs_7_), channel_id=1, source_target_pairs={{0,8},{1,9},{2,10},{3,11},{4,12},{5,13},{6,14},{7,15},{8,16},{9,17... | collective-permute-start | bytes 786440 | tf_op jit(solution)/shard_map/ppermute | solution.py:25
  30.0 12.8 %collective-permute-start.7 = (bf16[16,8192]{1,0:T(8,128)(2,1)S(1)}, bf16[16,8192]{1,0:T(8,128)(2,1)S(1)}, u32[]{:S(2)}, u32[]{:S(2)}) collective-permute-start(bf16[16,8192]{1,0:T(8,128)(2,1)S(1)} %shard_map.127.refs_7_), channel_id=1, source_target_pairs={{0,16},{1,17},{2,18},{3,19},{4,20},{5,21},{6,22},{7,23},{8,24},{9,... | collective-permute-start | bytes 786440 | tf_op jit(solution)/shard_map/ppermute | solution.py:25
  32.2 10.6 %collective-permute-start.10 = (bf16[16,8192]{1,0:T(8,128)(2,1)S(1)}, bf16[16,8192]{1,0:T(8,128)(2,1)S(1)}, u32[]{:S(2)}, u32[]{:S(2)}) collective-permute-start(bf16[16,8192]{1,0:T(8,128)(2,1)S(1)} %shard_map.127.refs_7_), channel_id=1, source_target_pairs={{0,64},{1,65},{2,66},{3,67},{4,68},{5,69},{6,70},{7,71},{8,72},{9,... | collective-permute-start | bytes 786440 | tf_op jit(solution)/shard_map/ppermute | solution.py:25
  43.2 21.0 %collective-permute-start.13 = (bf16[64,4096]{1,0:T(8,128)(2,1)S(1)}, bf16[64,4096]{1,0:T(8,128)(2,1)S(1)}, u32[]{:S(2)}, u32[]{:S(2)}) collective-permute-start(bf16[64,4096]{1,0:T(8,128)(2,1)S(1)} %pad_maximum_fusion), channel_id=1, source_target_pairs={{0,32},{1,33},{2,34},{3,35},{4,36},{5,37},{6,38},{7,39},{8,40},{9,... | collective-permute-start | bytes 1572872 | tf_op jit(solution)/shard_map/ppermute | solution.py:25
  43.3 20.9 %collective-permute-start.16 = (bf16[32,8192]{1,0:T(8,128)(2,1)S(1)}, bf16[32,8192]{1,0:T(8,128)(2,1)S(1)}, u32[]{:S(2)}, u32[]{:S(2)}) collective-permute-start(bf16[32,8192]{1,0:T(8,128)(2,1)S(1)} %maximum_maximum_fusion), channel_id=1, source_target_pairs={{0,4},{1,5},{2,6},{3,7},{4,0},{5,1},{6,2},{7,3},{8,12},{9,13},{10,... | collective-permute-start | bytes 1572872 | tf_op jit(solution)/shard_map/ppermute | solution.py:25
  43.8 20.4 %collective-permute-start.15 = (bf16[64,4096]{1,0:T(8,128)(2,1)S(1)}, bf16[64,4096]{1,0:T(8,128)(2,1)S(1)}, u32[]{:S(2)}, u32[]{:S(2)}) collective-permute-start(bf16[64,4096]{1,0:T(8,128)(2,1)S(1)} %pad_maximum_fusion.1), channel_id=1, source_target_pairs={{0,8},{1,9},{2,10},{3,11},{4,12},{5,13},{6,14},{7,15},{8,16},{9,17... | collective-permute-start | bytes 1572872 | tf_op jit(solution)/shard_map/ppermute | solution.py:25
  44.5 19.7 %collective-permute-start.12 = (bf16[80,4096]{1,0:T(8,128)(2,1)S(1)}, bf16[80,4096]{1,0:T(8,128)(2,1)S(1)}, u32[]{:S(2)}, u32[]{:S(2)}) collective-permute-start(bf16[80,4096]{1,0:T(8,128)(2,1)S(1)} %constant_dynamic-update-slice_fusion), channel_id=1, source_target_pairs={{0,96},{1,97},{2,98},{3,99},{4,100},{5,101},{6,102},{7,103},{8,104... | collective-permute-start | bytes 1966088 | tf_op jit(solution)/shard_map/ppermute | solution.py:25
  47.9 16.3 %collective-permute-start.14 = (bf16[80,4096]{1,0:T(8,128)(2,1)S(1)}, bf16[80,4096]{1,0:T(8,128)(2,1)S(1)}, u32[]{:S(2)}, u32[]{:S(2)}) collective-permute-start(bf16[80,4096]{1,0:T(8,128)(2,1)S(1)} %get-tuple-element.103), channel_id=1, source_target_pairs={{0,24},{1,25},{2,26},{3,27},{4,28},{5,29},{6,30},{7,31},{8,0},{9,1... | collective-permute-start | bytes 1966088 | tf_op jit(solution)/shard_map/ppermute | solution.py:25
  64.6 20.9 %collective-permute-start.19 = (bf16[64,4096]{1,0:T(8,128)(2,1)S(1)}, bf16[64,4096]{1,0:T(8,128)(2,1)S(1)}, u32[]{:S(2)}, u32[]{:S(2)}) collective-permute-start(bf16[64,4096]{1,0:T(8,128)(2,1)S(1)} %get-tuple-element.93), channel_id=1, source_target_pairs={{0,32},{1,33},{2,34},{3,35},{4,36},{5,37},{6,38},{7,39},{8,40},{9,... | collective-permute-start | bytes 1572872 | tf_op jit(solution)/shard_map/ppermute | solution.py:25
  65.0 20.5 %collective-permute-start.18 = (bf16[64,4096]{1,0:T(8,128)(2,1)S(1)}, bf16[64,4096]{1,0:T(8,128)(2,1)S(1)}, u32[]{:S(2)}, u32[]{:S(2)}) collective-permute-start(bf16[64,4096]{1,0:T(8,128)(2,1)S(1)} %get-tuple-element.94), channel_id=1, source_target_pairs={{0,96},{1,97},{2,98},{3,99},{4,100},{5,101},{6,102},{7,103},{8,104... | collective-permute-start | bytes 1572872 | tf_op jit(solution)/shard_map/ppermute | solution.py:25
  68.0 17.5 %collective-permute-start.21 = (bf16[64,4096]{1,0:T(8,128)(2,1)S(1)}, bf16[64,4096]{1,0:T(8,128)(2,1)S(1)}, u32[]{:S(2)}, u32[]{:S(2)}) collective-permute-start(bf16[64,4096]{1,0:T(8,128)(2,1)S(1)} %get-tuple-element.91), channel_id=1, source_target_pairs={{0,8},{1,9},{2,10},{3,11},{4,12},{5,13},{6,14},{7,15},{8,16},{9,17... | collective-permute-start | bytes 1572872 | tf_op jit(solution)/shard_map/ppermute | solution.py:25
  69.5 16.0 %collective-permute-start.20 = (bf16[64,4096]{1,0:T(8,128)(2,1)S(1)}, bf16[64,4096]{1,0:T(8,128)(2,1)S(1)}, u32[]{:S(2)}, u32[]{:S(2)}) collective-permute-start(bf16[64,4096]{1,0:T(8,128)(2,1)S(1)} %get-tuple-element.92), channel_id=1, source_target_pairs={{0,24},{1,25},{2,26},{3,27},{4,28},{5,29},{6,30},{7,31},{8,0},{9,1... | collective-permute-start | bytes 1572872 | tf_op jit(solution)/shard_map/ppermute | solution.py:25
  71.9 13.7 %collective-permute-start.22 = (bf16[32,8192]{1,0:T(8,128)(2,1)S(1)}, bf16[32,8192]{1,0:T(8,128)(2,1)S(1)}, u32[]{:S(2)}, u32[]{:S(2)}) collective-permute-start(bf16[32,8192]{1,0:T(8,128)(2,1)S(1)} %maximum_maximum_fusion.1), channel_id=1, source_target_pairs={{0,4},{1,5},{2,6},{3,7},{4,0},{5,1},{6,2},{7,3},{8,12},{9,13},{10,... | collective-permute-start | bytes 1572872 | tf_op jit(solution)/shard_map/ppermute | solution.py:25
  85.6 13.1 %collective-permute-start.26 = (bf16[16,4096]{1,0:T(8,128)(2,1)S(1)}, bf16[16,4096]{1,0:T(8,128)(2,1)S(1)}, u32[]{:S(2)}, u32[]{:S(2)}) collective-permute-start(bf16[16,4096]{1,0:T(8,128)(2,1)S(1)} %slice.103), channel_id=1, source_target_pairs={{0,8},{1,9},{2,10},{3,11},{4,12},{5,13},{6,14},{7,15},{8,16},{9,17... | collective-permute-start | bytes 393224 | tf_op jit(solution)/shard_map/ppermute | solution.py:25
  85.7 13.0 %collective-permute-start.24 = (bf16[16,4096]{1,0:T(8,128)(2,1)S(1)}, bf16[16,4096]{1,0:T(8,128)(2,1)S(1)}, u32[]{:S(2)}, u32[]{:S(2)}) collective-permute-start(bf16[16,4096]{1,0:T(8,128)(2,1)S(1)} %slice.100), channel_id=1, source_target_pairs={{0,32},{1,33},{2,34},{3,35},{4,36},{5,37},{6,38},{7,39},{8,40},{9,... | collective-permute-start | bytes 393224 | tf_op jit(solution)/shard_map/ppermute | solution.py:25
  85.8 12.9 %collective-permute-start.23 = (bf16[32,4096]{1,0:T(8,128)(2,1)S(1)}, bf16[32,4096]{1,0:T(8,128)(2,1)S(1)}, u32[]{:S(2)}, u32[]{:S(2)}) collective-permute-start(bf16[32,4096]{1,0:T(8,128)(2,1)S(1)} %pad_maximum_fusion.9), channel_id=1, source_target_pairs={{0,96},{1,97},{2,98},{3,99},{4,100},{5,101},{6,102},{7,103},{8,104... | collective-permute-start | bytes 786440 | tf_op jit(solution)/shard_map/ppermute | solution.py:25
  89.1 9.6 %collective-permute-start.25 = (bf16[32,4096]{1,0:T(8,128)(2,1)S(1)}, bf16[32,4096]{1,0:T(8,128)(2,1)S(1)}, u32[]{:S(2)}, u32[]{:S(2)}) collective-permute-start(bf16[32,4096]{1,0:T(8,128)(2,1)S(1)} %pad_maximum_fusion.10), channel_id=1, source_target_pairs={{0,24},{1,25},{2,26},{3,27},{4,28},{5,29},{6,30},{7,31},{8,0},{9,1... | collective-permute-start | bytes 786440 | tf_op jit(solution)/shard_map/ppermute | solution.py:25
  (14 other events, 148.4 us)

commit v3 on v2

--- a/solution.py
+++ b/solution.py
@@ -12,6 +12,8 @@
 BF16, F32 = jnp.bfloat16, jnp.float32
 DEVICES = [(z, y, x, c) for z in range(4) for y in range(4) for x in range(2) for c in range(4)]
 MIB = 1 << 20
+PARTS = 4
+GATE_FIRST = 16
 
 
 def device_id(z, y, x, c):
@@ -37,11 +39,15 @@
     return np.array(order)
 
 
-def norm_rows(values, average, gain, bias):
+def standardize(values, average):
     mean = jnp.dot(values, average, preferred_element_type=F32)
     centered = values.astype(F32) - mean
     var = jnp.dot((centered * centered).astype(BF16), average, preferred_element_type=F32)
-    return (centered * lax.rsqrt(var + 1e-05) * gain.reshape(1, 128) + bias.reshape(1, 128)).astype(BF16)
+    return centered * lax.rsqrt(var + 1e-05)
+
+
+def scale(values, gain, bias):
+    return (values * gain.reshape(1, 128) + bias.reshape(1, 128)).astype(BF16)
 
 
 def project_16(normed, weight, swap, store):
@@ -60,19 +66,31 @@
         store(h, swap[h].astype(BF16))
 
 
-def right_kernel(here, p0, p1, p2, p3, gain_in, bias_in, weight_in, out, normed, swap, gain, bias, weight, sem):
-    fetches = [
-        pltpu.make_async_copy(source, target, sem.at[n])
-        for n, (source, target) in enumerate(((gain_in, gain), (bias_in, bias), (weight_in, weight)))
-    ]
+def prepare_kernel(gain_in, bias_in, right_in, gate_in, gain, bias, right, wide, shift, gain_row, bias_row, gate, sem):
+    pairs = ((gain_in, gain_row), (bias_in, bias_row), (right_in, right), (gate_in, gate))
+    fetches = [pltpu.make_async_copy(source, target, sem.at[n]) for n, (source, target) in enumerate(pairs)]
     for fetch in fetches:
         fetch.start()
     for fetch in fetches:
         fetch.wait()
+    gain[...] = gain_row[...].reshape(1, 128)
+    bias[...] = bias_row[...].reshape(1, 128)
+    half = 0.5 * gate[...].astype(F32)
+    block = (jnp.broadcast_to(gain[...], (128, 128)).T * half).astype(BF16)
+    wide[...] = jnp.zeros((256, 256), BF16)
+    wide[:128, :128] = block
+    wide[128:, 128:] = block
+    rows = jnp.broadcast_to(bias[...], (8, 128))
+    made = jnp.dot(rows, half, preferred_element_type=F32, precision=lax.Precision.HIGHEST)[:1]
+    shift[:, :128] = made
+    shift[:, 128:] = made
+
+
+def right_kernel(here, p0, p1, p2, p3, gain, bias, weight, out, normed, swap):
     average = jnp.full((128, 128), 1 / 128, BF16)
     for s, piece in enumerate((p0, p1, p2, p3)):
         start = pl.multiple_of(lax.rem(here[0] - s + 4, 4) * 16, 16)
-        made = norm_rows(piece[...].reshape(256, 128), average, gain[...], bias[...])
+        made = scale(standardize(piece[...].reshape(256, 128), average), gain[...], bias[...])
         normed[:, pl.ds(start, 16), :] = made.reshape(16, 16, 128)
 
     def store(h, tile):
@@ -91,7 +109,7 @@
         for flip in range(4):
             piece = (left_0, left_1)[flip % 2][flip // 2, at].reshape(256, 128)
             start = pl.multiple_of((here[3] ^ flip) * 16, 16)
-            made = norm_rows(piece, average[...], gain[...], bias[...])
+            made = scale(standardize(piece, average[...]), gain[...], bias[...])
             mine[:, pl.ds(start, 16), :] = made.reshape(16, 16, 128)
 
         def store(h, tile, at=at):
@@ -133,13 +151,12 @@
         out[i], out[i + 1] = gate[:, :128], gate[:, 128:]
 
 
-def gate_kernel(half, pair, average, weight, bias, out):
-    rows, first = 8, half * 4
+def gate_kernel(first, pair, average, weight, bias, out):
     pltpu.emit_pipeline(
         functools.partial(gate_block, average, weight, bias),
-        grid=(4,),
-        in_specs=[pl.BlockSpec((rows, 512, 128), lambda n: (n + first, 0, 0))],
-        out_specs=[pl.BlockSpec((rows, 512, 128), lambda n: (n, 0, 0))],
+        grid=(out.shape[0] // 16,),
+        in_specs=[pl.BlockSpec((16, 512, 128), lambda n: (n + first, 0, 0))],
+        out_specs=[pl.BlockSpec((16, 512, 128), lambda n: (n, 0, 0))],
     )(pair, out)
 
 
@@ -148,7 +165,7 @@
     sources = refs[1 : 1 + n_src]
     gate_0, gate_1, lbd, wide_out, gain, bias = refs[1 + n_src : 7 + n_src]
     refs = refs[7 + n_src + has_out :]
-    out, right, product, gates, results, gate_sem, out_sem = refs
+    out, product, gates, results, gate_sem, out_sem = refs
     z, y, x = here[0], here[1], here[2]
     columns = 16 * len(blocks)
 
@@ -160,12 +177,12 @@
     def gate_copy(b, half):
         return pltpu.make_async_copy(
             (gate_0, gate_1)[half].at[:, column(b), :],
-            gates.at[pl.ds(half * 32, 32), pl.ds(b * 16, 16), :],
+            gates.at[pl.ds(half * GATE_FIRST, (GATE_FIRST, 64 - GATE_FIRST)[half]), pl.ds(b * 16, 16), :],
             gate_sem.at[b, half],
         )
 
     def out_copy(b, q):
-        rows = pl.ds(q * 16, 16)
+        rows = pl.ds(q * 64 // PARTS, 64 // PARTS)
         return pltpu.make_async_copy(
             results.at[rows, pl.ds(b * 16, 16), :], out.at[rows, column(b), :], out_sem.at[b, q]
         )
@@ -181,19 +198,24 @@
         swapped = jnp.where(lax.rem(member, 4) < 2, pltpu.roll(total, 6, 0), pltpu.roll(total, 2, 0))
         return total + swapped
 
-    for b, (_, halves) in enumerate(blocks):
-        for half, (src, row, lane) in enumerate(halves):
-            right[b * 16 : b * 16 + 16, half * 4096 : half * 4096 + 4096] = sources[src][
-                row : row + 16, lane : lane + 4096
-            ]
-
-    def multiply(g, carry):
-        panel = right[:, pl.ds(pl.multiple_of(g * 256, 256), 256)]
-        made = lax.dot_general(lbd[g], panel, (((1,), (1,)), ((), ())), preferred_element_type=F32)
-        product[:, g] = made.reshape(32, 8, columns)
-        return carry
-
-    lax.fori_loop(0, 32, multiply, 0, unroll=16)
+    for half in range(2):
+
+        def multiply(g, carry, half=half):
+            parts = []
+            for _, halves in blocks:
+                src, row, lane = halves[half]
+                at = pl.ds(pl.multiple_of(lane + g * 256, 256), 256)
+                parts.append(sources[src][row : row + 16, at])
+            made = lax.dot_general(
+                lbd[half * 16 + g],
+                jnp.concatenate(parts, 0),
+                (((1,), (1,)), ((), ())),
+                preferred_element_type=F32,
+            )
+            product[:, half * 16 + g] = made.reshape(32, 8, columns)
+            return carry
+
+        lax.fori_loop(0, 16, multiply, 0, unroll=16)
     for b in range(len(blocks)):
         gate_copy(b, 0).wait()
         gate_copy(b, 1).wait()
@@ -216,12 +238,12 @@
                 results[row, lanes] = (both[:, i2 * 128 : (i2 + 1) * 128] * gate).astype(BF16)
         return carry
 
-    for q in range(4):
-        lax.fori_loop(q * 8, q * 8 + 8, finish, 0, unroll=8 * 128 // columns)
+    for q in range(PARTS):
+        lax.fori_loop(q * 32 // PARTS, (q + 1) * 32 // PARTS, finish, 0, unroll=8)
         for b in range(len(blocks)):
             out_copy(b, q).start()
     for b in range(len(blocks)):
-        for q in range(4):
+        for q in range(PARTS):
             out_copy(b, q).wait()
 
 
@@ -240,36 +262,50 @@
         in_specs=[SMEM] + [VMEM] * len(sources) + [HBM] * 2 + [VMEM] * 4 + [HBM] * has_out,
         out_specs=HBM,
         scratch_shapes=[
-            pltpu.VMEM((n * 16, 8192), BF16),
             pltpu.VMEM((32, 32, 8, n * 16), F32),
             pltpu.VMEM((64, n * 16, 128), BF16),
             pltpu.VMEM((64, n * 16, 128), BF16),
             pltpu.SemaphoreType.DMA((n, 2)),
-            pltpu.SemaphoreType.DMA((n, 4)),
+            pltpu.SemaphoreType.DMA((n, PARTS)),
         ],
         input_output_aliases={len(args) - 1: 0} if has_out else {},
-        compiler_params=pltpu.CompilerParams(vmem_limit_bytes=(8 + 3 * n // 2) * MIB),
+        compiler_params=pltpu.CompilerParams(vmem_limit_bytes=(8 + 5 * n // 4) * MIB),
         cost_estimate=pl.CostEstimate(flops=n * 4 * 10**8, bytes_accessed=n * MIB, transcendentals=0),
     )(*args)
 
 
-def run_right(here, pieces, *weights):
+def run_prepare(*weights):
     weights = [pltpu.with_memory_space_constraint(w, pltpu.HBM) for w in weights]
+    return pl.pallas_call(
+        prepare_kernel,
+        out_shape=[
+            jax.ShapeDtypeStruct((1, 128), F32),
+            jax.ShapeDtypeStruct((1, 128), F32),
+            jax.ShapeDtypeStruct((128, 256), BF16),
+            jax.ShapeDtypeStruct((256, 256), BF16),
+            jax.ShapeDtypeStruct((1, 256), F32),
+        ],
+        in_specs=[HBM] * 4,
+        out_specs=[VMEM] * 5,
+        scratch_shapes=[
+            pltpu.VMEM((128,), F32),
+            pltpu.VMEM((128,), F32),
+            pltpu.VMEM((128, 128), BF16),
+            pltpu.SemaphoreType.DMA((4,)),
+        ],
+        compiler_params=pltpu.CompilerParams(vmem_limit_bytes=4 * MIB),
+    )(*weights)
+
+
+def run_right(here, pieces, gain, bias, weight):
     return pl.pallas_call(
         right_kernel,
         out_shape=jax.ShapeDtypeStruct((16, 8192), BF16),
-        in_specs=[SMEM] + [VMEM] * 4 + [HBM] * 3,
+        in_specs=[SMEM] + [VMEM] * 7,
         out_specs=VMEM,
-        scratch_shapes=[
-            pltpu.VMEM((16, 64, 128), BF16),
-            pltpu.VMEM((64, 16, 128), F32),
-            pltpu.VMEM((128,), F32),
-            pltpu.VMEM((128,), F32),
-            pltpu.VMEM((128, 256), BF16),
-            pltpu.SemaphoreType.DMA((3,)),
-        ],
-        compiler_params=pltpu.CompilerParams(vmem_limit_bytes=16 * MIB),
-    )(here, *pieces, *weights)
+        scratch_shapes=[pltpu.VMEM((16, 64, 128), BF16), pltpu.VMEM((64, 16, 128), F32)],
+        compiler_params=pltpu.CompilerParams(vmem_limit_bytes=8 * MIB),
+    )(here, *pieces, gain, bias, weight)
 
 
 def run_left(here, left_0, left_1, gain, bias, weight, w_out, out_gain, out_bias):
@@ -301,23 +337,15 @@
     )
 
 
-def gate_weights(gain, bias, weight):
-    eye = jnp.eye(2, dtype=F32)
-    weight = weight.astype(F32)
-    wide = jnp.kron(eye, gain.reshape(128, 1) * weight * 0.5).astype(BF16)
-    shift = 0.5 * jnp.dot(bias, weight, precision=lax.Precision.HIGHEST)
-    return wide, jnp.tile(shift, (1, 2))
-
-
-def run_gate(half, pair, wide, shift):
+def run_gate(first, rows, pair, wide, shift):
     average = jnp.kron(jnp.eye(2, dtype=BF16), jnp.full((128, 128), 1 / 128, BF16))
     return pl.pallas_call(
-        functools.partial(gate_kernel, half),
-        out_shape=pltpu.HBM((32, 512, 128), BF16),
+        functools.partial(gate_kernel, first // 16),
+        out_shape=pltpu.HBM((rows, 512, 128), BF16),
         in_specs=[HBM, VMEM, VMEM, VMEM],
         out_specs=HBM,
-        compiler_params=pltpu.CompilerParams(vmem_limit_bytes=20 * MIB),
-        cost_estimate=pl.CostEstimate(flops=8 * 10**9, bytes_accessed=1 * MIB, transcendentals=0),
+        compiler_params=pltpu.CompilerParams(vmem_limit_bytes=24 * MIB),
+        cost_estimate=pl.CostEstimate(flops=rows * 2 * 10**8, bytes_accessed=MIB, transcendentals=0),
     )(pltpu.with_memory_space_constraint(pair, pltpu.HBM), average, wide, shift)
 
 
@@ -331,7 +359,7 @@
     if far == 0:
         if near == 0:
             return "X0", 0
-        return (f"{other}1", 64) if near == 1 else ("X2", (near - 2) * 16)
+        return (f"{other}3", 64) if near == 3 else ("X2", (near - 1) * 16)
     if far != 2:
         if near == 0:
             return f"{first}{far}", 48
@@ -373,20 +401,19 @@
     row = lax.axis_index("row")
     z, y, x = row // 8, (row // 2) % 4, row % 2
     c = lax.axis_index("col")
-    gain, bias = ln_gain.reshape(1, 128), ln_bias.reshape(1, 128)
 
     here = jnp.stack([z, y, x, c]).astype(jnp.int32)
 
+    parts = [lax.dynamic_slice_in_dim(right_panel, ((c + s) % 4) * 16, 16, 0) for s in range(4)]
+    parts, weights = lax.optimization_barrier((parts, (ln_gain, ln_bias, w_right, w_gate)))
+    gain, bias, weight, wide, shift = run_prepare(*weights)
     pieces = []
     for s in range(4):
         pairs = [(device_id(z_, y_, x_, c_), device_id(c_ + s, y_, x_, z_)) for z_, y_, x_, c_ in DEVICES]
-        part = lax.dynamic_slice_in_dim(right_panel, ((c + s) % 4) * 16, 16, 0)
-        pieces.append(lax.ppermute(part, AXES, pairs))
-    rows = run_right(here, pieces, ln_gain, ln_bias, w_right)
-    left_2 = move(left_panel, dc=2)
-    rows, left_2, wide_gate = lax.optimization_barrier(
-        (rows, left_2, gate_weights(ln_gain, ln_bias, w_gate))
-    )
+        pieces.append(lax.ppermute(parts[s], AXES, pairs))
+    rows = run_right(here, pieces, gain, bias, weight)
+    rows, wide, shift = lax.optimization_barrier((rows, wide, shift))
+    wide_gate = (wide, shift)
 
     def cat(*parts):
         return jnp.concatenate(parts, 0)
@@ -417,27 +444,29 @@
     got["Y2"] = move(again, dy=2)
     got["Y1"], again = lax.optimization_barrier((got["Y1"], again))
     got["Z2"] = move(again, dz=2)
-    gate_0 = run_gate(0, pair_block, *wide_gate)
+    got["Y3"], again = lax.optimization_barrier((got["Y3"], left_panel))
+    left_2 = move(again, dc=2)
+    gate_0 = run_gate(0, GATE_FIRST, pair_block, *wide_gate)
     ones = ("Y1", "Y2", "Y3", "Z1", "Z2", "Z3", "X0")
-    gate_0, left_2 = together(*ones, more=[gate_0, left_2])
+    (gate_0,) = together(*ones, more=[gate_0])
     half_a = [got[n][:, :4096] for n in ones]
     half_b = [got[n][:, 4096:] for n in ones]
     to_z, to_y = cat(*half_a[:3], half_a[6]), cat(*half_b[3:])
-    got["A1"], got["A3"] = move(cat(to_z, half_b[6]), dz=-1), move(to_z, dz=1)
-    got["B1"], got["B3"] = move(cat(to_y, half_a[6]), dy=-1), move(to_y, dy=1)
-    got["X2"] = move(halves(cat(*half_a[1:3]), cat(*half_b[4:6])), dx=1)
+    got["A1"], got["A3"] = move(to_z, dz=-1), move(cat(to_z, half_b[6]), dz=1)
+    got["B1"], got["B3"] = move(to_y, dy=-1), move(cat(to_y, half_a[6]), dy=1)
+    got["X2"] = move(halves(cat(*half_a[:2]), cat(*half_b[3:5])), dx=1)
     left_0 = jnp.stack([left_panel, left_2])
     left_1 = move(left_0, dc=1)
-    gate_1 = run_gate(1, pair_block, *wide_gate)
+    gate_1 = run_gate(GATE_FIRST, 64 - GATE_FIRST, pair_block, *wide_gate)
     lbd, wide_out, gain_out, bias_out = run_left(
         here, left_0, left_1, gain, bias, w_left, w_out, out_gain, out_bias
     )
     gate_1, lbd = together("A1", "A3", "B1", "B3", "X2", more=[gate_1, lbd])
     gates = (gate_0, gate_1)
     a1, a3, b1, b3, x2 = (got[n] for n in ("A1", "A3", "B1", "B3", "X2"))
-    xa, xb = cat(b1[64:], x2[16:, :4096]), cat(a1[64:], x2[16:, 4096:])
-    got["PA1"], got["PA3"] = move(cat(xa, a1[:32]), dz=-1), move(cat(xa, a3[32:]), dz=1)
-    got["PB1"], got["PB3"] = move(cat(xb, b1[:32]), dy=-1), move(cat(xb, b3[32:]), dy=1)
+    xa, xb = cat(x2[:16, :4096], b3[64:]), cat(x2[:16, 4096:], a3[64:])
+    got["PA1"], got["PA3"] = move(cat(xa, a1[:32]), dz=-1), move(cat(xa, a3[32:64]), dz=1)
+    got["PB1"], got["PB3"] = move(cat(xb, b1[:32]), dy=-1), move(cat(xb, b3[32:64]), dy=1)
     got["X3"] = move(halves(cat(a1[16:32], a3[16:32]), cat(b1[16:32], b3[16:32])), dx=1)
     out = call(EARLY, None)
     (out,) = together("PA1", "PA3", "PB1", "PB3", "X3", more=[out])

time: 105 us -> 104 us (level)
  starting transfers between devices: 49.5 us -> 51.6 us
  Pallas kernels: 45.7 us -> 43.7 us
    ppermute x23, starting transfers between devices: 37.9 us -> 40.9 us  [move(): return lax.ppermute(value, AXES, pairs)]
    pallas_call x3, Pallas kernels: 22.1 us -> 20.3 us  [run_update(): pl.pallas_call(functools.partial(update_kernel, blocks, len(sources), has...]
    ppermute x4, waiting for transfers between devices: 0.01 us -> 1.54 us  [per_device(): pieces.append(lax.ppermute(parts[s], AXES, pairs))]
    ppermute x23, waiting for transfers between devices: 4.9 us -> 3.8 us  [move(): return lax.ppermute(value, AXES, pairs)]
    pallas_call x2 -> x3, Pallas kernels: 15.2 us -> 16.1 us  [the longest x2 15 us: run_gate(): pl.pallas_call(functools.partial(gate_kernel, first // 16), out_shape=plt...]
  transfers between devices with their start and end apart: 27 -> 27, of which waited for: 2 -> 6; matrix products, arithmetic and copies ran while one was open for 3% -> 1% of each run, Pallas kernels for 38% -> 35%
where the time goes in v3:
time: 104 us
  starting transfers between devices  51.6 us (50%)
  Pallas kernels  43.7 us (42%)
  waiting for transfers between devices  5.34 us (5%)
  local copies, waits for them, and re-layouts  1.6 us (2%)
    ppermute x23, starting transfers between devices, move(): return lax.ppermute(value, AXES, pairs)  40.9 us
    pallas_call x3, Pallas kernels, run_update(): pl.pallas_call(functools.partial(update_kernel, blocks, len(sources), has...  20.3 us
    pallas_call x2, Pallas kernels, run_gate(): pl.pallas_call(functools.partial(gate_kernel, first // 16), out_shape=plt...  15 us
    ppermute x4, starting transfers between devices, per_device(): pieces.append(lax.ppermute(parts[s], AXES, pairs))  10.7 us
    pallas_call x1, Pallas kernels, run_left(): pl.pallas_call(left_kernel, out_shape=[jax.ShapeDtypeStruct((32, 256, 256...  5.76 us
    ppermute x23, waiting for transfers between devices, move(): return lax.ppermute(value, AXES, pairs)  3.8 us
  transfers between devices with their start and end apart: 27, of which 6 were waited for; matrix products, arithmetic and copies ran while one was open for 1% of the time, Pallas kernels for 35%

profile of v3, /device:TPU:0, one launch (start us, length us, event | category | flops | bytes accessed | tf_op | source)
XLA Modules:
  0.0 103.5 jit_solution(13804551759043292537)
XLA Ops:
  1.7 3.3 %collective-permute-start.1 = (bf16[16,16,128]{2,1,0:T(8,128)(2,1)S(1)}, bf16[16,16,128]{2,1,0:T(8,128)(2,1)S(1)}, u32[]{:S(2)}, u32[]{:S(2)}) collective-permute-start(bf16[16,16,128]{2,1,0:T(8,128)(2,1)S(1)} %get-tuple-element.58), channel_id=1, source_target_pairs={{0,32},{1,64},{2,96},{3,0},{4,36},{5,68},{6,100},{7,4},{8,40},{9,7... | collective-permute-start | bytes 196616 | tf_op jit(solution)/shard_map/ppermute | solution.py:413
  5.0 4.3 %collective-permute-start.2 = (bf16[16,16,128]{2,1,0:T(8,128)(2,1)S(1)}, bf16[16,16,128]{2,1,0:T(8,128)(2,1)S(1)}, u32[]{:S(2)}, u32[]{:S(2)}) collective-permute-start(bf16[16,16,128]{2,1,0:T(8,128)(2,1)S(1)} %get-tuple-element.59), channel_id=1, source_target_pairs={{0,64},{1,96},{2,0},{3,32},{4,68},{5,100},{6,4},{7,36},{8,72},{9,1... | collective-permute-start | bytes 196616 | tf_op jit(solution)/shard_map/ppermute | solution.py:413
  9.3 2.3 %collective-permute-start.3 = (bf16[16,16,128]{2,1,0:T(8,128)(2,1)S(1)}, bf16[16,16,128]{2,1,0:T(8,128)(2,1)S(1)}, u32[]{:S(2)}, u32[]{:S(2)}) collective-permute-start(bf16[16,16,128]{2,1,0:T(8,128)(2,1)S(1)} %get-tuple-element.60), channel_id=1, source_target_pairs={{0,96},{1,0},{2,32},{3,64},{4,100},{5,4},{6,36},{7,68},{8,104},{9,... | collective-permute-start | bytes 196616 | tf_op jit(solution)/shard_map/ppermute | solution.py:413
  16.0 1.6 %collective-permute-start.7 = (bf16[16,8192]{1,0:T(8,128)(2,1)S(1)}, bf16[16,8192]{1,0:T(8,128)(2,1)S(1)}, u32[]{:S(2)}, u32[]{:S(2)}) collective-permute-start(bf16[16,8192]{1,0:T(8,128)(2,1)S(1)} %shard_map.128.refs_7_), channel_id=1, source_target_pairs={{0,8},{1,9},{2,10},{3,11},{4,12},{5,13},{6,14},{7,15},{8,16},{9,17... | collective-permute-start | bytes 786440 | tf_op jit(solution)/shard_map/ppermute | solution.py:27
  17.6 2.8 %collective-permute-start.5 = (bf16[16,8192]{1,0:T(8,128)(2,1)S(1)}, bf16[16,8192]{1,0:T(8,128)(2,1)S(1)}, u32[]{:S(2)}, u32[]{:S(2)}) collective-permute-start(bf16[16,8192]{1,0:T(8,128)(2,1)S(1)} %shard_map.128.refs_7_), channel_id=1, source_target_pairs={{0,4},{1,5},{2,6},{3,7},{4,0},{5,1},{6,2},{7,3},{8,12},{9,13},{10,... | collective-permute-start | bytes 786440 | tf_op jit(solution)/shard_map/ppermute | solution.py:27
  20.4 1.7 %collective-permute-start.4 = (bf16[16,8192]{1,0:T(8,128)(2,1)S(1)}, bf16[16,8192]{1,0:T(8,128)(2,1)S(1)}, u32[]{:S(2)}, u32[]{:S(2)}) collective-permute-start(bf16[16,8192]{1,0:T(8,128)(2,1)S(1)} %shard_map.128.refs_7_), channel_id=1, source_target_pairs={{0,24},{1,25},{2,26},{3,27},{4,28},{5,29},{6,30},{7,31},{8,0},{9,1... | collective-permute-start | bytes 786440 | tf_op jit(solution)/shard_map/ppermute | solution.py:27
  22.3 2.4 %collective-permute-start.10 = (bf16[16,8192]{1,0:T(8,128)(2,1)S(1)}, bf16[16,8192]{1,0:T(8,128)(2,1)S(1)}, u32[]{:S(2)}, u32[]{:S(2)}) collective-permute-start(bf16[16,8192]{1,0:T(8,128)(2,1)S(1)} %shard_map.128.refs_7_), channel_id=1, source_target_pairs={{0,32},{1,33},{2,34},{3,35},{4,36},{5,37},{6,38},{7,39},{8,40},{9,... | collective-permute-start | bytes 786440 | tf_op jit(solution)/shard_map/ppermute | solution.py:27
  26.1 1.6 %collective-permute-start.16 = (bf16[64,16,128]{2,1,0:T(8,128)(2,1)}, bf16[64,16,128]{2,1,0:T(8,128)(2,1)S(1)}, u32[]{:S(2)}, u32[]{:S(2)}) collective-permute-start(bf16[64,16,128]{2,1,0:T(8,128)(2,1)} %param.14), channel_id=1, source_target_pairs={{0,2},{1,3},{2,0},{3,1},{4,6},{5,7},{6,4},{7,5},{8,10},{9,11},{10,... | collective-permute-start | bytes 786440 | tf_op jit(solution)/shard_map/ppermute | solution.py:27
  27.7 2.7 %collective-permute-start.6 = (bf16[16,8192]{1,0:T(8,128)(2,1)S(1)}, bf16[16,8192]{1,0:T(8,128)(2,1)S(1)}, u32[]{:S(2)}, u32[]{:S(2)}) collective-permute-start(bf16[16,8192]{1,0:T(8,128)(2,1)S(1)} %shard_map.128.refs_7_), channel_id=1, source_target_pairs={{0,16},{1,17},{2,18},{3,19},{4,20},{5,21},{6,22},{7,23},{8,24},{9,... | collective-permute-start | bytes 786440 | tf_op jit(solution)/shard_map/ppermute | solution.py:27
  31.7 5.2 %shard_map.129.refs_14_.refs_10_ = bf16[16,512,128]{2,1,0:T(8,128)(2,1)} custom-call(bf16[64,512,128]{2,1,0:T(8,128)(2,1)} %pair.3, bf16[256,256]{1,0:T(8,128)(2,1)S(1)} %bitcast.15, bf16[256,256]{1,0:T(8,128)(2,1)S(1)} %get-tuple-element.76.weight, f32[1,256]{1,0:T(1,128)S(1)} %get-tuple-element.77.bias), custom_call_target="tpu_custom_call" | custom-call | flops 3200000000 | bytes 1048576 | tf_op jit(solution)/shard_map/pallas_call | solution.py:342
  37.1 2.1 %collective-permute-done.9.refs_12_ = bf16[16,8192]{1,0:T(8,128)(2,1)S(1)} collective-permute-done((bf16[16,8192]{1,0:T(8,128)(2,1)S(1)}, bf16[16,8192]{1,0:T(8,128)(2,1)S(1)}, u32[]{:S(2)}, u32[]{:S(2)}) %collective-permute-start.9) | collective-permute-done | bytes 262176 | tf_op jit(solution)/shard_map/ppermute | solution.py:27
  39.4 3.1 %collective-permute-start.15 = (bf16[32,8192]{1,0:T(8,128)(2,1)S(1)}, bf16[32,8192]{1,0:T(8,128)(2,1)S(1)}, u32[]{:S(2)}, u32[]{:S(2)}) collective-permute-start(bf16[32,8192]{1,0:T(8,128)(2,1)S(1)} %maximum_maximum_fusion), channel_id=1, source_target_pairs={{0,4},{1,5},{2,6},{3,7},{4,0},{5,1},{6,2},{7,3},{8,12},{9,13},{10,... | collective-permute-start | bytes 1572872 | tf_op jit(solution)/shard_map/ppermute | solution.py:27
  42.6 2.7 %collective-permute-start.11 = (bf16[64,4096]{1,0:T(8,128)(2,1)S(1)}, bf16[64,4096]{1,0:T(8,128)(2,1)S(1)}, u32[]{:S(2)}, u32[]{:S(2)}) collective-permute-start(bf16[64,4096]{1,0:T(8,128)(2,1)S(1)} %pad_maximum_fusion), channel_id=1, source_target_pairs={{0,96},{1,97},{2,98},{3,99},{4,100},{5,101},{6,102},{7,103},{8,104... | collective-permute-start | bytes 1572872 | tf_op jit(solution)/shard_map/ppermute | solution.py:27
  45.4 1.7 %collective-permute-start.13 = (bf16[64,4096]{1,0:T(8,128)(2,1)S(1)}, bf16[64,4096]{1,0:T(8,128)(2,1)S(1)}, u32[]{:S(2)}, u32[]{:S(2)}) collective-permute-start(bf16[64,4096]{1,0:T(8,128)(2,1)S(1)} %pad_maximum_fusion.1), channel_id=1, source_target_pairs={{0,24},{1,25},{2,26},{3,27},{4,28},{5,29},{6,30},{7,31},{8,0},{9,1... | collective-permute-start | bytes 1572872 | tf_op jit(solution)/shard_map/ppermute | solution.py:27
  47.9 9.8 %shard_map.130.refs_15_.refs_11_ = bf16[48,512,128]{2,1,0:T(8,128)(2,1)} custom-call(bf16[64,512,128]{2,1,0:T(8,128)(2,1)} %pair.3, bf16[256,256]{1,0:T(8,128)(2,1)S(1)} %bitcast.16, bf16[256,256]{1,0:T(8,128)(2,1)S(1)} %get-tuple-element.76.weight, f32[1,256]{1,0:T(1,128)S(1)} %get-tuple-element.77.bias), custom_call_target="tpu_custom_call" | custom-call | flops 9600000000 | bytes 1048576 | tf_op jit(solution)/shard_map/pallas_call | solution.py:342
  57.8 5.8 %shard_map.131 = (bf16[32,256,256]{2,1,0:T(8,128)(2,1)S(1)}, bf16[256,256]{1,0:T(8,128)(2,1)S(1)}, f32[32,8,128]{2,1,0:T(8,128)S(1)}, f32[32,8,128]{2,1,0:T(8,128)S(1)}) custom-call(s32[4]{0:T(128)S(1)} %pad_add_fusion.here.refs_0_, bf16[2,64,16,128]{3,2,1,0:T(8,128)(2,1)S(1)} %pad_maximum_fusion.2.left_0, ...), custom_call_target="tpu_custom_call" | custom-call | flops 4000000000 | bytes 12582912 | tf_op jit(solution)/shard_map/pallas_call | solution.py:317
  65.5 2.6 %collective-permute-start.18 = (bf16[64,4096]{1,0:T(8,128)(2,1)S(1)}, bf16[64,4096]{1,0:T(8,128)(2,1)S(1)}, u32[]{:S(2)}, u32[]{:S(2)}) collective-permute-start(bf16[64,4096]{1,0:T(8,128)(2,1)S(1)} %get-tuple-element.120), channel_id=1, source_target_pairs={{0,96},{1,97},{2,98},{3,99},{4,100},{5,101},{6,102},{7,103},{8,104... | collective-permute-start | bytes 1572872 | tf_op jit(solution)/shard_map/ppermute | solution.py:27
  68.3 3.2 %collective-permute-start.20 = (bf16[64,4096]{1,0:T(8,128)(2,1)S(1)}, bf16[64,4096]{1,0:T(8,128)(2,1)S(1)}, u32[]{:S(2)}, u32[]{:S(2)}) collective-permute-start(bf16[64,4096]{1,0:T(8,128)(2,1)S(1)} %get-tuple-element.118), channel_id=1, source_target_pairs={{0,24},{1,25},{2,26},{3,27},{4,28},{5,29},{6,30},{7,31},{8,0},{9,1... | collective-permute-start | bytes 1572872 | tf_op jit(solution)/shard_map/ppermute | solution.py:27
  71.6 3.5 %collective-permute-start.22 = (bf16[32,8192]{1,0:T(8,128)(2,1)S(1)}, bf16[32,8192]{1,0:T(8,128)(2,1)S(1)}, u32[]{:S(2)}, u32[]{:S(2)}) collective-permute-start(bf16[32,8192]{1,0:T(8,128)(2,1)S(1)} %maximum_maximum_fusion.1), channel_id=1, source_target_pairs={{0,4},{1,5},{2,6},{3,7},{4,0},{5,1},{6,2},{7,3},{8,12},{9,13},{10,... | collective-permute-start | bytes 1572872 | tf_op jit(solution)/shard_map/ppermute | solution.py:27
  75.1 8.9 %shard_map.132.refs_16_ = bf16[64,512,128]{2,1,0:T(8,128)(2,1)} custom-call(s32[4]{0:T(128)S(1)} %pad_add_fusion.here.refs_0_, bf16[64,4096]{1,0:T(8,128)(2,1)S(1)} %collective-permute-done.11.refs_1_, bf16[80,4096]{1,0:T(8,128)(2,1)S(1)} %collective-permute-done.12.refs_2_, bf16[64,4096]{1,0:T(8,128)(2,1)S(1)} %collective-permute-done.13.refs_3_, ...), custom_call_target="tpu_custom_call" | custom-call | flops 6400000000 | bytes 16777216 | tf_op jit(solution)/shard_map/pallas_call | solution.py:259
  85.1 3.3 %collective-permute-start.23 = (bf16[32,4096]{1,0:T(8,128)(2,1)S(1)}, bf16[32,4096]{1,0:T(8,128)(2,1)S(1)}, u32[]{:S(2)}, u32[]{:S(2)}) collective-permute-start(bf16[32,4096]{1,0:T(8,128)(2,1)S(1)} %pad_maximum_fusion.9), channel_id=1, source_target_pairs={{0,96},{1,97},{2,98},{3,99},{4,100},{5,101},{6,102},{7,103},{8,104... | collective-permute-start | bytes 786440 | tf_op jit(solution)/shard_map/ppermute | solution.py:27
  88.4 3.5 %collective-permute-start.25 = (bf16[32,4096]{1,0:T(8,128)(2,1)S(1)}, bf16[32,4096]{1,0:T(8,128)(2,1)S(1)}, u32[]{:S(2)}, u32[]{:S(2)}) collective-permute-start(bf16[32,4096]{1,0:T(8,128)(2,1)S(1)} %pad_maximum_fusion.10), channel_id=1, source_target_pairs={{0,24},{1,25},{2,26},{3,27},{4,28},{5,29},{6,30},{7,31},{8,0},{9,1... | collective-permute-start | bytes 786440 | tf_op jit(solution)/shard_map/ppermute | solution.py:27
  91.9 5.7 %shard_map.133.refs_16_ = bf16[64,512,128]{2,1,0:T(8,128)(2,1)} custom-call(s32[4]{0:T(128)S(1)} %pad_add_fusion.here.refs_0_, bf16[64,4096]{1,0:T(8,128)(2,1)S(1)} %collective-permute-done.11.refs_1_, bf16[80,4096]{1,0:T(8,128)(2,1)S(1)} %collective-permute-done.12.refs_2_, ...), custom_call_target="tpu_custom_call", output_to_operand_aliasing={{}: (16, {})} | custom-call | flops 3200000000 | bytes 8388608 | tf_op jit(solution)/shard_map/pallas_call | solution.py:259
  97.7 5.6 %shard_map.134 = bf16[64,512,128]{2,1,0:T(8,128)(2,1)} custom-call(s32[4]{0:T(128)S(1)} %pad_add_fusion.here.refs_0_, bf16[64,4096]{1,0:T(8,128)(2,1)S(1)} %collective-permute-done.19.refs_6_.refs_1_, bf16[64,4096]{1,0:T(8,128)(2,1)S(1)} %collective-permute-done.20.refs_7_.refs_2_, ...), custom_call_target="tpu_custom_call", output_to_operand_aliasing={{}: (16, {})} | custom-call | flops 3200000000 | bytes 8388608 | tf_op jit(solution)/shard_map/pallas_call | solution.py:259
  (96 shorter events, 13.0 us)
Async XLA Ops:
  1.0 11.8 %collective-permute-start = (bf16[16,16,128]{2,1,0:T(8,128)(2,1)S(1)}, bf16[16,16,128]{2,1,0:T(8,128)(2,1)S(1)}, u32[]{:S(2)}, u32[]{:S(2)}) collective-permute-start(bf16[16,16,128]{2,1,0:T(8,128)(2,1)S(1)} %get-tuple-element.57), channel_id=1, source_target_pairs={{0,0},{1,32},{2,64},{3,96},{4,4},{5,36},{6,68},{7,100},{8,8},{9,40... | collective-permute-start | bytes 196616 | tf_op jit(solution)/shard_map/ppermute | solution.py:413
  1.7 11.2 %collective-permute-start.1 = (bf16[16,16,128]{2,1,0:T(8,128)(2,1)S(1)}, bf16[16,16,128]{2,1,0:T(8,128)(2,1)S(1)}, u32[]{:S(2)}, u32[]{:S(2)}) collective-permute-start(bf16[16,16,128]{2,1,0:T(8,128)(2,1)S(1)} %get-tuple-element.58), channel_id=1, source_target_pairs={{0,32},{1,64},{2,96},{3,0},{4,36},{5,68},{6,100},{7,4},{8,40},{9,7... | collective-permute-start | bytes 196616 | tf_op jit(solution)/shard_map/ppermute | solution.py:413
  16.0 10.1 %collective-permute-start.7 = (bf16[16,8192]{1,0:T(8,128)(2,1)S(1)}, bf16[16,8192]{1,0:T(8,128)(2,1)S(1)}, u32[]{:S(2)}, u32[]{:S(2)}) collective-permute-start(bf16[16,8192]{1,0:T(8,128)(2,1)S(1)} %shard_map.128.refs_7_), channel_id=1, source_target_pairs={{0,8},{1,9},{2,10},{3,11},{4,12},{5,13},{6,14},{7,15},{8,16},{9,17... | collective-permute-start | bytes 786440 | tf_op jit(solution)/shard_map/ppermute | solution.py:27
  17.6 10.1 %collective-permute-start.5 = (bf16[16,8192]{1,0:T(8,128)(2,1)S(1)}, bf16[16,8192]{1,0:T(8,128)(2,1)S(1)}, u32[]{:S(2)}, u32[]{:S(2)}) collective-permute-start(bf16[16,8192]{1,0:T(8,128)(2,1)S(1)} %shard_map.128.refs_7_), channel_id=1, source_target_pairs={{0,4},{1,5},{2,6},{3,7},{4,0},{5,1},{6,2},{7,3},{8,12},{9,13},{10,... | collective-permute-start | bytes 786440 | tf_op jit(solution)/shard_map/ppermute | solution.py:27
  20.4 10.0 %collective-permute-start.4 = (bf16[16,8192]{1,0:T(8,128)(2,1)S(1)}, bf16[16,8192]{1,0:T(8,128)(2,1)S(1)}, u32[]{:S(2)}, u32[]{:S(2)}) collective-permute-start(bf16[16,8192]{1,0:T(8,128)(2,1)S(1)} %shard_map.128.refs_7_), channel_id=1, source_target_pairs={{0,24},{1,25},{2,26},{3,27},{4,28},{5,29},{6,30},{7,31},{8,0},{9,1... | collective-permute-start | bytes 786440 | tf_op jit(solution)/shard_map/ppermute | solution.py:27
  22.3 14.8 %collective-permute-start.10 = (bf16[16,8192]{1,0:T(8,128)(2,1)S(1)}, bf16[16,8192]{1,0:T(8,128)(2,1)S(1)}, u32[]{:S(2)}, u32[]{:S(2)}) collective-permute-start(bf16[16,8192]{1,0:T(8,128)(2,1)S(1)} %shard_map.128.refs_7_), channel_id=1, source_target_pairs={{0,32},{1,33},{2,34},{3,35},{4,36},{5,37},{6,38},{7,39},{8,40},{9,... | collective-permute-start | bytes 786440 | tf_op jit(solution)/shard_map/ppermute | solution.py:27
  24.7 12.4 %collective-permute-start.8 = (bf16[16,8192]{1,0:T(8,128)(2,1)S(1)}, bf16[16,8192]{1,0:T(8,128)(2,1)S(1)}, u32[]{:S(2)}, u32[]{:S(2)}) collective-permute-start(bf16[16,8192]{1,0:T(8,128)(2,1)S(1)} %shard_map.128.refs_7_), channel_id=1, source_target_pairs={{0,96},{1,97},{2,98},{3,99},{4,100},{5,101},{6,102},{7,103},{8,104... | collective-permute-start | bytes 786440 | tf_op jit(solution)/shard_map/ppermute | solution.py:27
  26.1 10.8 %collective-permute-start.16 = (bf16[64,16,128]{2,1,0:T(8,128)(2,1)}, bf16[64,16,128]{2,1,0:T(8,128)(2,1)S(1)}, u32[]{:S(2)}, u32[]{:S(2)}) collective-permute-start(bf16[64,16,128]{2,1,0:T(8,128)(2,1)} %param.14), channel_id=1, source_target_pairs={{0,2},{1,3},{2,0},{3,1},{4,6},{5,7},{6,4},{7,5},{8,10},{9,11},{10,... | collective-permute-start | bytes 786440 | tf_op jit(solution)/shard_map/ppermute | solution.py:27
  27.7 9.4 %collective-permute-start.6 = (bf16[16,8192]{1,0:T(8,128)(2,1)S(1)}, bf16[16,8192]{1,0:T(8,128)(2,1)S(1)}, u32[]{:S(2)}, u32[]{:S(2)}) collective-permute-start(bf16[16,8192]{1,0:T(8,128)(2,1)S(1)} %shard_map.128.refs_7_), channel_id=1, source_target_pairs={{0,16},{1,17},{2,18},{3,19},{4,20},{5,21},{6,22},{7,23},{8,24},{9,... | collective-permute-start | bytes 786440 | tf_op jit(solution)/shard_map/ppermute | solution.py:27
  37.0 10.2 %collective-permute-start.17 = (bf16[2,64,16,128]{3,2,1,0:T(8,128)(2,1)S(1)}, bf16[2,64,16,128]{3,2,1,0:T(8,128)(2,1)S(1)}, u32[]{:S(2)}, u32[]{:S(2)}) collective-permute-start(bf16[2,64,16,128]{3,2,1,0:T(8,128)(2,1)S(1)} %pad_maximum_fusion.2.left_0), channel_id=1, source_target_pairs={{0,1},{1,0},{2,3},{3,2},{4,5},{5,4},{6,7},{7,6},{8,9},{9,8},{10,11... | collective-permute-start | bytes 1572872 | tf_op jit(solution)/shard_map/ppermute | solution.py:27
  39.4 24.2 %collective-permute-start.15 = (bf16[32,8192]{1,0:T(8,128)(2,1)S(1)}, bf16[32,8192]{1,0:T(8,128)(2,1)S(1)}, u32[]{:S(2)}, u32[]{:S(2)}) collective-permute-start(bf16[32,8192]{1,0:T(8,128)(2,1)S(1)} %maximum_maximum_fusion), channel_id=1, source_target_pairs={{0,4},{1,5},{2,6},{3,7},{4,0},{5,1},{6,2},{7,3},{8,12},{9,13},{10,... | collective-permute-start | bytes 1572872 | tf_op jit(solution)/shard_map/ppermute | solution.py:27
  42.6 21.0 %collective-permute-start.11 = (bf16[64,4096]{1,0:T(8,128)(2,1)S(1)}, bf16[64,4096]{1,0:T(8,128)(2,1)S(1)}, u32[]{:S(2)}, u32[]{:S(2)}) collective-permute-start(bf16[64,4096]{1,0:T(8,128)(2,1)S(1)} %pad_maximum_fusion), channel_id=1, source_target_pairs={{0,96},{1,97},{2,98},{3,99},{4,100},{5,101},{6,102},{7,103},{8,104... | collective-permute-start | bytes 1572872 | tf_op jit(solution)/shard_map/ppermute | solution.py:27
  45.4 18.2 %collective-permute-start.13 = (bf16[64,4096]{1,0:T(8,128)(2,1)S(1)}, bf16[64,4096]{1,0:T(8,128)(2,1)S(1)}, u32[]{:S(2)}, u32[]{:S(2)}) collective-permute-start(bf16[64,4096]{1,0:T(8,128)(2,1)S(1)} %pad_maximum_fusion.1), channel_id=1, source_target_pairs={{0,24},{1,25},{2,26},{3,27},{4,28},{5,29},{6,30},{7,31},{8,0},{9,1... | collective-permute-start | bytes 1572872 | tf_op jit(solution)/shard_map/ppermute | solution.py:27
  47.1 17.0 %collective-permute-start.12 = (bf16[80,4096]{1,0:T(8,128)(2,1)S(1)}, bf16[80,4096]{1,0:T(8,128)(2,1)S(1)}, u32[]{:S(2)}, u32[]{:S(2)}) collective-permute-start(bf16[80,4096]{1,0:T(8,128)(2,1)S(1)} %constant_dynamic-update-slice_fusion), channel_id=1, source_target_pairs={{0,32},{1,33},{2,34},{3,35},{4,36},{5,37},{6,38},{7,39},{8,40},{9,... | collective-permute-start | bytes 1966088 | tf_op jit(solution)/shard_map/ppermute | solution.py:27
  47.3 17.2 %collective-permute-start.14 = (bf16[80,4096]{1,0:T(8,128)(2,1)S(1)}, bf16[80,4096]{1,0:T(8,128)(2,1)S(1)}, u32[]{:S(2)}, u32[]{:S(2)}) collective-permute-start(bf16[80,4096]{1,0:T(8,128)(2,1)S(1)} %get-tuple-element.121), channel_id=1, source_target_pairs={{0,8},{1,9},{2,10},{3,11},{4,12},{5,13},{6,14},{7,15},{8,16},{9,17... | collective-permute-start | bytes 1966088 | tf_op jit(solution)/shard_map/ppermute | solution.py:27
  64.8 19.2 %collective-permute-start.19 = (bf16[64,4096]{1,0:T(8,128)(2,1)S(1)}, bf16[64,4096]{1,0:T(8,128)(2,1)S(1)}, u32[]{:S(2)}, u32[]{:S(2)}) collective-permute-start(bf16[64,4096]{1,0:T(8,128)(2,1)S(1)} %get-tuple-element.119), channel_id=1, source_target_pairs={{0,32},{1,33},{2,34},{3,35},{4,36},{5,37},{6,38},{7,39},{8,40},{9,... | collective-permute-start | bytes 1572872 | tf_op jit(solution)/shard_map/ppermute | solution.py:27
  65.5 18.5 %collective-permute-start.18 = (bf16[64,4096]{1,0:T(8,128)(2,1)S(1)}, bf16[64,4096]{1,0:T(8,128)(2,1)S(1)}, u32[]{:S(2)}, u32[]{:S(2)}) collective-permute-start(bf16[64,4096]{1,0:T(8,128)(2,1)S(1)} %get-tuple-element.120), channel_id=1, source_target_pairs={{0,96},{1,97},{2,98},{3,99},{4,100},{5,101},{6,102},{7,103},{8,104... | collective-permute-start | bytes 1572872 | tf_op jit(solution)/shard_map/ppermute | solution.py:27
  68.2 15.8 %collective-permute-start.21 = (bf16[64,4096]{1,0:T(8,128)(2,1)S(1)}, bf16[64,4096]{1,0:T(8,128)(2,1)S(1)}, u32[]{:S(2)}, u32[]{:S(2)}) collective-permute-start(bf16[64,4096]{1,0:T(8,128)(2,1)S(1)} %get-tuple-element.117), channel_id=1, source_target_pairs={{0,8},{1,9},{2,10},{3,11},{4,12},{5,13},{6,14},{7,15},{8,16},{9,17... | collective-permute-start | bytes 1572872 | tf_op jit(solution)/shard_map/ppermute | solution.py:27
  68.3 15.7 %collective-permute-start.20 = (bf16[64,4096]{1,0:T(8,128)(2,1)S(1)}, bf16[64,4096]{1,0:T(8,128)(2,1)S(1)}, u32[]{:S(2)}, u32[]{:S(2)}) collective-permute-start(bf16[64,4096]{1,0:T(8,128)(2,1)S(1)} %get-tuple-element.118), channel_id=1, source_target_pairs={{0,24},{1,25},{2,26},{3,27},{4,28},{5,29},{6,30},{7,31},{8,0},{9,1... | collective-permute-start | bytes 1572872 | tf_op jit(solution)/shard_map/ppermute | solution.py:27
  71.6 13.2 %collective-permute-start.22 = (bf16[32,8192]{1,0:T(8,128)(2,1)S(1)}, bf16[32,8192]{1,0:T(8,128)(2,1)S(1)}, u32[]{:S(2)}, u32[]{:S(2)}) collective-permute-start(bf16[32,8192]{1,0:T(8,128)(2,1)S(1)} %maximum_maximum_fusion.1), channel_id=1, source_target_pairs={{0,4},{1,5},{2,6},{3,7},{4,0},{5,1},{6,2},{7,3},{8,12},{9,13},{10,... | collective-permute-start | bytes 1572872 | tf_op jit(solution)/shard_map/ppermute | solution.py:27
  84.9 12.7 %collective-permute-start.26 = (bf16[16,4096]{1,0:T(8,128)(2,1)S(1)}, bf16[16,4096]{1,0:T(8,128)(2,1)S(1)}, u32[]{:S(2)}, u32[]{:S(2)}) collective-permute-start(bf16[16,4096]{1,0:T(8,128)(2,1)S(1)} %slice.103), channel_id=1, source_target_pairs={{0,8},{1,9},{2,10},{3,11},{4,12},{5,13},{6,14},{7,15},{8,16},{9,17... | collective-permute-start | bytes 393224 | tf_op jit(solution)/shard_map/ppermute | solution.py:27
  85.0 12.7 %collective-permute-start.24 = (bf16[16,4096]{1,0:T(8,128)(2,1)S(1)}, bf16[16,4096]{1,0:T(8,128)(2,1)S(1)}, u32[]{:S(2)}, u32[]{:S(2)}) collective-permute-start(bf16[16,4096]{1,0:T(8,128)(2,1)S(1)} %slice.100), channel_id=1, source_target_pairs={{0,32},{1,33},{2,34},{3,35},{4,36},{5,37},{6,38},{7,39},{8,40},{9,... | collective-permute-start | bytes 393224 | tf_op jit(solution)/shard_map/ppermute | solution.py:27
  85.1 12.5 %collective-permute-start.23 = (bf16[32,4096]{1,0:T(8,128)(2,1)S(1)}, bf16[32,4096]{1,0:T(8,128)(2,1)S(1)}, u32[]{:S(2)}, u32[]{:S(2)}) collective-permute-start(bf16[32,4096]{1,0:T(8,128)(2,1)S(1)} %pad_maximum_fusion.9), channel_id=1, source_target_pairs={{0,96},{1,97},{2,98},{3,99},{4,100},{5,101},{6,102},{7,103},{8,104... | collective-permute-start | bytes 786440 | tf_op jit(solution)/shard_map/ppermute | solution.py:27
  88.4 9.2 %collective-permute-start.25 = (bf16[32,4096]{1,0:T(8,128)(2,1)S(1)}, bf16[32,4096]{1,0:T(8,128)(2,1)S(1)}, u32[]{:S(2)}, u32[]{:S(2)}) collective-permute-start(bf16[32,4096]{1,0:T(8,128)(2,1)S(1)} %pad_maximum_fusion.10), channel_id=1, source_target_pairs={{0,24},{1,25},{2,26},{3,27},{4,28},{5,29},{6,30},{7,31},{8,0},{9,1... | collective-permute-start | bytes 786440 | tf_op jit(solution)/shard_map/ppermute | solution.py:27
  (13 other events, 175.0 us)

commit v4 on v3

--- a/solution.py
+++ b/solution.py
@@ -101,7 +101,7 @@
 
 def left_kernel(
     here, left_0, left_1, average, gain, bias, weight, spread, order, w_out, out_gain, out_bias,
-    out, wide_out, wide_gain, wide_bias, normed, swap, rows,
+    out, wide_out, shift, normed, swap, rows,
 ):
     for quarter in range(4):
         at = slice(quarter * 16, quarter * 16 + 16)
@@ -127,16 +127,16 @@
         return carry
 
     lax.fori_loop(0, 32, body, 0, unroll=32)
-    made = jnp.dot(order[...], w_out[...].astype(F32), preferred_element_type=F32)
+    weight_out = w_out[...].astype(F32)
+    scaled = jnp.broadcast_to(out_gain[...], (128, 128)).T * weight_out
+    made = jnp.dot(order[...], scaled.astype(BF16), preferred_element_type=F32)
     second = lax.rem(lax.broadcasted_iota(jnp.int32, (256, 128), 0), 8) // 4
     wide_out[:, :128] = jnp.where(second == 0, made, 0.0).astype(BF16)
     wide_out[:, 128:] = jnp.where(second == 1, made, 0.0).astype(BF16)
-    for source, target in ((out_gain, wide_gain), (out_bias, wide_bias)):
-        columns = jnp.broadcast_to(source[...], (128, 128)).T
-        made = jnp.dot(
-            order[...], columns, preferred_element_type=F32, precision=lax.Precision.HIGHEST
-        )
-        target[...] = made.reshape(32, 8, 128)
+    rows_bias = jnp.broadcast_to(out_bias[...], (8, 128))
+    made = jnp.dot(rows_bias, weight_out, preferred_element_type=F32, precision=lax.Precision.HIGHEST)[:1]
+    shift[:, :128] = made
+    shift[:, 128:] = made
 
 
 def gate_block(average, weight, bias, pair, out):
@@ -163,8 +163,8 @@
 def update_kernel(blocks, n_src, has_out, *refs):
     here = refs[0]
     sources = refs[1 : 1 + n_src]
-    gate_0, gate_1, lbd, wide_out, gain, bias = refs[1 + n_src : 7 + n_src]
-    refs = refs[7 + n_src + has_out :]
+    gate_0, gate_1, lbd, wide_out, shift = refs[1 + n_src : 6 + n_src]
+    refs = refs[6 + n_src + has_out :]
     out, product, gates, results, gate_sem, out_sem = refs
     z, y, x = here[0], here[1], here[2]
     columns = 16 * len(blocks)
@@ -227,11 +227,12 @@
             mean = over_four(jnp.sum(values, axis=0)) * (1.0 / 128)
             centered = values - mean[None]
             var = over_four(jnp.sum(centered * centered, axis=0)) * (1.0 / 128)
-            normed = centered * lax.rsqrt(var + 1e-05)[None] * gain[...] + bias[...]
+            normed = centered * lax.rsqrt(var + 1e-05)[None]
             normed = normed.reshape(256, 128).astype(BF16)
             both = lax.dot_general(
                 normed, wide_out[...], (((0,), (0,)), ((), ())), preferred_element_type=F32
             )
+            both = both + shift[...]
             for i2 in range(2):
                 row = 2 * ip + i2
                 gate = gates[row, lanes].astype(F32)
@@ -252,14 +253,14 @@
 HBM = pl.BlockSpec(memory_space=pltpu.HBM)
 
 
-def run_update(blocks, here, sources, gates, lbd, wide_out, gain, bias, before):
+def run_update(blocks, here, sources, gates, lbd, wide_out, shift, before):
     n = len(blocks)
     has_out = before is not None
-    args = [here, *sources, *gates, lbd, wide_out, gain, bias] + ([before] if has_out else [])
+    args = [here, *sources, *gates, lbd, wide_out, shift] + ([before] if has_out else [])
     return pl.pallas_call(
         functools.partial(update_kernel, blocks, len(sources), has_out),
         out_shape=pltpu.HBM((64, 512, 128), BF16),
-        in_specs=[SMEM] + [VMEM] * len(sources) + [HBM] * 2 + [VMEM] * 4 + [HBM] * has_out,
+        in_specs=[SMEM] + [VMEM] * len(sources) + [HBM] * 2 + [VMEM] * 3 + [HBM] * has_out,
         out_specs=HBM,
         scratch_shapes=[
             pltpu.VMEM((32, 32, 8, n * 16), F32),
@@ -319,11 +320,10 @@
         out_shape=[
             jax.ShapeDtypeStruct((32, 256, 256), BF16),
             jax.ShapeDtypeStruct((256, 256), BF16),
-            jax.ShapeDtypeStruct((32, 8, 128), F32),
-            jax.ShapeDtypeStruct((32, 8, 128), F32),
+            jax.ShapeDtypeStruct((1, 256), F32),
         ],
         in_specs=[SMEM] + [VMEM] * 11,
-        out_specs=[VMEM] * 4,
+        out_specs=[VMEM] * 3,
         scratch_shapes=[
             pltpu.VMEM((4, 16, 64, 128), BF16),
             pltpu.VMEM((4, 64, 16, 128), F32),
@@ -332,7 +332,7 @@
         compiler_params=pltpu.CompilerParams(vmem_limit_bytes=20 * MIB),
         cost_estimate=pl.CostEstimate(flops=4 * 10**9, bytes_accessed=12 * MIB, transcendentals=0),
     )(
-        here, left_0, left_1, jnp.full((128, 128), 1 / 128, BF16), gain, bias, weight, jnp.asarray(spread, BF16), jnp.asarray(order.reshape(256, 128)),
+        here, left_0, left_1, jnp.full((128, 128), 1 / 128, BF16), gain, bias, weight, jnp.asarray(spread, BF16), jnp.asarray(order.reshape(256, 128), BF16),
         w_out, out_gain.reshape(1, 128), out_bias.reshape(1, 128),
     )
 
@@ -368,7 +368,7 @@
         return f"P{first}{far}", 0 if near == 1 else 16
     if near == 0:
         return f"P{first}3", 48
-    return (f"Q{first}1", (near - 1) * 16) if near < 3 else (f"Q{first}3", 0)
+    return (f"Q{first}1", (near - 1) * 16) if near < 3 else ("X4", 0)
 
 
 def place_a(z, y, x):
@@ -431,7 +431,7 @@
             places = [p(*d) for p in (place_a, place_b)]
             found.append((d, [(names.index(name), row, lane) for name, row, lane in places]))
         sources = [got[n] for n in names]
-        return run_update(found, here, sources, gates, lbd, wide_out, gain_out, bias_out, before)
+        return run_update(found, here, sources, gates, lbd, wide_out, shift_out, before)
 
     def halves(a, b):
         return jnp.concatenate([a, b], 1)
@@ -458,7 +458,7 @@
     left_0 = jnp.stack([left_panel, left_2])
     left_1 = move(left_0, dc=1)
     gate_1 = run_gate(GATE_FIRST, 64 - GATE_FIRST, pair_block, *wide_gate)
-    lbd, wide_out, gain_out, bias_out = run_left(
+    lbd, wide_out, shift_out = run_left(
         here, left_0, left_1, gain, bias, w_left, w_out, out_gain, out_bias
     )
     gate_1, lbd = together("A1", "A3", "B1", "B3", "X2", more=[gate_1, lbd])
@@ -471,10 +471,11 @@
     out = call(EARLY, None)
     (out,) = together("PA1", "PA3", "PB1", "PB3", "X3", more=[out])
     x3 = got["X3"]
-    got["QA1"], got["QA3"] = move(cat(got["PA1"][:16], x3[:16, :4096]), dz=-1), move(got["PA3"][16:32], dz=1)
-    got["QB1"], got["QB3"] = move(cat(got["PB1"][:16], x3[:16, 4096:]), dy=-1), move(got["PB3"][16:32], dy=1)
+    got["QA1"] = move(cat(got["PA1"][:16], x3[:16, :4096]), dz=-1)
+    got["QB1"] = move(cat(got["PB1"][:16], x3[:16, 4096:]), dy=-1)
+    got["X4"] = move(halves(got["PA3"][32:48], got["PB3"][32:48]), dx=1)
     out = call(OTHERS[:8], out)
-    (out,) = together("QA1", "QA3", "QB1", "QB3", more=[out])
+    (out,) = together("QA1", "QB1", "X4", more=[out])
     return call(LATE + OTHERS[8:], out)
 
 

time: 104 us -> 102 us (0.981)
  Pallas kernels: 43.7 us -> 42.3 us
    pallas_call x3, Pallas kernels: 20.3 us -> 19 us  [run_update(): pl.pallas_call(functools.partial(update_kernel, blocks, len(sources), has...]
    ppermute x23 -> x22, starting transfers between devices: 40.9 us -> 40.1 us  [move(): return lax.ppermute(value, AXES, pairs)]
    ppermute x23 -> x22, waiting for transfers between devices: 3.8 us -> 4.53 us  [move(): return lax.ppermute(value, AXES, pairs)]
  transfers between devices with their start and end apart: 27 -> 26, of which waited for: 6 -> 6; matrix products, arithmetic and copies ran while one was open for 1% -> 1% of each run, Pallas kernels for 35% -> 35%
where the time goes in v4:
time: 102 us
  starting transfers between devices  50.8 us (50%)
  Pallas kernels  42.3 us (41%)
  waiting for transfers between devices  6.07 us (6%)
  local copies, waits for them, and re-layouts  1.6 us (2%)
    ppermute x22, starting transfers between devices, move(): return lax.ppermute(value, AXES, pairs)  40.1 us
    pallas_call x3, Pallas kernels, run_update(): pl.pallas_call(functools.partial(update_kernel, blocks, len(sources), has...  19 us
    pallas_call x2, Pallas kernels, run_gate(): pl.pallas_call(functools.partial(gate_kernel, first // 16), out_shape=plt...  15 us
    ppermute x4, starting transfers between devices, per_device(): pieces.append(lax.ppermute(parts[s], AXES, pairs))  10.7 us
    pallas_call x1, Pallas kernels, run_left(): pl.pallas_call(left_kernel, out_shape=[jax.ShapeDtypeStruct((32, 256, 256...  5.58 us
    ppermute x22, waiting for transfers between devices, move(): return lax.ppermute(value, AXES, pairs)  4.53 us
  transfers between devices with their start and end apart: 26, of which 6 were waited for; matrix products, arithmetic and copies ran while one was open for 1% of the time, Pallas kernels for 35%

profile of v4, /device:TPU:0, one launch (start us, length us, event | category | flops | bytes accessed | tf_op | source)
XLA Modules:
  0.0 102.0 jit_solution(16985004025818164823)
XLA Ops:
  1.7 3.3 %collective-permute-start.1 = (bf16[16,16,128]{2,1,0:T(8,128)(2,1)S(1)}, bf16[16,16,128]{2,1,0:T(8,128)(2,1)S(1)}, u32[]{:S(2)}, u32[]{:S(2)}) collective-permute-start(bf16[16,16,128]{2,1,0:T(8,128)(2,1)S(1)} %get-tuple-element.56), channel_id=1, source_target_pairs={{0,32},{1,64},{2,96},{3,0},{4,36},{5,68},{6,100},{7,4},{8,40},{9,7... | collective-permute-start | bytes 196616 | tf_op jit(solution)/shard_map/ppermute | solution.py:413
  5.0 4.3 %collective-permute-start.2 = (bf16[16,16,128]{2,1,0:T(8,128)(2,1)S(1)}, bf16[16,16,128]{2,1,0:T(8,128)(2,1)S(1)}, u32[]{:S(2)}, u32[]{:S(2)}) collective-permute-start(bf16[16,16,128]{2,1,0:T(8,128)(2,1)S(1)} %get-tuple-element.57), channel_id=1, source_target_pairs={{0,64},{1,96},{2,0},{3,32},{4,68},{5,100},{6,4},{7,36},{8,72},{9,1... | collective-permute-start | bytes 196616 | tf_op jit(solution)/shard_map/ppermute | solution.py:413
  9.3 2.3 %collective-permute-start.3 = (bf16[16,16,128]{2,1,0:T(8,128)(2,1)S(1)}, bf16[16,16,128]{2,1,0:T(8,128)(2,1)S(1)}, u32[]{:S(2)}, u32[]{:S(2)}) collective-permute-start(bf16[16,16,128]{2,1,0:T(8,128)(2,1)S(1)} %get-tuple-element.58), channel_id=1, source_target_pairs={{0,96},{1,0},{2,32},{3,64},{4,100},{5,4},{6,36},{7,68},{8,104},{9,... | collective-permute-start | bytes 196616 | tf_op jit(solution)/shard_map/ppermute | solution.py:413
  14.4 1.6 %shard_map.128.refs_7_ = bf16[16,8192]{1,0:T(8,128)(2,1)S(1)} custom-call(s32[4]{0:T(128)S(1)} %pad_add_fusion.here.refs_0_, bf16[16,16,128]{2,1,0:T(8,128)(2,1)S(1)} %collective-permute-done.p0, bf16[16,16,128]{2,1,0:T(8,128)(2,1)S(1)} %collective-permute-done.1.p1, bf16[16,16,128]{2,1,0:T(8,128)(2,1)S(1)} %collective-permute-done.2.p2, ...), custom_call_target="tpu_custom_call" | custom-call | tf_op jit(solution)/shard_map/pallas_call | solution.py:302
  16.0 1.6 %collective-permute-start.7 = (bf16[16,8192]{1,0:T(8,128)(2,1)S(1)}, bf16[16,8192]{1,0:T(8,128)(2,1)S(1)}, u32[]{:S(2)}, u32[]{:S(2)}) collective-permute-start(bf16[16,8192]{1,0:T(8,128)(2,1)S(1)} %shard_map.128.refs_7_), channel_id=1, source_target_pairs={{0,8},{1,9},{2,10},{3,11},{4,12},{5,13},{6,14},{7,15},{8,16},{9,17... | collective-permute-start | bytes 786440 | tf_op jit(solution)/shard_map/ppermute | solution.py:27
  17.6 2.8 %collective-permute-start.5 = (bf16[16,8192]{1,0:T(8,128)(2,1)S(1)}, bf16[16,8192]{1,0:T(8,128)(2,1)S(1)}, u32[]{:S(2)}, u32[]{:S(2)}) collective-permute-start(bf16[16,8192]{1,0:T(8,128)(2,1)S(1)} %shard_map.128.refs_7_), channel_id=1, source_target_pairs={{0,4},{1,5},{2,6},{3,7},{4,0},{5,1},{6,2},{7,3},{8,12},{9,13},{10,... | collective-permute-start | bytes 786440 | tf_op jit(solution)/shard_map/ppermute | solution.py:27
  20.4 1.7 %collective-permute-start.4 = (bf16[16,8192]{1,0:T(8,128)(2,1)S(1)}, bf16[16,8192]{1,0:T(8,128)(2,1)S(1)}, u32[]{:S(2)}, u32[]{:S(2)}) collective-permute-start(bf16[16,8192]{1,0:T(8,128)(2,1)S(1)} %shard_map.128.refs_7_), channel_id=1, source_target_pairs={{0,24},{1,25},{2,26},{3,27},{4,28},{5,29},{6,30},{7,31},{8,0},{9,1... | collective-permute-start | bytes 786440 | tf_op jit(solution)/shard_map/ppermute | solution.py:27
  22.3 2.4 %collective-permute-start.10 = (bf16[16,8192]{1,0:T(8,128)(2,1)S(1)}, bf16[16,8192]{1,0:T(8,128)(2,1)S(1)}, u32[]{:S(2)}, u32[]{:S(2)}) collective-permute-start(bf16[16,8192]{1,0:T(8,128)(2,1)S(1)} %shard_map.128.refs_7_), channel_id=1, source_target_pairs={{0,32},{1,33},{2,34},{3,35},{4,36},{5,37},{6,38},{7,39},{8,40},{9,... | collective-permute-start | bytes 786440 | tf_op jit(solution)/shard_map/ppermute | solution.py:27
  26.1 1.6 %collective-permute-start.16 = (bf16[64,16,128]{2,1,0:T(8,128)(2,1)}, bf16[64,16,128]{2,1,0:T(8,128)(2,1)S(1)}, u32[]{:S(2)}, u32[]{:S(2)}) collective-permute-start(bf16[64,16,128]{2,1,0:T(8,128)(2,1)} %param.14), channel_id=1, source_target_pairs={{0,2},{1,3},{2,0},{3,1},{4,6},{5,7},{6,4},{7,5},{8,10},{9,11},{10,... | collective-permute-start | bytes 786440 | tf_op jit(solution)/shard_map/ppermute | solution.py:27
  27.7 2.7 %collective-permute-start.6 = (bf16[16,8192]{1,0:T(8,128)(2,1)S(1)}, bf16[16,8192]{1,0:T(8,128)(2,1)S(1)}, u32[]{:S(2)}, u32[]{:S(2)}) collective-permute-start(bf16[16,8192]{1,0:T(8,128)(2,1)S(1)} %shard_map.128.refs_7_), channel_id=1, source_target_pairs={{0,16},{1,17},{2,18},{3,19},{4,20},{5,21},{6,22},{7,23},{8,24},{9,... | collective-permute-start | bytes 786440 | tf_op jit(solution)/shard_map/ppermute | solution.py:27
  31.7 5.2 %shard_map.129.refs_14_.refs_10_.refs_9_ = bf16[16,512,128]{2,1,0:T(8,128)(2,1)} custom-call(bf16[64,512,128]{2,1,0:T(8,128)(2,1)} %pair.3, bf16[256,256]{1,0:T(8,128)(2,1)S(1)} %bitcast.15, bf16[256,256]{1,0:T(8,128)(2,1)S(1)} %get-tuple-element.74.weight, f32[1,256]{1,0:T(1,128)S(1)} %get-tuple-element.75.bias), custom_call_target="tpu_custom_call" | custom-call | flops 3200000000 | bytes 1048576 | tf_op jit(solution)/shard_map/pallas_call | solution.py:342
  37.1 2.1 %collective-permute-done.9.refs_12_ = bf16[16,8192]{1,0:T(8,128)(2,1)S(1)} collective-permute-done((bf16[16,8192]{1,0:T(8,128)(2,1)S(1)}, bf16[16,8192]{1,0:T(8,128)(2,1)S(1)}, u32[]{:S(2)}, u32[]{:S(2)}) %collective-permute-start.9) | collective-permute-done | bytes 262176 | tf_op jit(solution)/shard_map/ppermute | solution.py:27
  39.4 3.1 %collective-permute-start.15 = (bf16[32,8192]{1,0:T(8,128)(2,1)S(1)}, bf16[32,8192]{1,0:T(8,128)(2,1)S(1)}, u32[]{:S(2)}, u32[]{:S(2)}) collective-permute-start(bf16[32,8192]{1,0:T(8,128)(2,1)S(1)} %maximum_maximum_fusion), channel_id=1, source_target_pairs={{0,4},{1,5},{2,6},{3,7},{4,0},{5,1},{6,2},{7,3},{8,12},{9,13},{10,... | collective-permute-start | bytes 1572872 | tf_op jit(solution)/shard_map/ppermute | solution.py:27
  42.6 2.7 %collective-permute-start.11 = (bf16[64,4096]{1,0:T(8,128)(2,1)S(1)}, bf16[64,4096]{1,0:T(8,128)(2,1)S(1)}, u32[]{:S(2)}, u32[]{:S(2)}) collective-permute-start(bf16[64,4096]{1,0:T(8,128)(2,1)S(1)} %pad_maximum_fusion), channel_id=1, source_target_pairs={{0,96},{1,97},{2,98},{3,99},{4,100},{5,101},{6,102},{7,103},{8,104... | collective-permute-start | bytes 1572872 | tf_op jit(solution)/shard_map/ppermute | solution.py:27
  45.4 1.7 %collective-permute-start.13 = (bf16[64,4096]{1,0:T(8,128)(2,1)S(1)}, bf16[64,4096]{1,0:T(8,128)(2,1)S(1)}, u32[]{:S(2)}, u32[]{:S(2)}) collective-permute-start(bf16[64,4096]{1,0:T(8,128)(2,1)S(1)} %pad_maximum_fusion.1), channel_id=1, source_target_pairs={{0,24},{1,25},{2,26},{3,27},{4,28},{5,29},{6,30},{7,31},{8,0},{9,1... | collective-permute-start | bytes 1572872 | tf_op jit(solution)/shard_map/ppermute | solution.py:27
  47.9 9.8 %shard_map.130.refs_15_.refs_11_.refs_10_ = bf16[48,512,128]{2,1,0:T(8,128)(2,1)} custom-call(bf16[64,512,128]{2,1,0:T(8,128)(2,1)} %pair.3, bf16[256,256]{1,0:T(8,128)(2,1)S(1)} %bitcast.16, bf16[256,256]{1,0:T(8,128)(2,1)S(1)} %get-tuple-element.74.weight, f32[1,256]{1,0:T(1,128)S(1)} %get-tuple-element.75.bias), custom_call_target="tpu_custom_call" | custom-call | flops 9600000000 | bytes 1048576 | tf_op jit(solution)/shard_map/pallas_call | solution.py:342
  57.8 5.6 %shard_map.131 = (bf16[32,256,256]{2,1,0:T(8,128)(2,1)S(1)}, bf16[256,256]{1,0:T(8,128)(2,1)S(1)}, f32[1,256]{1,0:T(1,128)S(1)}) custom-call(s32[4]{0:T(128)S(1)} %pad_add_fusion.here.refs_0_, bf16[2,64,16,128]{3,2,1,0:T(8,128)(2,1)S(1)} %pad_maximum_fusion.2.left_0, bf16[2,64,16,128]{3,2,1,0:T(8,128)(2,1)S(1)} %collective-permute-done.17.left_1, ...), custom_call_target="tpu_custom_call" | custom-call | flops 4000000000 | bytes 12582912 | tf_op jit(solution)/shard_map/pallas_call | solution.py:318
  65.5 2.7 %collective-permute-start.18 = (bf16[64,4096]{1,0:T(8,128)(2,1)S(1)}, bf16[64,4096]{1,0:T(8,128)(2,1)S(1)}, u32[]{:S(2)}, u32[]{:S(2)}) collective-permute-start(bf16[64,4096]{1,0:T(8,128)(2,1)S(1)} %get-tuple-element.116), channel_id=1, source_target_pairs={{0,96},{1,97},{2,98},{3,99},{4,100},{5,101},{6,102},{7,103},{8,104... | collective-permute-start | bytes 1572872 | tf_op jit(solution)/shard_map/ppermute | solution.py:27
  68.3 3.2 %collective-permute-start.20 = (bf16[64,4096]{1,0:T(8,128)(2,1)S(1)}, bf16[64,4096]{1,0:T(8,128)(2,1)S(1)}, u32[]{:S(2)}, u32[]{:S(2)}) collective-permute-start(bf16[64,4096]{1,0:T(8,128)(2,1)S(1)} %get-tuple-element.114), channel_id=1, source_target_pairs={{0,24},{1,25},{2,26},{3,27},{4,28},{5,29},{6,30},{7,31},{8,0},{9,1... | collective-permute-start | bytes 1572872 | tf_op jit(solution)/shard_map/ppermute | solution.py:27
  71.6 3.5 %collective-permute-start.22 = (bf16[32,8192]{1,0:T(8,128)(2,1)S(1)}, bf16[32,8192]{1,0:T(8,128)(2,1)S(1)}, u32[]{:S(2)}, u32[]{:S(2)}) collective-permute-start(bf16[32,8192]{1,0:T(8,128)(2,1)S(1)} %maximum_maximum_fusion.1), channel_id=1, source_target_pairs={{0,4},{1,5},{2,6},{3,7},{4,0},{5,1},{6,2},{7,3},{8,12},{9,13},{10,... | collective-permute-start | bytes 1572872 | tf_op jit(solution)/shard_map/ppermute | solution.py:27
  75.1 8.3 %shard_map.132.refs_15_ = bf16[64,512,128]{2,1,0:T(8,128)(2,1)} custom-call(s32[4]{0:T(128)S(1)} %pad_add_fusion.here.refs_0_, bf16[64,4096]{1,0:T(8,128)(2,1)S(1)} %collective-permute-done.11.refs_1_, bf16[80,4096]{1,0:T(8,128)(2,1)S(1)} %collective-permute-done.12.refs_2_, bf16[64,4096]{1,0:T(8,128)(2,1)S(1)} %collective-permute-done.13.refs_3_, ...), custom_call_target="tpu_custom_call" | custom-call | flops 6400000000 | bytes 16777216 | tf_op jit(solution)/shard_map/pallas_call | solution.py:260
  87.5 3.6 %collective-permute-start.25 = (bf16[16,8192]{1,0:T(8,128)(2,1)S(1)}, bf16[16,8192]{1,0:T(8,128)(2,1)S(1)}, u32[]{:S(2)}, u32[]{:S(2)}) collective-permute-start(bf16[16,8192]{1,0:T(8,128)(2,1)S(1)} %pad_maximum_fusion.11), channel_id=1, source_target_pairs={{0,4},{1,5},{2,6},{3,7},{4,0},{5,1},{6,2},{7,3},{8,12},{9,13},{10,... | collective-permute-start | bytes 786440 | tf_op jit(solution)/shard_map/ppermute | solution.py:27
  91.1 5.3 %shard_map.133.refs_14_ = bf16[64,512,128]{2,1,0:T(8,128)(2,1)} custom-call(s32[4]{0:T(128)S(1)} %pad_add_fusion.here.refs_0_, bf16[64,4096]{1,0:T(8,128)(2,1)S(1)} %collective-permute-done.11.refs_1_, bf16[80,4096]{1,0:T(8,128)(2,1)S(1)} %collective-permute-done.12.refs_2_, ...), custom_call_target="tpu_custom_call", output_to_operand_aliasing={{}: (15, {})} | custom-call | flops 3200000000 | bytes 8388608 | tf_op jit(solution)/shard_map/pallas_call | solution.py:260
  96.5 5.3 %shard_map.134 = bf16[64,512,128]{2,1,0:T(8,128)(2,1)} custom-call(s32[4]{0:T(128)S(1)} %pad_add_fusion.here.refs_0_, bf16[64,4096]{1,0:T(8,128)(2,1)S(1)} %collective-permute-done.19.refs_6_.refs_1_, bf16[64,4096]{1,0:T(8,128)(2,1)S(1)} %collective-permute-done.20.refs_7_.refs_2_, ...), custom_call_target="tpu_custom_call", output_to_operand_aliasing={{}: (14, {})} | custom-call | flops 3200000000 | bytes 8388608 | tf_op jit(solution)/shard_map/pallas_call | solution.py:260
  (95 shorter events, 14.6 us)
Async XLA Ops:
  1.0 11.8 %collective-permute-start = (bf16[16,16,128]{2,1,0:T(8,128)(2,1)S(1)}, bf16[16,16,128]{2,1,0:T(8,128)(2,1)S(1)}, u32[]{:S(2)}, u32[]{:S(2)}) collective-permute-start(bf16[16,16,128]{2,1,0:T(8,128)(2,1)S(1)} %get-tuple-element.55), channel_id=1, source_target_pairs={{0,0},{1,32},{2,64},{3,96},{4,4},{5,36},{6,68},{7,100},{8,8},{9,40... | collective-permute-start | bytes 196616 | tf_op jit(solution)/shard_map/ppermute | solution.py:413
  1.7 11.2 %collective-permute-start.1 = (bf16[16,16,128]{2,1,0:T(8,128)(2,1)S(1)}, bf16[16,16,128]{2,1,0:T(8,128)(2,1)S(1)}, u32[]{:S(2)}, u32[]{:S(2)}) collective-permute-start(bf16[16,16,128]{2,1,0:T(8,128)(2,1)S(1)} %get-tuple-element.56), channel_id=1, source_target_pairs={{0,32},{1,64},{2,96},{3,0},{4,36},{5,68},{6,100},{7,4},{8,40},{9,7... | collective-permute-start | bytes 196616 | tf_op jit(solution)/shard_map/ppermute | solution.py:413
  5.0 9.0 %collective-permute-start.2 = (bf16[16,16,128]{2,1,0:T(8,128)(2,1)S(1)}, bf16[16,16,128]{2,1,0:T(8,128)(2,1)S(1)}, u32[]{:S(2)}, u32[]{:S(2)}) collective-permute-start(bf16[16,16,128]{2,1,0:T(8,128)(2,1)S(1)} %get-tuple-element.57), channel_id=1, source_target_pairs={{0,64},{1,96},{2,0},{3,32},{4,68},{5,100},{6,4},{7,36},{8,72},{9,1... | collective-permute-start | bytes 196616 | tf_op jit(solution)/shard_map/ppermute | solution.py:413
  16.0 10.1 %collective-permute-start.7 = (bf16[16,8192]{1,0:T(8,128)(2,1)S(1)}, bf16[16,8192]{1,0:T(8,128)(2,1)S(1)}, u32[]{:S(2)}, u32[]{:S(2)}) collective-permute-start(bf16[16,8192]{1,0:T(8,128)(2,1)S(1)} %shard_map.128.refs_7_), channel_id=1, source_target_pairs={{0,8},{1,9},{2,10},{3,11},{4,12},{5,13},{6,14},{7,15},{8,16},{9,17... | collective-permute-start | bytes 786440 | tf_op jit(solution)/shard_map/ppermute | solution.py:27
  17.6 10.1 %collective-permute-start.5 = (bf16[16,8192]{1,0:T(8,128)(2,1)S(1)}, bf16[16,8192]{1,0:T(8,128)(2,1)S(1)}, u32[]{:S(2)}, u32[]{:S(2)}) collective-permute-start(bf16[16,8192]{1,0:T(8,128)(2,1)S(1)} %shard_map.128.refs_7_), channel_id=1, source_target_pairs={{0,4},{1,5},{2,6},{3,7},{4,0},{5,1},{6,2},{7,3},{8,12},{9,13},{10,... | collective-permute-start | bytes 786440 | tf_op jit(solution)/shard_map/ppermute | solution.py:27
  20.4 10.0 %collective-permute-start.4 = (bf16[16,8192]{1,0:T(8,128)(2,1)S(1)}, bf16[16,8192]{1,0:T(8,128)(2,1)S(1)}, u32[]{:S(2)}, u32[]{:S(2)}) collective-permute-start(bf16[16,8192]{1,0:T(8,128)(2,1)S(1)} %shard_map.128.refs_7_), channel_id=1, source_target_pairs={{0,24},{1,25},{2,26},{3,27},{4,28},{5,29},{6,30},{7,31},{8,0},{9,1... | collective-permute-start | bytes 786440 | tf_op jit(solution)/shard_map/ppermute | solution.py:27
  22.3 14.8 %collective-permute-start.10 = (bf16[16,8192]{1,0:T(8,128)(2,1)S(1)}, bf16[16,8192]{1,0:T(8,128)(2,1)S(1)}, u32[]{:S(2)}, u32[]{:S(2)}) collective-permute-start(bf16[16,8192]{1,0:T(8,128)(2,1)S(1)} %shard_map.128.refs_7_), channel_id=1, source_target_pairs={{0,32},{1,33},{2,34},{3,35},{4,36},{5,37},{6,38},{7,39},{8,40},{9,... | collective-permute-start | bytes 786440 | tf_op jit(solution)/shard_map/ppermute | solution.py:27
  24.7 12.4 %collective-permute-start.8 = (bf16[16,8192]{1,0:T(8,128)(2,1)S(1)}, bf16[16,8192]{1,0:T(8,128)(2,1)S(1)}, u32[]{:S(2)}, u32[]{:S(2)}) collective-permute-start(bf16[16,8192]{1,0:T(8,128)(2,1)S(1)} %shard_map.128.refs_7_), channel_id=1, source_target_pairs={{0,96},{1,97},{2,98},{3,99},{4,100},{5,101},{6,102},{7,103},{8,104... | collective-permute-start | bytes 786440 | tf_op jit(solution)/shard_map/ppermute | solution.py:27
  26.1 10.9 %collective-permute-start.16 = (bf16[64,16,128]{2,1,0:T(8,128)(2,1)}, bf16[64,16,128]{2,1,0:T(8,128)(2,1)S(1)}, u32[]{:S(2)}, u32[]{:S(2)}) collective-permute-start(bf16[64,16,128]{2,1,0:T(8,128)(2,1)} %param.14), channel_id=1, source_target_pairs={{0,2},{1,3},{2,0},{3,1},{4,6},{5,7},{6,4},{7,5},{8,10},{9,11},{10,... | collective-permute-start | bytes 786440 | tf_op jit(solution)/shard_map/ppermute | solution.py:27
  27.7 9.4 %collective-permute-start.6 = (bf16[16,8192]{1,0:T(8,128)(2,1)S(1)}, bf16[16,8192]{1,0:T(8,128)(2,1)S(1)}, u32[]{:S(2)}, u32[]{:S(2)}) collective-permute-start(bf16[16,8192]{1,0:T(8,128)(2,1)S(1)} %shard_map.128.refs_7_), channel_id=1, source_target_pairs={{0,16},{1,17},{2,18},{3,19},{4,20},{5,21},{6,22},{7,23},{8,24},{9,... | collective-permute-start | bytes 786440 | tf_op jit(solution)/shard_map/ppermute | solution.py:27
  37.0 10.2 %collective-permute-start.17 = (bf16[2,64,16,128]{3,2,1,0:T(8,128)(2,1)S(1)}, bf16[2,64,16,128]{3,2,1,0:T(8,128)(2,1)S(1)}, u32[]{:S(2)}, u32[]{:S(2)}) collective-permute-start(bf16[2,64,16,128]{3,2,1,0:T(8,128)(2,1)S(1)} %pad_maximum_fusion.2.left_0), channel_id=1, source_target_pairs={{0,1},{1,0},{2,3},{3,2},{4,5},{5,4},{6,7},{7,6},{8,9},{9,8},{10,11... | collective-permute-start | bytes 1572872 | tf_op jit(solution)/shard_map/ppermute | solution.py:27
  39.4 24.0 %collective-permute-start.15 = (bf16[32,8192]{1,0:T(8,128)(2,1)S(1)}, bf16[32,8192]{1,0:T(8,128)(2,1)S(1)}, u32[]{:S(2)}, u32[]{:S(2)}) collective-permute-start(bf16[32,8192]{1,0:T(8,128)(2,1)S(1)} %maximum_maximum_fusion), channel_id=1, source_target_pairs={{0,4},{1,5},{2,6},{3,7},{4,0},{5,1},{6,2},{7,3},{8,12},{9,13},{10,... | collective-permute-start | bytes 1572872 | tf_op jit(solution)/shard_map/ppermute | solution.py:27
  42.6 20.8 %collective-permute-start.11 = (bf16[64,4096]{1,0:T(8,128)(2,1)S(1)}, bf16[64,4096]{1,0:T(8,128)(2,1)S(1)}, u32[]{:S(2)}, u32[]{:S(2)}) collective-permute-start(bf16[64,4096]{1,0:T(8,128)(2,1)S(1)} %pad_maximum_fusion), channel_id=1, source_target_pairs={{0,96},{1,97},{2,98},{3,99},{4,100},{5,101},{6,102},{7,103},{8,104... | collective-permute-start | bytes 1572872 | tf_op jit(solution)/shard_map/ppermute | solution.py:27
  45.4 18.0 %collective-permute-start.13 = (bf16[64,4096]{1,0:T(8,128)(2,1)S(1)}, bf16[64,4096]{1,0:T(8,128)(2,1)S(1)}, u32[]{:S(2)}, u32[]{:S(2)}) collective-permute-start(bf16[64,4096]{1,0:T(8,128)(2,1)S(1)} %pad_maximum_fusion.1), channel_id=1, source_target_pairs={{0,24},{1,25},{2,26},{3,27},{4,28},{5,29},{6,30},{7,31},{8,0},{9,1... | collective-permute-start | bytes 1572872 | tf_op jit(solution)/shard_map/ppermute | solution.py:27
  47.1 17.1 %collective-permute-start.12 = (bf16[80,4096]{1,0:T(8,128)(2,1)S(1)}, bf16[80,4096]{1,0:T(8,128)(2,1)S(1)}, u32[]{:S(2)}, u32[]{:S(2)}) collective-permute-start(bf16[80,4096]{1,0:T(8,128)(2,1)S(1)} %constant_dynamic-update-slice_fusion), channel_id=1, source_target_pairs={{0,32},{1,33},{2,34},{3,35},{4,36},{5,37},{6,38},{7,39},{8,40},{9,... | collective-permute-start | bytes 1966088 | tf_op jit(solution)/shard_map/ppermute | solution.py:27
  47.3 17.2 %collective-permute-start.14 = (bf16[80,4096]{1,0:T(8,128)(2,1)S(1)}, bf16[80,4096]{1,0:T(8,128)(2,1)S(1)}, u32[]{:S(2)}, u32[]{:S(2)}) collective-permute-start(bf16[80,4096]{1,0:T(8,128)(2,1)S(1)} %get-tuple-element.117), channel_id=1, source_target_pairs={{0,8},{1,9},{2,10},{3,11},{4,12},{5,13},{6,14},{7,15},{8,16},{9,17... | collective-permute-start | bytes 1966088 | tf_op jit(solution)/shard_map/ppermute | solution.py:27
  64.8 18.7 %collective-permute-start.19 = (bf16[64,4096]{1,0:T(8,128)(2,1)S(1)}, bf16[64,4096]{1,0:T(8,128)(2,1)S(1)}, u32[]{:S(2)}, u32[]{:S(2)}) collective-permute-start(bf16[64,4096]{1,0:T(8,128)(2,1)S(1)} %get-tuple-element.115), channel_id=1, source_target_pairs={{0,32},{1,33},{2,34},{3,35},{4,36},{5,37},{6,38},{7,39},{8,40},{9,... | collective-permute-start | bytes 1572872 | tf_op jit(solution)/shard_map/ppermute | solution.py:27
  65.5 18.0 %collective-permute-start.18 = (bf16[64,4096]{1,0:T(8,128)(2,1)S(1)}, bf16[64,4096]{1,0:T(8,128)(2,1)S(1)}, u32[]{:S(2)}, u32[]{:S(2)}) collective-permute-start(bf16[64,4096]{1,0:T(8,128)(2,1)S(1)} %get-tuple-element.116), channel_id=1, source_target_pairs={{0,96},{1,97},{2,98},{3,99},{4,100},{5,101},{6,102},{7,103},{8,104... | collective-permute-start | bytes 1572872 | tf_op jit(solution)/shard_map/ppermute | solution.py:27
  68.2 15.3 %collective-permute-start.21 = (bf16[64,4096]{1,0:T(8,128)(2,1)S(1)}, bf16[64,4096]{1,0:T(8,128)(2,1)S(1)}, u32[]{:S(2)}, u32[]{:S(2)}) collective-permute-start(bf16[64,4096]{1,0:T(8,128)(2,1)S(1)} %get-tuple-element.113), channel_id=1, source_target_pairs={{0,8},{1,9},{2,10},{3,11},{4,12},{5,13},{6,14},{7,15},{8,16},{9,17... | collective-permute-start | bytes 1572872 | tf_op jit(solution)/shard_map/ppermute | solution.py:27
  68.3 15.2 %collective-permute-start.20 = (bf16[64,4096]{1,0:T(8,128)(2,1)S(1)}, bf16[64,4096]{1,0:T(8,128)(2,1)S(1)}, u32[]{:S(2)}, u32[]{:S(2)}) collective-permute-start(bf16[64,4096]{1,0:T(8,128)(2,1)S(1)} %get-tuple-element.114), channel_id=1, source_target_pairs={{0,24},{1,25},{2,26},{3,27},{4,28},{5,29},{6,30},{7,31},{8,0},{9,1... | collective-permute-start | bytes 1572872 | tf_op jit(solution)/shard_map/ppermute | solution.py:27
  71.6 13.2 %collective-permute-start.22 = (bf16[32,8192]{1,0:T(8,128)(2,1)S(1)}, bf16[32,8192]{1,0:T(8,128)(2,1)S(1)}, u32[]{:S(2)}, u32[]{:S(2)}) collective-permute-start(bf16[32,8192]{1,0:T(8,128)(2,1)S(1)} %maximum_maximum_fusion.1), channel_id=1, source_target_pairs={{0,4},{1,5},{2,6},{3,7},{4,0},{5,1},{6,2},{7,3},{8,12},{9,13},{10,... | collective-permute-start | bytes 1572872 | tf_op jit(solution)/shard_map/ppermute | solution.py:27
  84.9 11.5 %collective-permute-start.23 = (bf16[32,4096]{1,0:T(8,128)(2,1)S(1)}, bf16[32,4096]{1,0:T(8,128)(2,1)S(1)}, u32[]{:S(2)}, u32[]{:S(2)}) collective-permute-start(bf16[32,4096]{1,0:T(8,128)(2,1)S(1)} %pad_maximum_fusion.9), channel_id=1, source_target_pairs={{0,96},{1,97},{2,98},{3,99},{4,100},{5,101},{6,102},{7,103},{8,104... | collective-permute-start | bytes 786440 | tf_op jit(solution)/shard_map/ppermute | solution.py:27
  86.4 10.1 %collective-permute-start.24 = (bf16[32,4096]{1,0:T(8,128)(2,1)S(1)}, bf16[32,4096]{1,0:T(8,128)(2,1)S(1)}, u32[]{:S(2)}, u32[]{:S(2)}) collective-permute-start(bf16[32,4096]{1,0:T(8,128)(2,1)S(1)} %pad_maximum_fusion.10), channel_id=1, source_target_pairs={{0,24},{1,25},{2,26},{3,27},{4,28},{5,29},{6,30},{7,31},{8,0},{9,1... | collective-permute-start | bytes 786440 | tf_op jit(solution)/shard_map/ppermute | solution.py:27
  87.5 8.9 %collective-permute-start.25 = (bf16[16,8192]{1,0:T(8,128)(2,1)S(1)}, bf16[16,8192]{1,0:T(8,128)(2,1)S(1)}, u32[]{:S(2)}, u32[]{:S(2)}) collective-permute-start(bf16[16,8192]{1,0:T(8,128)(2,1)S(1)} %pad_maximum_fusion.11), channel_id=1, source_target_pairs={{0,4},{1,5},{2,6},{3,7},{4,0},{5,1},{6,2},{7,3},{8,12},{9,13},{10,... | collective-permute-start | bytes 786440 | tf_op jit(solution)/shard_map/ppermute | solution.py:27
  (12 other events, 166.0 us)

commit v5 on v4

--- a/solution.py
+++ b/solution.py
@@ -187,9 +187,9 @@
             results.at[rows, pl.ds(b * 16, 16), :], out.at[rows, column(b), :], out_sem.at[b, q]
         )
 
-    for b in range(len(blocks)):
-        gate_copy(b, 0).start()
-        gate_copy(b, 1).start()
+    for half in range(2):
+        for b in range(len(blocks)):
+            gate_copy(b, half).start()
     member = lax.broadcasted_iota(jnp.int32, (8, 128), 0)
 
     def over_four(total):
@@ -216,10 +216,6 @@
             return carry
 
         lax.fori_loop(0, 16, multiply, 0, unroll=16)
-    for b in range(len(blocks)):
-        gate_copy(b, 0).wait()
-        gate_copy(b, 1).wait()
-
     def finish(ip, carry):
         for part in range(columns // 128):
             lanes = slice(part * 128, part * 128 + 128)
@@ -240,6 +236,9 @@
         return carry
 
     for q in range(PARTS):
+        if q < 2:
+            for b in range(len(blocks)):
+                gate_copy(b, q).wait()
         lax.fori_loop(q * 32 // PARTS, (q + 1) * 32 // PARTS, finish, 0, unroll=8)
         for b in range(len(blocks)):
             out_copy(b, q).start()
@@ -440,10 +439,7 @@
     got["X0"] = move(rows, dx=1)
     for step in (1, 3):
         got[f"Y{step}"], got[f"Z{step}"] = move(rows, dy=-step), move(rows, dz=-step)
-    got["X0"], again = lax.optimization_barrier((got["X0"], rows))
-    got["Y2"] = move(again, dy=2)
-    got["Y1"], again = lax.optimization_barrier((got["Y1"], again))
-    got["Z2"] = move(again, dz=2)
+    got["Y2"], got["Z2"] = move(got["Y1"], dy=-1), move(got["Z1"], dz=-1)
     got["Y3"], again = lax.optimization_barrier((got["Y3"], left_panel))
     left_2 = move(again, dc=2)
     gate_0 = run_gate(0, GATE_FIRST, pair_block, *wide_gate)

time: 102 us -> 97.5 us (0.956)
  starting transfers between devices: 50.8 us -> 44.6 us
  waiting for transfers between devices: 6.07 us -> 7.44 us
    ppermute x22, starting transfers between devices: 40.1 us -> 34 us  [move(): return lax.ppermute(value, AXES, pairs)]
    ppermute x22, waiting for transfers between devices: 4.53 us -> 5.9 us  [move(): return lax.ppermute(value, AXES, pairs)]
  transfers between devices with their start and end apart: 26 -> 26, of which waited for: 6 -> 5; matrix products, arithmetic and copies ran while one was open for 1% -> 1% of each run, Pallas kernels for 35% -> 36%
where the time goes in v5:
time: 97.5 us; the launch traced here: 97.2 us
  starting transfers between devices  44.6 us (46%)
  Pallas kernels  42.4 us (43%)
  waiting for transfers between devices  7.44 us (8%)
  local copies, waits for them, and re-layouts  1.6 us (2%)
    ppermute x22, starting transfers between devices, move(): return lax.ppermute(value, AXES, pairs)  34 us
    pallas_call x3, Pallas kernels, run_update(): pl.pallas_call(functools.partial(update_kernel, blocks, len(sources), has...  19 us
    pallas_call x2, Pallas kernels, run_gate(): pl.pallas_call(functools.partial(gate_kernel, first // 16), out_shape=plt...  15 us
    ppermute x4, starting transfers between devices, per_device(): pieces.append(lax.ppermute(parts[s], AXES, pairs))  10.7 us
    ppermute x22, waiting for transfers between devices, move(): return lax.ppermute(value, AXES, pairs)  5.9 us
    pallas_call x1, Pallas kernels, run_left(): pl.pallas_call(left_kernel, out_shape=[jax.ShapeDtypeStruct((32, 256, 256...  5.59 us
  transfers between devices with their start and end apart: 26, of which 5 were waited for; matrix products, arithmetic and copies ran while one was open for 1% of the time, Pallas kernels for 36%

profile of v5, /device:TPU:0, one launch (start us, length us, event | category | flops | bytes accessed | tf_op | source)
XLA Modules:
  0.0 97.2 jit_solution(16860082726576137970)
XLA Ops:
  1.7 3.3 %collective-permute-start.1 = (bf16[16,16,128]{2,1,0:T(8,128)(2,1)S(1)}, bf16[16,16,128]{2,1,0:T(8,128)(2,1)S(1)}, u32[]{:S(2)}, u32[]{:S(2)}) collective-permute-start(bf16[16,16,128]{2,1,0:T(8,128)(2,1)S(1)} %get-tuple-element.52), channel_id=1, source_target_pairs={{0,32},{1,64},{2,96},{3,0},{4,36},{5,68},{6,100},{7,4},{8,40},{9,7... | collective-permute-start | bytes 196616 | tf_op jit(solution)/shard_map/ppermute | solution.py:412
  5.0 4.3 %collective-permute-start.2 = (bf16[16,16,128]{2,1,0:T(8,128)(2,1)S(1)}, bf16[16,16,128]{2,1,0:T(8,128)(2,1)S(1)}, u32[]{:S(2)}, u32[]{:S(2)}) collective-permute-start(bf16[16,16,128]{2,1,0:T(8,128)(2,1)S(1)} %get-tuple-element.53), channel_id=1, source_target_pairs={{0,64},{1,96},{2,0},{3,32},{4,68},{5,100},{6,4},{7,36},{8,72},{9,1... | collective-permute-start | bytes 196616 | tf_op jit(solution)/shard_map/ppermute | solution.py:412
  9.3 2.3 %collective-permute-start.3 = (bf16[16,16,128]{2,1,0:T(8,128)(2,1)S(1)}, bf16[16,16,128]{2,1,0:T(8,128)(2,1)S(1)}, u32[]{:S(2)}, u32[]{:S(2)}) collective-permute-start(bf16[16,16,128]{2,1,0:T(8,128)(2,1)S(1)} %get-tuple-element.54), channel_id=1, source_target_pairs={{0,96},{1,0},{2,32},{3,64},{4,100},{5,4},{6,36},{7,68},{8,104},{9,... | collective-permute-start | bytes 196616 | tf_op jit(solution)/shard_map/ppermute | solution.py:412
  14.4 1.6 %shard_map.128.refs_7_ = bf16[16,8192]{1,0:T(8,128)(2,1)S(1)} custom-call(s32[4]{0:T(128)S(1)} %pad_add_fusion.here.refs_0_, bf16[16,16,128]{2,1,0:T(8,128)(2,1)S(1)} %collective-permute-done.p0, bf16[16,16,128]{2,1,0:T(8,128)(2,1)S(1)} %collective-permute-done.1.p1, bf16[16,16,128]{2,1,0:T(8,128)(2,1)S(1)} %collective-permute-done.2.p2, ...), custom_call_target="tpu_custom_call" | custom-call | tf_op jit(solution)/shard_map/pallas_call | solution.py:301
  16.0 1.6 %collective-permute-start.6 = (bf16[16,8192]{1,0:T(8,128)(2,1)S(1)}, bf16[16,8192]{1,0:T(8,128)(2,1)S(1)}, u32[]{:S(2)}, u32[]{:S(2)}) collective-permute-start(bf16[16,8192]{1,0:T(8,128)(2,1)S(1)} %shard_map.128.refs_7_), channel_id=1, source_target_pairs={{0,8},{1,9},{2,10},{3,11},{4,12},{5,13},{6,14},{7,15},{8,16},{9,17... | collective-permute-start | bytes 786440 | tf_op jit(solution)/shard_map/ppermute | solution.py:27
  17.6 3.7 %collective-permute-start.7 = (bf16[16,8192]{1,0:T(8,128)(2,1)S(1)}, bf16[16,8192]{1,0:T(8,128)(2,1)S(1)}, u32[]{:S(2)}, u32[]{:S(2)}) collective-permute-start(bf16[16,8192]{1,0:T(8,128)(2,1)S(1)} %shard_map.128.refs_7_), channel_id=1, source_target_pairs={{0,96},{1,97},{2,98},{3,99},{4,100},{5,101},{6,102},{7,103},{8,104... | collective-permute-start | bytes 786440 | tf_op jit(solution)/shard_map/ppermute | solution.py:27
  21.3 1.7 %collective-permute-start.4 = (bf16[16,8192]{1,0:T(8,128)(2,1)S(1)}, bf16[16,8192]{1,0:T(8,128)(2,1)S(1)}, u32[]{:S(2)}, u32[]{:S(2)}) collective-permute-start(bf16[16,8192]{1,0:T(8,128)(2,1)S(1)} %shard_map.128.refs_7_), channel_id=1, source_target_pairs={{0,24},{1,25},{2,26},{3,27},{4,28},{5,29},{6,30},{7,31},{8,0},{9,1... | collective-permute-start | bytes 786440 | tf_op jit(solution)/shard_map/ppermute | solution.py:27
  23.1 2.9 %collective-permute-start.10 = (bf16[16,8192]{1,0:T(8,128)(2,1)S(1)}, bf16[16,8192]{1,0:T(8,128)(2,1)S(1)}, u32[]{:S(2)}, u32[]{:S(2)}) collective-permute-start(bf16[16,8192]{1,0:T(8,128)(2,1)S(1)} %shard_map.128.refs_7_), channel_id=1, source_target_pairs={{0,4},{1,5},{2,6},{3,7},{4,0},{5,1},{6,2},{7,3},{8,12},{9,13},{10,... | collective-permute-start | bytes 786440 | tf_op jit(solution)/shard_map/ppermute | solution.py:27
  26.0 1.7 %collective-permute-start.16 = (bf16[64,16,128]{2,1,0:T(8,128)(2,1)}, bf16[64,16,128]{2,1,0:T(8,128)(2,1)S(1)}, u32[]{:S(2)}, u32[]{:S(2)}) collective-permute-start(bf16[64,16,128]{2,1,0:T(8,128)(2,1)} %param.14), channel_id=1, source_target_pairs={{0,2},{1,3},{2,0},{3,1},{4,6},{5,7},{6,4},{7,5},{8,10},{9,11},{10,... | collective-permute-start | bytes 786440 | tf_op jit(solution)/shard_map/ppermute | solution.py:27
  27.7 2.2 %collective-permute-start.8 = (bf16[16,8192]{1,0:T(8,128)(2,1)S(1)}, bf16[16,8192]{1,0:T(8,128)(2,1)S(1)}, u32[]{:S(2)}, u32[]{:S(2)}) collective-permute-start(bf16[16,8192]{1,0:T(8,128)(2,1)S(1)} %collective-permute-done.7.refs_11_), channel_id=1, source_target_pairs={{0,96},{1,97},{2,98},{3,99},{4,100},{5,101},{6,102},{7,103},{8,104... | collective-permute-start | bytes 786440 | tf_op jit(solution)/shard_map/ppermute | solution.py:27
  29.9 1.8 %collective-permute-start.5 = (bf16[16,8192]{1,0:T(8,128)(2,1)S(1)}, bf16[16,8192]{1,0:T(8,128)(2,1)S(1)}, u32[]{:S(2)}, u32[]{:S(2)}) collective-permute-start(bf16[16,8192]{1,0:T(8,128)(2,1)S(1)} %collective-permute-done.4.refs_8_), channel_id=1, source_target_pairs={{0,24},{1,25},{2,26},{3,27},{4,28},{5,29},{6,30},{7,31},{8,0},{9,1... | collective-permute-start | bytes 786440 | tf_op jit(solution)/shard_map/ppermute | solution.py:27
  31.7 5.2 %shard_map.129.refs_14_.refs_10_.refs_9_ = bf16[16,512,128]{2,1,0:T(8,128)(2,1)} custom-call(bf16[64,512,128]{2,1,0:T(8,128)(2,1)} %pair.3, bf16[256,256]{1,0:T(8,128)(2,1)S(1)} %bitcast.15, bf16[256,256]{1,0:T(8,128)(2,1)S(1)} %get-tuple-element.66.weight, f32[1,256]{1,0:T(1,128)S(1)} %get-tuple-element.67.bias), custom_call_target="tpu_custom_call" | custom-call | flops 3200000000 | bytes 1048576 | tf_op jit(solution)/shard_map/pallas_call | solution.py:341
  37.2 3.0 %collective-permute-start.15 = (bf16[32,8192]{1,0:T(8,128)(2,1)S(1)}, bf16[32,8192]{1,0:T(8,128)(2,1)S(1)}, u32[]{:S(2)}, u32[]{:S(2)}) collective-permute-start(bf16[32,8192]{1,0:T(8,128)(2,1)S(1)} %maximum_maximum_fusion), channel_id=1, source_target_pairs={{0,4},{1,5},{2,6},{3,7},{4,0},{5,1},{6,2},{7,3},{8,12},{9,13},{10,... | collective-permute-start | bytes 1572872 | tf_op jit(solution)/shard_map/ppermute | solution.py:27
  41.4 2.0 %collective-permute-start.13 = (bf16[64,4096]{1,0:T(8,128)(2,1)S(1)}, bf16[64,4096]{1,0:T(8,128)(2,1)S(1)}, u32[]{:S(2)}, u32[]{:S(2)}) collective-permute-start(bf16[64,4096]{1,0:T(8,128)(2,1)S(1)} %pad_maximum_fusion.1), channel_id=1, source_target_pairs={{0,24},{1,25},{2,26},{3,27},{4,28},{5,29},{6,30},{7,31},{8,0},{9,1... | collective-permute-start | bytes 1572872 | tf_op jit(solution)/shard_map/ppermute | solution.py:27
  45.3 9.8 %shard_map.130.refs_15_.refs_11_.refs_10_ = bf16[48,512,128]{2,1,0:T(8,128)(2,1)} custom-call(bf16[64,512,128]{2,1,0:T(8,128)(2,1)} %pair.3, bf16[256,256]{1,0:T(8,128)(2,1)S(1)} %bitcast.16, bf16[256,256]{1,0:T(8,128)(2,1)S(1)} %get-tuple-element.66.weight, f32[1,256]{1,0:T(1,128)S(1)} %get-tuple-element.67.bias), custom_call_target="tpu_custom_call" | custom-call | flops 9600000000 | bytes 1048576 | tf_op jit(solution)/shard_map/pallas_call | solution.py:341
  55.2 5.6 %shard_map.131 = (bf16[32,256,256]{2,1,0:T(8,128)(2,1)S(1)}, bf16[256,256]{1,0:T(8,128)(2,1)S(1)}, f32[1,256]{1,0:T(1,128)S(1)}) custom-call(s32[4]{0:T(128)S(1)} %pad_add_fusion.here.refs_0_, bf16[2,64,16,128]{3,2,1,0:T(8,128)(2,1)S(1)} %pad_maximum_fusion.2.left_0, bf16[2,64,16,128]{3,2,1,0:T(8,128)(2,1)S(1)} %collective-permute-done.17.left_1, ...), custom_call_target="tpu_custom_call" | custom-call | flops 4000000000 | bytes 12582912 | tf_op jit(solution)/shard_map/pallas_call | solution.py:317
  62.5 2.9 %collective-permute-start.18 = (bf16[64,4096]{1,0:T(8,128)(2,1)S(1)}, bf16[64,4096]{1,0:T(8,128)(2,1)S(1)}, u32[]{:S(2)}, u32[]{:S(2)}) collective-permute-start(bf16[64,4096]{1,0:T(8,128)(2,1)S(1)} %get-tuple-element.108), channel_id=1, source_target_pairs={{0,96},{1,97},{2,98},{3,99},{4,100},{5,101},{6,102},{7,103},{8,104... | collective-permute-start | bytes 1572872 | tf_op jit(solution)/shard_map/ppermute | solution.py:27
  65.6 3.2 %collective-permute-start.20 = (bf16[64,4096]{1,0:T(8,128)(2,1)S(1)}, bf16[64,4096]{1,0:T(8,128)(2,1)S(1)}, u32[]{:S(2)}, u32[]{:S(2)}) collective-permute-start(bf16[64,4096]{1,0:T(8,128)(2,1)S(1)} %get-tuple-element.106), channel_id=1, source_target_pairs={{0,24},{1,25},{2,26},{3,27},{4,28},{5,29},{6,30},{7,31},{8,0},{9,1... | collective-permute-start | bytes 1572872 | tf_op jit(solution)/shard_map/ppermute | solution.py:27
  69.8 8.4 %shard_map.132.refs_15_ = bf16[64,512,128]{2,1,0:T(8,128)(2,1)} custom-call(s32[4]{0:T(128)S(1)} %pad_add_fusion.here.refs_0_, bf16[64,4096]{1,0:T(8,128)(2,1)S(1)} %collective-permute-done.11.refs_1_, bf16[80,4096]{1,0:T(8,128)(2,1)S(1)} %collective-permute-done.12.refs_2_, bf16[64,4096]{1,0:T(8,128)(2,1)S(1)} %collective-permute-done.13.refs_3_, ...), custom_call_target="tpu_custom_call" | custom-call | flops 6400000000 | bytes 16777216 | tf_op jit(solution)/shard_map/pallas_call | solution.py:259
  78.2 3.0 %collective-permute-done.22.refs_7_ = bf16[32,8192]{1,0:T(8,128)(2,1)S(1)} collective-permute-done((bf16[32,8192]{1,0:T(8,128)(2,1)S(1)}, bf16[32,8192]{1,0:T(8,128)(2,1)S(1)}, u32[]{:S(2)}, u32[]{:S(2)}) %collective-permute-start.22) | collective-permute-done | bytes 524320 | tf_op jit(solution)/shard_map/ppermute | solution.py:27
  81.7 1.7 %collective-permute-start.24 = (bf16[32,4096]{1,0:T(8,128)(2,1)S(1)}, bf16[32,4096]{1,0:T(8,128)(2,1)S(1)}, u32[]{:S(2)}, u32[]{:S(2)}) collective-permute-start(bf16[32,4096]{1,0:T(8,128)(2,1)S(1)} %pad_maximum_fusion.10), channel_id=1, source_target_pairs={{0,24},{1,25},{2,26},{3,27},{4,28},{5,29},{6,30},{7,31},{8,0},{9,1... | collective-permute-start | bytes 786440 | tf_op jit(solution)/shard_map/ppermute | solution.py:27
  84.4 5.3 %shard_map.133.refs_14_ = bf16[64,512,128]{2,1,0:T(8,128)(2,1)} custom-call(s32[4]{0:T(128)S(1)} %pad_add_fusion.here.refs_0_, bf16[64,4096]{1,0:T(8,128)(2,1)S(1)} %collective-permute-done.11.refs_1_, bf16[80,4096]{1,0:T(8,128)(2,1)S(1)} %collective-permute-done.12.refs_2_, ...), custom_call_target="tpu_custom_call", output_to_operand_aliasing={{}: (15, {})} | custom-call | flops 3200000000 | bytes 8388608 | tf_op jit(solution)/shard_map/pallas_call | solution.py:259
  89.8 1.9 %collective-permute-done.25.refs_8_ = bf16[16,8192]{1,0:T(8,128)(2,1)S(1)} collective-permute-done((bf16[16,8192]{1,0:T(8,128)(2,1)S(1)}, bf16[16,8192]{1,0:T(8,128)(2,1)S(1)}, u32[]{:S(2)}, u32[]{:S(2)}) %collective-permute-start.25) | collective-permute-done | bytes 262176 | tf_op jit(solution)/shard_map/ppermute | solution.py:27
  91.7 5.3 %shard_map.134 = bf16[64,512,128]{2,1,0:T(8,128)(2,1)} custom-call(s32[4]{0:T(128)S(1)} %pad_add_fusion.here.refs_0_, bf16[64,4096]{1,0:T(8,128)(2,1)S(1)} %collective-permute-done.19.refs_6_.refs_1_, bf16[64,4096]{1,0:T(8,128)(2,1)S(1)} %collective-permute-done.20.refs_7_.refs_2_, ...), custom_call_target="tpu_custom_call", output_to_operand_aliasing={{}: (14, {})} | custom-call | flops 3200000000 | bytes 8388608 | tf_op jit(solution)/shard_map/pallas_call | solution.py:259
  (95 shorter events, 12.0 us)
Async XLA Ops:
  1.0 11.8 %collective-permute-start = (bf16[16,16,128]{2,1,0:T(8,128)(2,1)S(1)}, bf16[16,16,128]{2,1,0:T(8,128)(2,1)S(1)}, u32[]{:S(2)}, u32[]{:S(2)}) collective-permute-start(bf16[16,16,128]{2,1,0:T(8,128)(2,1)S(1)} %get-tuple-element.51), channel_id=1, source_target_pairs={{0,0},{1,32},{2,64},{3,96},{4,4},{5,36},{6,68},{7,100},{8,8},{9,40... | collective-permute-start | bytes 196616 | tf_op jit(solution)/shard_map/ppermute | solution.py:412
  1.7 11.2 %collective-permute-start.1 = (bf16[16,16,128]{2,1,0:T(8,128)(2,1)S(1)}, bf16[16,16,128]{2,1,0:T(8,128)(2,1)S(1)}, u32[]{:S(2)}, u32[]{:S(2)}) collective-permute-start(bf16[16,16,128]{2,1,0:T(8,128)(2,1)S(1)} %get-tuple-element.52), channel_id=1, source_target_pairs={{0,32},{1,64},{2,96},{3,0},{4,36},{5,68},{6,100},{7,4},{8,40},{9,7... | collective-permute-start | bytes 196616 | tf_op jit(solution)/shard_map/ppermute | solution.py:412
  5.0 9.0 %collective-permute-start.2 = (bf16[16,16,128]{2,1,0:T(8,128)(2,1)S(1)}, bf16[16,16,128]{2,1,0:T(8,128)(2,1)S(1)}, u32[]{:S(2)}, u32[]{:S(2)}) collective-permute-start(bf16[16,16,128]{2,1,0:T(8,128)(2,1)S(1)} %get-tuple-element.53), channel_id=1, source_target_pairs={{0,64},{1,96},{2,0},{3,32},{4,68},{5,100},{6,4},{7,36},{8,72},{9,1... | collective-permute-start | bytes 196616 | tf_op jit(solution)/shard_map/ppermute | solution.py:412
  16.0 10.0 %collective-permute-start.6 = (bf16[16,8192]{1,0:T(8,128)(2,1)S(1)}, bf16[16,8192]{1,0:T(8,128)(2,1)S(1)}, u32[]{:S(2)}, u32[]{:S(2)}) collective-permute-start(bf16[16,8192]{1,0:T(8,128)(2,1)S(1)} %shard_map.128.refs_7_), channel_id=1, source_target_pairs={{0,8},{1,9},{2,10},{3,11},{4,12},{5,13},{6,14},{7,15},{8,16},{9,17... | collective-permute-start | bytes 786440 | tf_op jit(solution)/shard_map/ppermute | solution.py:27
  17.6 10.1 %collective-permute-start.7 = (bf16[16,8192]{1,0:T(8,128)(2,1)S(1)}, bf16[16,8192]{1,0:T(8,128)(2,1)S(1)}, u32[]{:S(2)}, u32[]{:S(2)}) collective-permute-start(bf16[16,8192]{1,0:T(8,128)(2,1)S(1)} %shard_map.128.refs_7_), channel_id=1, source_target_pairs={{0,96},{1,97},{2,98},{3,99},{4,100},{5,101},{6,102},{7,103},{8,104... | collective-permute-start | bytes 786440 | tf_op jit(solution)/shard_map/ppermute | solution.py:27
  21.3 8.6 %collective-permute-start.4 = (bf16[16,8192]{1,0:T(8,128)(2,1)S(1)}, bf16[16,8192]{1,0:T(8,128)(2,1)S(1)}, u32[]{:S(2)}, u32[]{:S(2)}) collective-permute-start(bf16[16,8192]{1,0:T(8,128)(2,1)S(1)} %shard_map.128.refs_7_), channel_id=1, source_target_pairs={{0,24},{1,25},{2,26},{3,27},{4,28},{5,29},{6,30},{7,31},{8,0},{9,1... | collective-permute-start | bytes 786440 | tf_op jit(solution)/shard_map/ppermute | solution.py:27
  23.1 13.9 %collective-permute-start.10 = (bf16[16,8192]{1,0:T(8,128)(2,1)S(1)}, bf16[16,8192]{1,0:T(8,128)(2,1)S(1)}, u32[]{:S(2)}, u32[]{:S(2)}) collective-permute-start(bf16[16,8192]{1,0:T(8,128)(2,1)S(1)} %shard_map.128.refs_7_), channel_id=1, source_target_pairs={{0,4},{1,5},{2,6},{3,7},{4,0},{5,1},{6,2},{7,3},{8,12},{9,13},{10,... | collective-permute-start | bytes 786440 | tf_op jit(solution)/shard_map/ppermute | solution.py:27
  26.0 11.1 %collective-permute-start.9 = (bf16[16,8192]{1,0:T(8,128)(2,1)S(1)}, bf16[16,8192]{1,0:T(8,128)(2,1)S(1)}, u32[]{:S(2)}, u32[]{:S(2)}) collective-permute-start(bf16[16,8192]{1,0:T(8,128)(2,1)S(1)} %shard_map.128.refs_7_), channel_id=1, source_target_pairs={{0,32},{1,33},{2,34},{3,35},{4,36},{5,37},{6,38},{7,39},{8,40},{9,... | collective-permute-start | bytes 786440 | tf_op jit(solution)/shard_map/ppermute | solution.py:27
  26.0 10.9 %collective-permute-start.16 = (bf16[64,16,128]{2,1,0:T(8,128)(2,1)}, bf16[64,16,128]{2,1,0:T(8,128)(2,1)S(1)}, u32[]{:S(2)}, u32[]{:S(2)}) collective-permute-start(bf16[64,16,128]{2,1,0:T(8,128)(2,1)} %param.14), channel_id=1, source_target_pairs={{0,2},{1,3},{2,0},{3,1},{4,6},{5,7},{6,4},{7,5},{8,10},{9,11},{10,... | collective-permute-start | bytes 786440 | tf_op jit(solution)/shard_map/ppermute | solution.py:27
  27.7 9.4 %collective-permute-start.8 = (bf16[16,8192]{1,0:T(8,128)(2,1)S(1)}, bf16[16,8192]{1,0:T(8,128)(2,1)S(1)}, u32[]{:S(2)}, u32[]{:S(2)}) collective-permute-start(bf16[16,8192]{1,0:T(8,128)(2,1)S(1)} %collective-permute-done.7.refs_11_), channel_id=1, source_target_pairs={{0,96},{1,97},{2,98},{3,99},{4,100},{5,101},{6,102},{7,103},{8,104... | collective-permute-start | bytes 786440 | tf_op jit(solution)/shard_map/ppermute | solution.py:27
  37.0 8.0 %collective-permute-start.17 = (bf16[2,64,16,128]{3,2,1,0:T(8,128)(2,1)S(1)}, bf16[2,64,16,128]{3,2,1,0:T(8,128)(2,1)S(1)}, u32[]{:S(2)}, u32[]{:S(2)}) collective-permute-start(bf16[2,64,16,128]{3,2,1,0:T(8,128)(2,1)S(1)} %pad_maximum_fusion.2.left_0), channel_id=1, source_target_pairs={{0,1},{1,0},{2,3},{3,2},{4,5},{5,4},{6,7},{7,6},{8,9},{9,8},{10,11... | collective-permute-start | bytes 1572872 | tf_op jit(solution)/shard_map/ppermute | solution.py:27
  37.2 23.6 %collective-permute-start.15 = (bf16[32,8192]{1,0:T(8,128)(2,1)S(1)}, bf16[32,8192]{1,0:T(8,128)(2,1)S(1)}, u32[]{:S(2)}, u32[]{:S(2)}) collective-permute-start(bf16[32,8192]{1,0:T(8,128)(2,1)S(1)} %maximum_maximum_fusion), channel_id=1, source_target_pairs={{0,4},{1,5},{2,6},{3,7},{4,0},{5,1},{6,2},{7,3},{8,12},{9,13},{10,... | collective-permute-start | bytes 1572872 | tf_op jit(solution)/shard_map/ppermute | solution.py:27
  40.4 20.4 %collective-permute-start.11 = (bf16[64,4096]{1,0:T(8,128)(2,1)S(1)}, bf16[64,4096]{1,0:T(8,128)(2,1)S(1)}, u32[]{:S(2)}, u32[]{:S(2)}) collective-permute-start(bf16[64,4096]{1,0:T(8,128)(2,1)S(1)} %pad_maximum_fusion), channel_id=1, source_target_pairs={{0,96},{1,97},{2,98},{3,99},{4,100},{5,101},{6,102},{7,103},{8,104... | collective-permute-start | bytes 1572872 | tf_op jit(solution)/shard_map/ppermute | solution.py:27
  41.4 19.4 %collective-permute-start.13 = (bf16[64,4096]{1,0:T(8,128)(2,1)S(1)}, bf16[64,4096]{1,0:T(8,128)(2,1)S(1)}, u32[]{:S(2)}, u32[]{:S(2)}) collective-permute-start(bf16[64,4096]{1,0:T(8,128)(2,1)S(1)} %pad_maximum_fusion.1), channel_id=1, source_target_pairs={{0,24},{1,25},{2,26},{3,27},{4,28},{5,29},{6,30},{7,31},{8,0},{9,1... | collective-permute-start | bytes 1572872 | tf_op jit(solution)/shard_map/ppermute | solution.py:27
  43.4 17.4 %collective-permute-start.12 = (bf16[80,4096]{1,0:T(8,128)(2,1)S(1)}, bf16[80,4096]{1,0:T(8,128)(2,1)S(1)}, u32[]{:S(2)}, u32[]{:S(2)}) collective-permute-start(bf16[80,4096]{1,0:T(8,128)(2,1)S(1)} %constant_dynamic-update-slice_fusion), channel_id=1, source_target_pairs={{0,32},{1,33},{2,34},{3,35},{4,36},{5,37},{6,38},{7,39},{8,40},{9,... | collective-permute-start | bytes 1966088 | tf_op jit(solution)/shard_map/ppermute | solution.py:27
  45.0 16.8 %collective-permute-start.14 = (bf16[80,4096]{1,0:T(8,128)(2,1)S(1)}, bf16[80,4096]{1,0:T(8,128)(2,1)S(1)}, u32[]{:S(2)}, u32[]{:S(2)}) collective-permute-start(bf16[80,4096]{1,0:T(8,128)(2,1)S(1)} %get-tuple-element.109), channel_id=1, source_target_pairs={{0,8},{1,9},{2,10},{3,11},{4,12},{5,13},{6,14},{7,15},{8,16},{9,17... | collective-permute-start | bytes 1966088 | tf_op jit(solution)/shard_map/ppermute | solution.py:27
  62.1 16.1 %collective-permute-start.19 = (bf16[64,4096]{1,0:T(8,128)(2,1)S(1)}, bf16[64,4096]{1,0:T(8,128)(2,1)S(1)}, u32[]{:S(2)}, u32[]{:S(2)}) collective-permute-start(bf16[64,4096]{1,0:T(8,128)(2,1)S(1)} %get-tuple-element.107), channel_id=1, source_target_pairs={{0,32},{1,33},{2,34},{3,35},{4,36},{5,37},{6,38},{7,39},{8,40},{9,... | collective-permute-start | bytes 1572872 | tf_op jit(solution)/shard_map/ppermute | solution.py:27
  62.5 15.7 %collective-permute-start.18 = (bf16[64,4096]{1,0:T(8,128)(2,1)S(1)}, bf16[64,4096]{1,0:T(8,128)(2,1)S(1)}, u32[]{:S(2)}, u32[]{:S(2)}) collective-permute-start(bf16[64,4096]{1,0:T(8,128)(2,1)S(1)} %get-tuple-element.108), channel_id=1, source_target_pairs={{0,96},{1,97},{2,98},{3,99},{4,100},{5,101},{6,102},{7,103},{8,104... | collective-permute-start | bytes 1572872 | tf_op jit(solution)/shard_map/ppermute | solution.py:27
  65.5 12.7 %collective-permute-start.21 = (bf16[64,4096]{1,0:T(8,128)(2,1)S(1)}, bf16[64,4096]{1,0:T(8,128)(2,1)S(1)}, u32[]{:S(2)}, u32[]{:S(2)}) collective-permute-start(bf16[64,4096]{1,0:T(8,128)(2,1)S(1)} %get-tuple-element.105), channel_id=1, source_target_pairs={{0,8},{1,9},{2,10},{3,11},{4,12},{5,13},{6,14},{7,15},{8,16},{9,17... | collective-permute-start | bytes 1572872 | tf_op jit(solution)/shard_map/ppermute | solution.py:27
  65.6 12.6 %collective-permute-start.20 = (bf16[64,4096]{1,0:T(8,128)(2,1)S(1)}, bf16[64,4096]{1,0:T(8,128)(2,1)S(1)}, u32[]{:S(2)}, u32[]{:S(2)}) collective-permute-start(bf16[64,4096]{1,0:T(8,128)(2,1)S(1)} %get-tuple-element.106), channel_id=1, source_target_pairs={{0,24},{1,25},{2,26},{3,27},{4,28},{5,29},{6,30},{7,31},{8,0},{9,1... | collective-permute-start | bytes 1572872 | tf_op jit(solution)/shard_map/ppermute | solution.py:27
  68.9 12.3 %collective-permute-start.22 = (bf16[32,8192]{1,0:T(8,128)(2,1)S(1)}, bf16[32,8192]{1,0:T(8,128)(2,1)S(1)}, u32[]{:S(2)}, u32[]{:S(2)}) collective-permute-start(bf16[32,8192]{1,0:T(8,128)(2,1)S(1)} %maximum_maximum_fusion.1), channel_id=1, source_target_pairs={{0,4},{1,5},{2,6},{3,7},{4,0},{5,1},{6,2},{7,3},{8,12},{9,13},{10,... | collective-permute-start | bytes 1572872 | tf_op jit(solution)/shard_map/ppermute | solution.py:27
  81.3 8.5 %collective-permute-start.23 = (bf16[32,4096]{1,0:T(8,128)(2,1)S(1)}, bf16[32,4096]{1,0:T(8,128)(2,1)S(1)}, u32[]{:S(2)}, u32[]{:S(2)}) collective-permute-start(bf16[32,4096]{1,0:T(8,128)(2,1)S(1)} %pad_maximum_fusion.9), channel_id=1, source_target_pairs={{0,96},{1,97},{2,98},{3,99},{4,100},{5,101},{6,102},{7,103},{8,104... | collective-permute-start | bytes 786440 | tf_op jit(solution)/shard_map/ppermute | solution.py:27
  81.7 8.1 %collective-permute-start.24 = (bf16[32,4096]{1,0:T(8,128)(2,1)S(1)}, bf16[32,4096]{1,0:T(8,128)(2,1)S(1)}, u32[]{:S(2)}, u32[]{:S(2)}) collective-permute-start(bf16[32,4096]{1,0:T(8,128)(2,1)S(1)} %pad_maximum_fusion.10), channel_id=1, source_target_pairs={{0,24},{1,25},{2,26},{3,27},{4,28},{5,29},{6,30},{7,31},{8,0},{9,1... | collective-permute-start | bytes 786440 | tf_op jit(solution)/shard_map/ppermute | solution.py:27
  83.5 8.2 %collective-permute-start.25 = (bf16[16,8192]{1,0:T(8,128)(2,1)S(1)}, bf16[16,8192]{1,0:T(8,128)(2,1)S(1)}, u32[]{:S(2)}, u32[]{:S(2)}) collective-permute-start(bf16[16,8192]{1,0:T(8,128)(2,1)S(1)} %pad_maximum_fusion.11), channel_id=1, source_target_pairs={{0,4},{1,5},{2,6},{3,7},{4,0},{5,1},{6,2},{7,3},{8,12},{9,13},{10,... | collective-permute-start | bytes 786440 | tf_op jit(solution)/shard_map/ppermute | solution.py:27
  (12 other events, 154.1 us)

commit v6 on v5

--- a/solution.py
+++ b/solution.py
@@ -12,8 +12,9 @@
 BF16, F32 = jnp.bfloat16, jnp.float32
 DEVICES = [(z, y, x, c) for z in range(4) for y in range(4) for x in range(2) for c in range(4)]
 MIB = 1 << 20
+ENDS = (0, 24, 44, 56, 64)
 PARTS = 4
-GATE_FIRST = 16
+GATE_FIRST = 24
 
 
 def device_id(z, y, x, c):
@@ -89,7 +90,7 @@
 def right_kernel(here, p0, p1, p2, p3, gain, bias, weight, out, normed, swap):
     average = jnp.full((128, 128), 1 / 128, BF16)
     for s, piece in enumerate((p0, p1, p2, p3)):
-        start = pl.multiple_of(lax.rem(here[0] - s + 4, 4) * 16, 16)
+        start = pl.multiple_of((here[0] ^ s) * 16, 16)
         made = scale(standardize(piece[...].reshape(256, 128), average), gain[...], bias[...])
         normed[:, pl.ds(start, 16), :] = made.reshape(16, 16, 128)
 
@@ -151,13 +152,15 @@
         out[i], out[i + 1] = gate[:, :128], gate[:, 128:]
 
 
-def gate_kernel(first, pair, average, weight, bias, out):
+def gate_kernel(first, block, pair, average, weight, bias, out):
+    rows = out.shape[0]
+    spec = pl.BlockSpec((block, 512, 128), lambda n: (n, 0, 0))
     pltpu.emit_pipeline(
         functools.partial(gate_block, average, weight, bias),
-        grid=(out.shape[0] // 16,),
-        in_specs=[pl.BlockSpec((16, 512, 128), lambda n: (n + first, 0, 0))],
-        out_specs=[pl.BlockSpec((16, 512, 128), lambda n: (n, 0, 0))],
-    )(pair, out)
+        grid=(rows // block,),
+        in_specs=[spec],
+        out_specs=[spec],
+    )(pair.at[pl.ds(first, rows)], out)
 
 
 def update_kernel(blocks, n_src, has_out, *refs):
@@ -182,7 +185,7 @@
         )
 
     def out_copy(b, q):
-        rows = pl.ds(q * 64 // PARTS, 64 // PARTS)
+        rows = pl.ds(ENDS[q], ENDS[q + 1] - ENDS[q])
         return pltpu.make_async_copy(
             results.at[rows, pl.ds(b * 16, 16), :], out.at[rows, column(b), :], out_sem.at[b, q]
         )
@@ -239,7 +242,7 @@
         if q < 2:
             for b in range(len(blocks)):
                 gate_copy(b, q).wait()
-        lax.fori_loop(q * 32 // PARTS, (q + 1) * 32 // PARTS, finish, 0, unroll=8)
+        lax.fori_loop(ENDS[q] // 2, ENDS[q + 1] // 2, finish, 0, unroll=(ENDS[q + 1] - ENDS[q]) // 2)
         for b in range(len(blocks)):
             out_copy(b, q).start()
     for b in range(len(blocks)):
@@ -339,7 +342,7 @@
 def run_gate(first, rows, pair, wide, shift):
     average = jnp.kron(jnp.eye(2, dtype=BF16), jnp.full((128, 128), 1 / 128, BF16))
     return pl.pallas_call(
-        functools.partial(gate_kernel, first // 16),
+        functools.partial(gate_kernel, first, rows // 2),
         out_shape=pltpu.HBM((rows, 512, 128), BF16),
         in_specs=[HBM, VMEM, VMEM, VMEM],
         out_specs=HBM,
@@ -403,12 +406,12 @@
 
     here = jnp.stack([z, y, x, c]).astype(jnp.int32)
 
-    parts = [lax.dynamic_slice_in_dim(right_panel, ((c + s) % 4) * 16, 16, 0) for s in range(4)]
+    parts = [lax.dynamic_slice_in_dim(right_panel, (c ^ s) * 16, 16, 0) for s in range(4)]
     parts, weights = lax.optimization_barrier((parts, (ln_gain, ln_bias, w_right, w_gate)))
     gain, bias, weight, wide, shift = run_prepare(*weights)
     pieces = []
     for s in range(4):
-        pairs = [(device_id(z_, y_, x_, c_), device_id(c_ + s, y_, x_, z_)) for z_, y_, x_, c_ in DEVICES]
+        pairs = [(device_id(z_, y_, x_, c_), device_id(c_ ^ s, y_, x_, z_)) for z_, y_, x_, c_ in DEVICES]
         pieces.append(lax.ppermute(parts[s], AXES, pairs))
     rows = run_right(here, pieces, gain, bias, weight)
     rows, wide, shift = lax.optimization_barrier((rows, wide, shift))

time: 97.5 us -> 96.8 us (level)
  starting transfers between devices: 44.6 us -> 41.4 us
  waiting for transfers between devices: 7.44 us -> 10.2 us
    ppermute x22, starting transfers between devices: 34 us -> 31.7 us  [move(): return lax.ppermute(value, AXES, pairs)]
    ppermute x22, waiting for transfers between devices: 5.9 us -> 7.54 us  [move(): return lax.ppermute(value, AXES, pairs)]
    ppermute x4, waiting for transfers between devices: 1.54 us -> 2.68 us  [per_device(): pieces.append(lax.ppermute(parts[s], AXES, pairs))]
  transfers between devices with their start and end apart: 26 -> 26, of which waited for: 5 -> 7; matrix products, arithmetic and copies ran while one was open for 1% -> 1% of each run, Pallas kernels for 36% -> 37%
where the time goes in v6:
time: 96.8 us; the launch traced here: 96.6 us
  Pallas kernels  42.2 us (44%)
  starting transfers between devices  41.4 us (43%)
  waiting for transfers between devices  10.2 us (11%)
  local copies, waits for them, and re-layouts  1.55 us (2%)
    ppermute x22, starting transfers between devices, move(): return lax.ppermute(value, AXES, pairs)  31.7 us
    pallas_call x3, Pallas kernels, run_update(): pl.pallas_call(functools.partial(update_kernel, blocks, len(sources), has...  19 us
    pallas_call x2, Pallas kernels, run_gate(): pl.pallas_call(functools.partial(gate_kernel, first, rows // 2), out_shap...  15 us
    ppermute x4, starting transfers between devices, per_device(): pieces.append(lax.ppermute(parts[s], AXES, pairs))  9.73 us
    ppermute x22, waiting for transfers between devices, move(): return lax.ppermute(value, AXES, pairs)  7.54 us
    pallas_call x1, Pallas kernels, run_left(): pl.pallas_call(left_kernel, out_shape=[jax.ShapeDtypeStruct((32, 256, 256...  5.59 us
    ppermute x4, waiting for transfers between devices, per_device(): pieces.append(lax.ppermute(parts[s], AXES, pairs))  2.68 us
  transfers between devices with their start and end apart: 26, of which 7 were waited for; matrix products, arithmetic and copies ran while one was open for 1% of the time, Pallas kernels for 37%

profile of v6, /device:TPU:0, one launch (start us, length us, event | category | flops | bytes accessed | tf_op | source)
XLA Modules:
  0.0 96.6 jit_solution(3125534181722193252)
XLA Ops:
  1.6 3.3 %collective-permute-start.1 = (bf16[16,16,128]{2,1,0:T(8,128)(2,1)S(1)}, bf16[16,16,128]{2,1,0:T(8,128)(2,1)S(1)}, u32[]{:S(2)}, u32[]{:S(2)}) collective-permute-start(bf16[16,16,128]{2,1,0:T(8,128)(2,1)S(1)} %get-tuple-element.52), channel_id=1, source_target_pairs={{0,32},{1,0},{2,96},{3,64},{4,36},{5,4},{6,100},{7,68},{8,40},{9,8... | collective-permute-start | bytes 196616 | tf_op jit(solution)/shard_map/ppermute | solution.py:415
  5.0 4.3 %collective-permute-start.2 = (bf16[16,16,128]{2,1,0:T(8,128)(2,1)S(1)}, bf16[16,16,128]{2,1,0:T(8,128)(2,1)S(1)}, u32[]{:S(2)}, u32[]{:S(2)}) collective-permute-start(bf16[16,16,128]{2,1,0:T(8,128)(2,1)S(1)} %get-tuple-element.53), channel_id=1, source_target_pairs={{0,64},{1,96},{2,0},{3,32},{4,68},{5,100},{6,4},{7,36},{8,72},{9,1... | collective-permute-start | bytes 196616 | tf_op jit(solution)/shard_map/ppermute | solution.py:415
  9.3 1.4 %collective-permute-start.3 = (bf16[16,16,128]{2,1,0:T(8,128)(2,1)S(1)}, bf16[16,16,128]{2,1,0:T(8,128)(2,1)S(1)}, u32[]{:S(2)}, u32[]{:S(2)}) collective-permute-start(bf16[16,16,128]{2,1,0:T(8,128)(2,1)S(1)} %get-tuple-element.54), channel_id=1, source_target_pairs={{0,96},{1,64},{2,32},{3,0},{4,100},{5,68},{6,36},{7,4},{8,104},{9,... | collective-permute-start | bytes 196616 | tf_op jit(solution)/shard_map/ppermute | solution.py:415
  11.9 2.1 %collective-permute-done.2.p2 = bf16[16,16,128]{2,1,0:T(8,128)(2,1)S(1)} collective-permute-done((bf16[16,16,128]{2,1,0:T(8,128)(2,1)S(1)}, bf16[16,16,128]{2,1,0:T(8,128)(2,1)S(1)}, u32[]{:S(2)}, u32[]{:S(2)}) %collective-permute-start.2) | collective-permute-done | bytes 65568 | tf_op jit(solution)/shard_map/ppermute | solution.py:415
  14.5 1.6 %shard_map.128.refs_7_ = bf16[16,8192]{1,0:T(8,128)(2,1)S(1)} custom-call(s32[4]{0:T(128)S(1)} %pad_add_fusion.here.refs_0_, bf16[16,16,128]{2,1,0:T(8,128)(2,1)S(1)} %collective-permute-done.p0, bf16[16,16,128]{2,1,0:T(8,128)(2,1)S(1)} %collective-permute-done.1.p1, bf16[16,16,128]{2,1,0:T(8,128)(2,1)S(1)} %collective-permute-done.2.p2, ...), custom_call_target="tpu_custom_call" | custom-call | tf_op jit(solution)/shard_map/pallas_call | solution.py:304
  16.2 1.6 %collective-permute-start.6 = (bf16[16,8192]{1,0:T(8,128)(2,1)S(1)}, bf16[16,8192]{1,0:T(8,128)(2,1)S(1)}, u32[]{:S(2)}, u32[]{:S(2)}) collective-permute-start(bf16[16,8192]{1,0:T(8,128)(2,1)S(1)} %shard_map.128.refs_7_), channel_id=1, source_target_pairs={{0,8},{1,9},{2,10},{3,11},{4,12},{5,13},{6,14},{7,15},{8,16},{9,17... | collective-permute-start | bytes 786440 | tf_op jit(solution)/shard_map/ppermute | solution.py:28
  17.8 3.4 %collective-permute-start.7 = (bf16[16,8192]{1,0:T(8,128)(2,1)S(1)}, bf16[16,8192]{1,0:T(8,128)(2,1)S(1)}, u32[]{:S(2)}, u32[]{:S(2)}) collective-permute-start(bf16[16,8192]{1,0:T(8,128)(2,1)S(1)} %shard_map.128.refs_7_), channel_id=1, source_target_pairs={{0,96},{1,97},{2,98},{3,99},{4,100},{5,101},{6,102},{7,103},{8,104... | collective-permute-start | bytes 786440 | tf_op jit(solution)/shard_map/ppermute | solution.py:28
  21.3 1.7 %collective-permute-start.4 = (bf16[16,8192]{1,0:T(8,128)(2,1)S(1)}, bf16[16,8192]{1,0:T(8,128)(2,1)S(1)}, u32[]{:S(2)}, u32[]{:S(2)}) collective-permute-start(bf16[16,8192]{1,0:T(8,128)(2,1)S(1)} %shard_map.128.refs_7_), channel_id=1, source_target_pairs={{0,24},{1,25},{2,26},{3,27},{4,28},{5,29},{6,30},{7,31},{8,0},{9,1... | collective-permute-start | bytes 786440 | tf_op jit(solution)/shard_map/ppermute | solution.py:28
  23.1 3.0 %collective-permute-start.10 = (bf16[16,8192]{1,0:T(8,128)(2,1)S(1)}, bf16[16,8192]{1,0:T(8,128)(2,1)S(1)}, u32[]{:S(2)}, u32[]{:S(2)}) collective-permute-start(bf16[16,8192]{1,0:T(8,128)(2,1)S(1)} %shard_map.128.refs_7_), channel_id=1, source_target_pairs={{0,4},{1,5},{2,6},{3,7},{4,0},{5,1},{6,2},{7,3},{8,12},{9,13},{10,... | collective-permute-start | bytes 786440 | tf_op jit(solution)/shard_map/ppermute | solution.py:28
  26.6 1.6 %collective-permute-start.16 = (bf16[64,16,128]{2,1,0:T(8,128)(2,1)}, bf16[64,16,128]{2,1,0:T(8,128)(2,1)S(1)}, u32[]{:S(2)}, u32[]{:S(2)}) collective-permute-start(bf16[64,16,128]{2,1,0:T(8,128)(2,1)} %param.14), channel_id=1, source_target_pairs={{0,2},{1,3},{2,0},{3,1},{4,6},{5,7},{6,4},{7,5},{8,10},{9,11},{10,... | collective-permute-start | bytes 786440 | tf_op jit(solution)/shard_map/ppermute | solution.py:28
  29.4 1.8 %collective-permute-start.5 = (bf16[16,8192]{1,0:T(8,128)(2,1)S(1)}, bf16[16,8192]{1,0:T(8,128)(2,1)S(1)}, u32[]{:S(2)}, u32[]{:S(2)}) collective-permute-start(bf16[16,8192]{1,0:T(8,128)(2,1)S(1)} %collective-permute-done.4.refs_8_), channel_id=1, source_target_pairs={{0,24},{1,25},{2,26},{3,27},{4,28},{5,29},{6,30},{7,31},{8,0},{9,1... | collective-permute-start | bytes 786440 | tf_op jit(solution)/shard_map/ppermute | solution.py:28
  31.2 6.1 %shard_map.129.refs_14_.refs_10_.refs_9_ = bf16[24,512,128]{2,1,0:T(8,128)(2,1)} custom-call(bf16[64,512,128]{2,1,0:T(8,128)(2,1)} %pair.3, bf16[256,256]{1,0:T(8,128)(2,1)S(1)} %bitcast.15, bf16[256,256]{1,0:T(8,128)(2,1)S(1)} %get-tuple-element.66.weight, f32[1,256]{1,0:T(1,128)S(1)} %get-tuple-element.67.bias), custom_call_target="tpu_custom_call" | custom-call | flops 4800000000 | bytes 1048576 | tf_op jit(solution)/shard_map/pallas_call | solution.py:344
  37.7 2.9 %collective-permute-start.15 = (bf16[32,8192]{1,0:T(8,128)(2,1)S(1)}, bf16[32,8192]{1,0:T(8,128)(2,1)S(1)}, u32[]{:S(2)}, u32[]{:S(2)}) collective-permute-start(bf16[32,8192]{1,0:T(8,128)(2,1)S(1)} %maximum_maximum_fusion), channel_id=1, source_target_pairs={{0,4},{1,5},{2,6},{3,7},{4,0},{5,1},{6,2},{7,3},{8,12},{9,13},{10,... | collective-permute-start | bytes 1572872 | tf_op jit(solution)/shard_map/ppermute | solution.py:28
  41.7 2.3 %collective-permute-start.13 = (bf16[64,4096]{1,0:T(8,128)(2,1)S(1)}, bf16[64,4096]{1,0:T(8,128)(2,1)S(1)}, u32[]{:S(2)}, u32[]{:S(2)}) collective-permute-start(bf16[64,4096]{1,0:T(8,128)(2,1)S(1)} %pad_maximum_fusion.1), channel_id=1, source_target_pairs={{0,24},{1,25},{2,26},{3,27},{4,28},{5,29},{6,30},{7,31},{8,0},{9,1... | collective-permute-start | bytes 1572872 | tf_op jit(solution)/shard_map/ppermute | solution.py:28
  45.6 8.9 %shard_map.130.refs_15_.refs_11_.refs_10_ = bf16[40,512,128]{2,1,0:T(8,128)(2,1)} custom-call(bf16[64,512,128]{2,1,0:T(8,128)(2,1)} %pair.3, bf16[256,256]{1,0:T(8,128)(2,1)S(1)} %bitcast.16, bf16[256,256]{1,0:T(8,128)(2,1)S(1)} %get-tuple-element.66.weight, f32[1,256]{1,0:T(1,128)S(1)} %get-tuple-element.67.bias), custom_call_target="tpu_custom_call" | custom-call | flops 8000000000 | bytes 1048576 | tf_op jit(solution)/shard_map/pallas_call | solution.py:344
  54.5 5.6 %shard_map.131 = (bf16[32,256,256]{2,1,0:T(8,128)(2,1)S(1)}, bf16[256,256]{1,0:T(8,128)(2,1)S(1)}, f32[1,256]{1,0:T(1,128)S(1)}) custom-call(s32[4]{0:T(128)S(1)} %pad_add_fusion.here.refs_0_, bf16[2,64,16,128]{3,2,1,0:T(8,128)(2,1)S(1)} %pad_maximum_fusion.2.left_0, bf16[2,64,16,128]{3,2,1,0:T(8,128)(2,1)S(1)} %collective-permute-done.17.left_1, ...), custom_call_target="tpu_custom_call" | custom-call | flops 4000000000 | bytes 12582912 | tf_op jit(solution)/shard_map/pallas_call | solution.py:320
  60.5 1.7 %collective-permute-done.14.refs_4_ = bf16[80,4096]{1,0:T(8,128)(2,1)S(1)} collective-permute-done((bf16[80,4096]{1,0:T(8,128)(2,1)S(1)}, bf16[80,4096]{1,0:T(8,128)(2,1)S(1)}, u32[]{:S(2)}, u32[]{:S(2)}) %collective-permute-start.14) | collective-permute-done | bytes 655392 | tf_op jit(solution)/shard_map/ppermute | solution.py:28
  62.9 2.9 %collective-permute-start.18 = (bf16[64,4096]{1,0:T(8,128)(2,1)S(1)}, bf16[64,4096]{1,0:T(8,128)(2,1)S(1)}, u32[]{:S(2)}, u32[]{:S(2)}) collective-permute-start(bf16[64,4096]{1,0:T(8,128)(2,1)S(1)} %get-tuple-element.108), channel_id=1, source_target_pairs={{0,96},{1,97},{2,98},{3,99},{4,100},{5,101},{6,102},{7,103},{8,104... | collective-permute-start | bytes 1572872 | tf_op jit(solution)/shard_map/ppermute | solution.py:28
  66.0 3.2 %collective-permute-start.20 = (bf16[64,4096]{1,0:T(8,128)(2,1)S(1)}, bf16[64,4096]{1,0:T(8,128)(2,1)S(1)}, u32[]{:S(2)}, u32[]{:S(2)}) collective-permute-start(bf16[64,4096]{1,0:T(8,128)(2,1)S(1)} %get-tuple-element.106), channel_id=1, source_target_pairs={{0,24},{1,25},{2,26},{3,27},{4,28},{5,29},{6,30},{7,31},{8,0},{9,1... | collective-permute-start | bytes 1572872 | tf_op jit(solution)/shard_map/ppermute | solution.py:28
  70.1 8.3 %shard_map.132.refs_15_ = bf16[64,512,128]{2,1,0:T(8,128)(2,1)} custom-call(s32[4]{0:T(128)S(1)} %pad_add_fusion.here.refs_0_, bf16[64,4096]{1,0:T(8,128)(2,1)S(1)} %collective-permute-done.11.refs_1_, bf16[80,4096]{1,0:T(8,128)(2,1)S(1)} %collective-permute-done.12.refs_2_, bf16[64,4096]{1,0:T(8,128)(2,1)S(1)} %collective-permute-done.13.refs_3_, ...), custom_call_target="tpu_custom_call" | custom-call | flops 6400000000 | bytes 16777216 | tf_op jit(solution)/shard_map/pallas_call | solution.py:262
  78.4 3.3 %collective-permute-done.22.refs_7_ = bf16[32,8192]{1,0:T(8,128)(2,1)S(1)} collective-permute-done((bf16[32,8192]{1,0:T(8,128)(2,1)S(1)}, bf16[32,8192]{1,0:T(8,128)(2,1)S(1)}, u32[]{:S(2)}, u32[]{:S(2)}) %collective-permute-start.22) | collective-permute-done | bytes 524320 | tf_op jit(solution)/shard_map/ppermute | solution.py:28
  84.0 5.4 %shard_map.133.refs_14_ = bf16[64,512,128]{2,1,0:T(8,128)(2,1)} custom-call(s32[4]{0:T(128)S(1)} %pad_add_fusion.here.refs_0_, bf16[64,4096]{1,0:T(8,128)(2,1)S(1)} %collective-permute-done.11.refs_1_, bf16[80,4096]{1,0:T(8,128)(2,1)S(1)} %collective-permute-done.12.refs_2_, ...), custom_call_target="tpu_custom_call", output_to_operand_aliasing={{}: (15, {})} | custom-call | flops 3200000000 | bytes 8388608 | tf_op jit(solution)/shard_map/pallas_call | solution.py:262
  89.4 1.6 %collective-permute-done.25.refs_8_ = bf16[16,8192]{1,0:T(8,128)(2,1)S(1)} collective-permute-done((bf16[16,8192]{1,0:T(8,128)(2,1)S(1)}, bf16[16,8192]{1,0:T(8,128)(2,1)S(1)}, u32[]{:S(2)}, u32[]{:S(2)}) %collective-permute-start.25) | collective-permute-done | bytes 262176 | tf_op jit(solution)/shard_map/ppermute | solution.py:28
  91.1 5.4 %shard_map.134 = bf16[64,512,128]{2,1,0:T(8,128)(2,1)} custom-call(s32[4]{0:T(128)S(1)} %pad_add_fusion.here.refs_0_, bf16[64,4096]{1,0:T(8,128)(2,1)S(1)} %collective-permute-done.19.refs_6_.refs_1_, bf16[64,4096]{1,0:T(8,128)(2,1)S(1)} %collective-permute-done.20.refs_7_.refs_2_, ...), custom_call_target="tpu_custom_call", output_to_operand_aliasing={{}: (14, {})} | custom-call | flops 3200000000 | bytes 8388608 | tf_op jit(solution)/shard_map/pallas_call | solution.py:262
  (95 shorter events, 12.6 us)
Async XLA Ops:
  1.0 10.9 %collective-permute-start = (bf16[16,16,128]{2,1,0:T(8,128)(2,1)S(1)}, bf16[16,16,128]{2,1,0:T(8,128)(2,1)S(1)}, u32[]{:S(2)}, u32[]{:S(2)}) collective-permute-start(bf16[16,16,128]{2,1,0:T(8,128)(2,1)S(1)} %get-tuple-element.51), channel_id=1, source_target_pairs={{0,0},{1,32},{2,64},{3,96},{4,4},{5,36},{6,68},{7,100},{8,8},{9,40... | collective-permute-start | bytes 196616 | tf_op jit(solution)/shard_map/ppermute | solution.py:415
  1.6 10.2 %collective-permute-start.1 = (bf16[16,16,128]{2,1,0:T(8,128)(2,1)S(1)}, bf16[16,16,128]{2,1,0:T(8,128)(2,1)S(1)}, u32[]{:S(2)}, u32[]{:S(2)}) collective-permute-start(bf16[16,16,128]{2,1,0:T(8,128)(2,1)S(1)} %get-tuple-element.52), channel_id=1, source_target_pairs={{0,32},{1,0},{2,96},{3,64},{4,36},{5,4},{6,100},{7,68},{8,40},{9,8... | collective-permute-start | bytes 196616 | tf_op jit(solution)/shard_map/ppermute | solution.py:415
  5.0 9.0 %collective-permute-start.2 = (bf16[16,16,128]{2,1,0:T(8,128)(2,1)S(1)}, bf16[16,16,128]{2,1,0:T(8,128)(2,1)S(1)}, u32[]{:S(2)}, u32[]{:S(2)}) collective-permute-start(bf16[16,16,128]{2,1,0:T(8,128)(2,1)S(1)} %get-tuple-element.53), channel_id=1, source_target_pairs={{0,64},{1,96},{2,0},{3,32},{4,68},{5,100},{6,4},{7,36},{8,72},{9,1... | collective-permute-start | bytes 196616 | tf_op jit(solution)/shard_map/ppermute | solution.py:415
  16.2 10.4 %collective-permute-start.6 = (bf16[16,8192]{1,0:T(8,128)(2,1)S(1)}, bf16[16,8192]{1,0:T(8,128)(2,1)S(1)}, u32[]{:S(2)}, u32[]{:S(2)}) collective-permute-start(bf16[16,8192]{1,0:T(8,128)(2,1)S(1)} %shard_map.128.refs_7_), channel_id=1, source_target_pairs={{0,8},{1,9},{2,10},{3,11},{4,12},{5,13},{6,14},{7,15},{8,16},{9,17... | collective-permute-start | bytes 786440 | tf_op jit(solution)/shard_map/ppermute | solution.py:28
  17.8 10.4 %collective-permute-start.7 = (bf16[16,8192]{1,0:T(8,128)(2,1)S(1)}, bf16[16,8192]{1,0:T(8,128)(2,1)S(1)}, u32[]{:S(2)}, u32[]{:S(2)}) collective-permute-start(bf16[16,8192]{1,0:T(8,128)(2,1)S(1)} %shard_map.128.refs_7_), channel_id=1, source_target_pairs={{0,96},{1,97},{2,98},{3,99},{4,100},{5,101},{6,102},{7,103},{8,104... | collective-permute-start | bytes 786440 | tf_op jit(solution)/shard_map/ppermute | solution.py:28
  21.3 8.1 %collective-permute-start.4 = (bf16[16,8192]{1,0:T(8,128)(2,1)S(1)}, bf16[16,8192]{1,0:T(8,128)(2,1)S(1)}, u32[]{:S(2)}, u32[]{:S(2)}) collective-permute-start(bf16[16,8192]{1,0:T(8,128)(2,1)S(1)} %shard_map.128.refs_7_), channel_id=1, source_target_pairs={{0,24},{1,25},{2,26},{3,27},{4,28},{5,29},{6,30},{7,31},{8,0},{9,1... | collective-permute-start | bytes 786440 | tf_op jit(solution)/shard_map/ppermute | solution.py:28
  23.1 14.4 %collective-permute-start.10 = (bf16[16,8192]{1,0:T(8,128)(2,1)S(1)}, bf16[16,8192]{1,0:T(8,128)(2,1)S(1)}, u32[]{:S(2)}, u32[]{:S(2)}) collective-permute-start(bf16[16,8192]{1,0:T(8,128)(2,1)S(1)} %shard_map.128.refs_7_), channel_id=1, source_target_pairs={{0,4},{1,5},{2,6},{3,7},{4,0},{5,1},{6,2},{7,3},{8,12},{9,13},{10,... | collective-permute-start | bytes 786440 | tf_op jit(solution)/shard_map/ppermute | solution.py:28
  26.1 11.4 %collective-permute-start.9 = (bf16[16,8192]{1,0:T(8,128)(2,1)S(1)}, bf16[16,8192]{1,0:T(8,128)(2,1)S(1)}, u32[]{:S(2)}, u32[]{:S(2)}) collective-permute-start(bf16[16,8192]{1,0:T(8,128)(2,1)S(1)} %shard_map.128.refs_7_), channel_id=1, source_target_pairs={{0,32},{1,33},{2,34},{3,35},{4,36},{5,37},{6,38},{7,39},{8,40},{9,... | collective-permute-start | bytes 786440 | tf_op jit(solution)/shard_map/ppermute | solution.py:28
  26.6 10.7 %collective-permute-start.16 = (bf16[64,16,128]{2,1,0:T(8,128)(2,1)}, bf16[64,16,128]{2,1,0:T(8,128)(2,1)S(1)}, u32[]{:S(2)}, u32[]{:S(2)}) collective-permute-start(bf16[64,16,128]{2,1,0:T(8,128)(2,1)} %param.14), channel_id=1, source_target_pairs={{0,2},{1,3},{2,0},{3,1},{4,6},{5,7},{6,4},{7,5},{8,10},{9,11},{10,... | collective-permute-start | bytes 786440 | tf_op jit(solution)/shard_map/ppermute | solution.py:28
  28.2 9.3 %collective-permute-start.8 = (bf16[16,8192]{1,0:T(8,128)(2,1)S(1)}, bf16[16,8192]{1,0:T(8,128)(2,1)S(1)}, u32[]{:S(2)}, u32[]{:S(2)}) collective-permute-start(bf16[16,8192]{1,0:T(8,128)(2,1)S(1)} %collective-permute-done.7.refs_11_), channel_id=1, source_target_pairs={{0,96},{1,97},{2,98},{3,99},{4,100},{5,101},{6,102},{7,103},{8,104... | collective-permute-start | bytes 786440 | tf_op jit(solution)/shard_map/ppermute | solution.py:28
  29.4 8.1 %collective-permute-start.5 = (bf16[16,8192]{1,0:T(8,128)(2,1)S(1)}, bf16[16,8192]{1,0:T(8,128)(2,1)S(1)}, u32[]{:S(2)}, u32[]{:S(2)}) collective-permute-start(bf16[16,8192]{1,0:T(8,128)(2,1)S(1)} %collective-permute-done.4.refs_8_), channel_id=1, source_target_pairs={{0,24},{1,25},{2,26},{3,27},{4,28},{5,29},{6,30},{7,31},{8,0},{9,1... | collective-permute-start | bytes 786440 | tf_op jit(solution)/shard_map/ppermute | solution.py:28
  37.4 7.9 %collective-permute-start.17 = (bf16[2,64,16,128]{3,2,1,0:T(8,128)(2,1)S(1)}, bf16[2,64,16,128]{3,2,1,0:T(8,128)(2,1)S(1)}, u32[]{:S(2)}, u32[]{:S(2)}) collective-permute-start(bf16[2,64,16,128]{3,2,1,0:T(8,128)(2,1)S(1)} %pad_maximum_fusion.2.left_0), channel_id=1, source_target_pairs={{0,1},{1,0},{2,3},{3,2},{4,5},{5,4},{6,7},{7,6},{8,9},{9,8},{10,11... | collective-permute-start | bytes 1572872 | tf_op jit(solution)/shard_map/ppermute | solution.py:28
  37.7 22.5 %collective-permute-start.15 = (bf16[32,8192]{1,0:T(8,128)(2,1)S(1)}, bf16[32,8192]{1,0:T(8,128)(2,1)S(1)}, u32[]{:S(2)}, u32[]{:S(2)}) collective-permute-start(bf16[32,8192]{1,0:T(8,128)(2,1)S(1)} %maximum_maximum_fusion), channel_id=1, source_target_pairs={{0,4},{1,5},{2,6},{3,7},{4,0},{5,1},{6,2},{7,3},{8,12},{9,13},{10,... | collective-permute-start | bytes 1572872 | tf_op jit(solution)/shard_map/ppermute | solution.py:28
  40.8 19.4 %collective-permute-start.11 = (bf16[64,4096]{1,0:T(8,128)(2,1)S(1)}, bf16[64,4096]{1,0:T(8,128)(2,1)S(1)}, u32[]{:S(2)}, u32[]{:S(2)}) collective-permute-start(bf16[64,4096]{1,0:T(8,128)(2,1)S(1)} %pad_maximum_fusion), channel_id=1, source_target_pairs={{0,96},{1,97},{2,98},{3,99},{4,100},{5,101},{6,102},{7,103},{8,104... | collective-permute-start | bytes 1572872 | tf_op jit(solution)/shard_map/ppermute | solution.py:28
  41.7 18.4 %collective-permute-start.13 = (bf16[64,4096]{1,0:T(8,128)(2,1)S(1)}, bf16[64,4096]{1,0:T(8,128)(2,1)S(1)}, u32[]{:S(2)}, u32[]{:S(2)}) collective-permute-start(bf16[64,4096]{1,0:T(8,128)(2,1)S(1)} %pad_maximum_fusion.1), channel_id=1, source_target_pairs={{0,24},{1,25},{2,26},{3,27},{4,28},{5,29},{6,30},{7,31},{8,0},{9,1... | collective-permute-start | bytes 1572872 | tf_op jit(solution)/shard_map/ppermute | solution.py:28
  44.0 16.5 %collective-permute-start.12 = (bf16[80,4096]{1,0:T(8,128)(2,1)S(1)}, bf16[80,4096]{1,0:T(8,128)(2,1)S(1)}, u32[]{:S(2)}, u32[]{:S(2)}) collective-permute-start(bf16[80,4096]{1,0:T(8,128)(2,1)S(1)} %constant_dynamic-update-slice_fusion), channel_id=1, source_target_pairs={{0,32},{1,33},{2,34},{3,35},{4,36},{5,37},{6,38},{7,39},{8,40},{9,... | collective-permute-start | bytes 1966088 | tf_op jit(solution)/shard_map/ppermute | solution.py:28
  45.3 16.9 %collective-permute-start.14 = (bf16[80,4096]{1,0:T(8,128)(2,1)S(1)}, bf16[80,4096]{1,0:T(8,128)(2,1)S(1)}, u32[]{:S(2)}, u32[]{:S(2)}) collective-permute-start(bf16[80,4096]{1,0:T(8,128)(2,1)S(1)} %get-tuple-element.109), channel_id=1, source_target_pairs={{0,8},{1,9},{2,10},{3,11},{4,12},{5,13},{6,14},{7,15},{8,16},{9,17... | collective-permute-start | bytes 1966088 | tf_op jit(solution)/shard_map/ppermute | solution.py:28
  62.5 15.8 %collective-permute-start.19 = (bf16[64,4096]{1,0:T(8,128)(2,1)S(1)}, bf16[64,4096]{1,0:T(8,128)(2,1)S(1)}, u32[]{:S(2)}, u32[]{:S(2)}) collective-permute-start(bf16[64,4096]{1,0:T(8,128)(2,1)S(1)} %get-tuple-element.107), channel_id=1, source_target_pairs={{0,32},{1,33},{2,34},{3,35},{4,36},{5,37},{6,38},{7,39},{8,40},{9,... | collective-permute-start | bytes 1572872 | tf_op jit(solution)/shard_map/ppermute | solution.py:28
  62.9 15.4 %collective-permute-start.18 = (bf16[64,4096]{1,0:T(8,128)(2,1)S(1)}, bf16[64,4096]{1,0:T(8,128)(2,1)S(1)}, u32[]{:S(2)}, u32[]{:S(2)}) collective-permute-start(bf16[64,4096]{1,0:T(8,128)(2,1)S(1)} %get-tuple-element.108), channel_id=1, source_target_pairs={{0,96},{1,97},{2,98},{3,99},{4,100},{5,101},{6,102},{7,103},{8,104... | collective-permute-start | bytes 1572872 | tf_op jit(solution)/shard_map/ppermute | solution.py:28
  65.9 12.5 %collective-permute-start.21 = (bf16[64,4096]{1,0:T(8,128)(2,1)S(1)}, bf16[64,4096]{1,0:T(8,128)(2,1)S(1)}, u32[]{:S(2)}, u32[]{:S(2)}) collective-permute-start(bf16[64,4096]{1,0:T(8,128)(2,1)S(1)} %get-tuple-element.105), channel_id=1, source_target_pairs={{0,8},{1,9},{2,10},{3,11},{4,12},{5,13},{6,14},{7,15},{8,16},{9,17... | collective-permute-start | bytes 1572872 | tf_op jit(solution)/shard_map/ppermute | solution.py:28
  66.0 12.4 %collective-permute-start.20 = (bf16[64,4096]{1,0:T(8,128)(2,1)S(1)}, bf16[64,4096]{1,0:T(8,128)(2,1)S(1)}, u32[]{:S(2)}, u32[]{:S(2)}) collective-permute-start(bf16[64,4096]{1,0:T(8,128)(2,1)S(1)} %get-tuple-element.106), channel_id=1, source_target_pairs={{0,24},{1,25},{2,26},{3,27},{4,28},{5,29},{6,30},{7,31},{8,0},{9,1... | collective-permute-start | bytes 1572872 | tf_op jit(solution)/shard_map/ppermute | solution.py:28
  69.3 12.4 %collective-permute-start.22 = (bf16[32,8192]{1,0:T(8,128)(2,1)S(1)}, bf16[32,8192]{1,0:T(8,128)(2,1)S(1)}, u32[]{:S(2)}, u32[]{:S(2)}) collective-permute-start(bf16[32,8192]{1,0:T(8,128)(2,1)S(1)} %maximum_maximum_fusion.1), channel_id=1, source_target_pairs={{0,4},{1,5},{2,6},{3,7},{4,0},{5,1},{6,2},{7,3},{8,12},{9,13},{10,... | collective-permute-start | bytes 1572872 | tf_op jit(solution)/shard_map/ppermute | solution.py:28
  81.8 7.7 %collective-permute-start.23 = (bf16[32,4096]{1,0:T(8,128)(2,1)S(1)}, bf16[32,4096]{1,0:T(8,128)(2,1)S(1)}, u32[]{:S(2)}, u32[]{:S(2)}) collective-permute-start(bf16[32,4096]{1,0:T(8,128)(2,1)S(1)} %pad_maximum_fusion.9), channel_id=1, source_target_pairs={{0,96},{1,97},{2,98},{3,99},{4,100},{5,101},{6,102},{7,103},{8,104... | collective-permute-start | bytes 786440 | tf_op jit(solution)/shard_map/ppermute | solution.py:28
  82.8 8.2 %collective-permute-start.25 = (bf16[16,8192]{1,0:T(8,128)(2,1)S(1)}, bf16[16,8192]{1,0:T(8,128)(2,1)S(1)}, u32[]{:S(2)}, u32[]{:S(2)}) collective-permute-start(bf16[16,8192]{1,0:T(8,128)(2,1)S(1)} %pad_maximum_fusion.11), channel_id=1, source_target_pairs={{0,4},{1,5},{2,6},{3,7},{4,0},{5,1},{6,2},{7,3},{8,12},{9,13},{10,... | collective-permute-start | bytes 786440 | tf_op jit(solution)/shard_map/ppermute | solution.py:28
  (12 other events, 120.6 us)

commit v7 on v6

--- a/solution.py
+++ b/solution.py
@@ -89,10 +89,11 @@
 
 def right_kernel(here, p0, p1, p2, p3, gain, bias, weight, out, normed, swap):
     average = jnp.full((128, 128), 1 / 128, BF16)
-    for s, piece in enumerate((p0, p1, p2, p3)):
+    values = jnp.concatenate([piece[...].reshape(256, 128) for piece in (p0, p1, p2, p3)], 0)
+    made = scale(standardize(values, average), gain[...], bias[...])
+    for s in range(4):
         start = pl.multiple_of((here[0] ^ s) * 16, 16)
-        made = scale(standardize(piece[...].reshape(256, 128), average), gain[...], bias[...])
-        normed[:, pl.ds(start, 16), :] = made.reshape(16, 16, 128)
+        normed[:, pl.ds(start, 16), :] = made[s * 256 : (s + 1) * 256].reshape(16, 16, 128)
 
     def store(h, tile):
         out[:, h * 128 : (h + 1) * 128] = tile

time: 96.8 us -> 96.8 us (level)
  transfers between devices with their start and end apart: 26 -> 26, of which waited for: 7 -> 7; matrix products, arithmetic and copies ran while one was open for 1% -> 1% of each run, Pallas kernels for 37% -> 36%
where the time goes in v7:
time: 96.8 us; the launch traced here: 96.6 us
  Pallas kernels  42.2 us (44%)
  starting transfers between devices  41.4 us (43%)
  waiting for transfers between devices  10.2 us (11%)
  local copies, waits for them, and re-layouts  1.55 us (2%)
    ppermute x22, starting transfers between devices, move(): return lax.ppermute(value, AXES, pairs)  31.7 us
    pallas_call x3, Pallas kernels, run_update(): pl.pallas_call(functools.partial(update_kernel, blocks, len(sources), has...  19 us
    pallas_call x2, Pallas kernels, run_gate(): pl.pallas_call(functools.partial(gate_kernel, first, rows // 2), out_shap...  15 us
    ppermute x4, starting transfers between devices, per_device(): pieces.append(lax.ppermute(parts[s], AXES, pairs))  9.73 us
    ppermute x22, waiting for transfers between devices, move(): return lax.ppermute(value, AXES, pairs)  7.57 us
    pallas_call x1, Pallas kernels, run_left(): pl.pallas_call(left_kernel, out_shape=[jax.ShapeDtypeStruct((32, 256, 256...  5.58 us
    ppermute x4, waiting for transfers between devices, per_device(): pieces.append(lax.ppermute(parts[s], AXES, pairs))  2.68 us
  transfers between devices with their start and end apart: 26, of which 7 were waited for; matrix products, arithmetic and copies ran while one was open for 1% of the time, Pallas kernels for 36%

profile of v7, /device:TPU:0, one launch (start us, length us, event | category | flops | bytes accessed | tf_op | source)
XLA Modules:
  0.0 96.6 jit_solution(9546695426444850211)
XLA Ops:
  1.6 3.3 %collective-permute-start.1 = (bf16[16,16,128]{2,1,0:T(8,128)(2,1)S(1)}, bf16[16,16,128]{2,1,0:T(8,128)(2,1)S(1)}, u32[]{:S(2)}, u32[]{:S(2)}) collective-permute-start(bf16[16,16,128]{2,1,0:T(8,128)(2,1)S(1)} %get-tuple-element.52), channel_id=1, source_target_pairs={{0,32},{1,0},{2,96},{3,64},{4,36},{5,4},{6,100},{7,68},{8,40},{9,8... | collective-permute-start | bytes 196616 | tf_op jit(solution)/shard_map/ppermute | solution.py:416
  5.0 4.3 %collective-permute-start.2 = (bf16[16,16,128]{2,1,0:T(8,128)(2,1)S(1)}, bf16[16,16,128]{2,1,0:T(8,128)(2,1)S(1)}, u32[]{:S(2)}, u32[]{:S(2)}) collective-permute-start(bf16[16,16,128]{2,1,0:T(8,128)(2,1)S(1)} %get-tuple-element.53), channel_id=1, source_target_pairs={{0,64},{1,96},{2,0},{3,32},{4,68},{5,100},{6,4},{7,36},{8,72},{9,1... | collective-permute-start | bytes 196616 | tf_op jit(solution)/shard_map/ppermute | solution.py:416
  9.3 1.4 %collective-permute-start.3 = (bf16[16,16,128]{2,1,0:T(8,128)(2,1)S(1)}, bf16[16,16,128]{2,1,0:T(8,128)(2,1)S(1)}, u32[]{:S(2)}, u32[]{:S(2)}) collective-permute-start(bf16[16,16,128]{2,1,0:T(8,128)(2,1)S(1)} %get-tuple-element.54), channel_id=1, source_target_pairs={{0,96},{1,64},{2,32},{3,0},{4,100},{5,68},{6,36},{7,4},{8,104},{9,... | collective-permute-start | bytes 196616 | tf_op jit(solution)/shard_map/ppermute | solution.py:416
  11.9 2.1 %collective-permute-done.2.p2 = bf16[16,16,128]{2,1,0:T(8,128)(2,1)S(1)} collective-permute-done((bf16[16,16,128]{2,1,0:T(8,128)(2,1)S(1)}, bf16[16,16,128]{2,1,0:T(8,128)(2,1)S(1)}, u32[]{:S(2)}, u32[]{:S(2)}) %collective-permute-start.2) | collective-permute-done | bytes 65568 | tf_op jit(solution)/shard_map/ppermute | solution.py:416
  14.5 1.6 %shard_map.128.refs_7_ = bf16[16,8192]{1,0:T(8,128)(2,1)S(1)} custom-call(s32[4]{0:T(128)S(1)} %pad_add_fusion.here.refs_0_, bf16[16,16,128]{2,1,0:T(8,128)(2,1)S(1)} %collective-permute-done.p0, bf16[16,16,128]{2,1,0:T(8,128)(2,1)S(1)} %collective-permute-done.1.p1, bf16[16,16,128]{2,1,0:T(8,128)(2,1)S(1)} %collective-permute-done.2.p2, ...), custom_call_target="tpu_custom_call" | custom-call | tf_op jit(solution)/shard_map/pallas_call | solution.py:305
  16.2 1.6 %collective-permute-start.6 = (bf16[16,8192]{1,0:T(8,128)(2,1)S(1)}, bf16[16,8192]{1,0:T(8,128)(2,1)S(1)}, u32[]{:S(2)}, u32[]{:S(2)}) collective-permute-start(bf16[16,8192]{1,0:T(8,128)(2,1)S(1)} %shard_map.128.refs_7_), channel_id=1, source_target_pairs={{0,8},{1,9},{2,10},{3,11},{4,12},{5,13},{6,14},{7,15},{8,16},{9,17... | collective-permute-start | bytes 786440 | tf_op jit(solution)/shard_map/ppermute | solution.py:28
  17.8 3.5 %collective-permute-start.7 = (bf16[16,8192]{1,0:T(8,128)(2,1)S(1)}, bf16[16,8192]{1,0:T(8,128)(2,1)S(1)}, u32[]{:S(2)}, u32[]{:S(2)}) collective-permute-start(bf16[16,8192]{1,0:T(8,128)(2,1)S(1)} %shard_map.128.refs_7_), channel_id=1, source_target_pairs={{0,96},{1,97},{2,98},{3,99},{4,100},{5,101},{6,102},{7,103},{8,104... | collective-permute-start | bytes 786440 | tf_op jit(solution)/shard_map/ppermute | solution.py:28
  21.2 1.7 %collective-permute-start.4 = (bf16[16,8192]{1,0:T(8,128)(2,1)S(1)}, bf16[16,8192]{1,0:T(8,128)(2,1)S(1)}, u32[]{:S(2)}, u32[]{:S(2)}) collective-permute-start(bf16[16,8192]{1,0:T(8,128)(2,1)S(1)} %shard_map.128.refs_7_), channel_id=1, source_target_pairs={{0,24},{1,25},{2,26},{3,27},{4,28},{5,29},{6,30},{7,31},{8,0},{9,1... | collective-permute-start | bytes 786440 | tf_op jit(solution)/shard_map/ppermute | solution.py:28
  23.1 3.0 %collective-permute-start.10 = (bf16[16,8192]{1,0:T(8,128)(2,1)S(1)}, bf16[16,8192]{1,0:T(8,128)(2,1)S(1)}, u32[]{:S(2)}, u32[]{:S(2)}) collective-permute-start(bf16[16,8192]{1,0:T(8,128)(2,1)S(1)} %shard_map.128.refs_7_), channel_id=1, source_target_pairs={{0,4},{1,5},{2,6},{3,7},{4,0},{5,1},{6,2},{7,3},{8,12},{9,13},{10,... | collective-permute-start | bytes 786440 | tf_op jit(solution)/shard_map/ppermute | solution.py:28
  26.6 1.6 %collective-permute-start.16 = (bf16[64,16,128]{2,1,0:T(8,128)(2,1)}, bf16[64,16,128]{2,1,0:T(8,128)(2,1)S(1)}, u32[]{:S(2)}, u32[]{:S(2)}) collective-permute-start(bf16[64,16,128]{2,1,0:T(8,128)(2,1)} %param.14), channel_id=1, source_target_pairs={{0,2},{1,3},{2,0},{3,1},{4,6},{5,7},{6,4},{7,5},{8,10},{9,11},{10,... | collective-permute-start | bytes 786440 | tf_op jit(solution)/shard_map/ppermute | solution.py:28
  29.4 1.8 %collective-permute-start.5 = (bf16[16,8192]{1,0:T(8,128)(2,1)S(1)}, bf16[16,8192]{1,0:T(8,128)(2,1)S(1)}, u32[]{:S(2)}, u32[]{:S(2)}) collective-permute-start(bf16[16,8192]{1,0:T(8,128)(2,1)S(1)} %collective-permute-done.4.refs_8_), channel_id=1, source_target_pairs={{0,24},{1,25},{2,26},{3,27},{4,28},{5,29},{6,30},{7,31},{8,0},{9,1... | collective-permute-start | bytes 786440 | tf_op jit(solution)/shard_map/ppermute | solution.py:28
  31.2 6.1 %shard_map.129.refs_14_.refs_10_.refs_9_ = bf16[24,512,128]{2,1,0:T(8,128)(2,1)} custom-call(bf16[64,512,128]{2,1,0:T(8,128)(2,1)} %pair.3, bf16[256,256]{1,0:T(8,128)(2,1)S(1)} %bitcast.15, bf16[256,256]{1,0:T(8,128)(2,1)S(1)} %get-tuple-element.66.weight, f32[1,256]{1,0:T(1,128)S(1)} %get-tuple-element.67.bias), custom_call_target="tpu_custom_call" | custom-call | flops 4800000000 | bytes 1048576 | tf_op jit(solution)/shard_map/pallas_call | solution.py:345
  37.6 3.0 %collective-permute-start.15 = (bf16[32,8192]{1,0:T(8,128)(2,1)S(1)}, bf16[32,8192]{1,0:T(8,128)(2,1)S(1)}, u32[]{:S(2)}, u32[]{:S(2)}) collective-permute-start(bf16[32,8192]{1,0:T(8,128)(2,1)S(1)} %maximum_maximum_fusion), channel_id=1, source_target_pairs={{0,4},{1,5},{2,6},{3,7},{4,0},{5,1},{6,2},{7,3},{8,12},{9,13},{10,... | collective-permute-start | bytes 1572872 | tf_op jit(solution)/shard_map/ppermute | solution.py:28
  41.7 2.2 %collective-permute-start.13 = (bf16[64,4096]{1,0:T(8,128)(2,1)S(1)}, bf16[64,4096]{1,0:T(8,128)(2,1)S(1)}, u32[]{:S(2)}, u32[]{:S(2)}) collective-permute-start(bf16[64,4096]{1,0:T(8,128)(2,1)S(1)} %pad_maximum_fusion.1), channel_id=1, source_target_pairs={{0,24},{1,25},{2,26},{3,27},{4,28},{5,29},{6,30},{7,31},{8,0},{9,1... | collective-permute-start | bytes 1572872 | tf_op jit(solution)/shard_map/ppermute | solution.py:28
  45.6 8.9 %shard_map.130.refs_15_.refs_11_.refs_10_ = bf16[40,512,128]{2,1,0:T(8,128)(2,1)} custom-call(bf16[64,512,128]{2,1,0:T(8,128)(2,1)} %pair.3, bf16[256,256]{1,0:T(8,128)(2,1)S(1)} %bitcast.16, bf16[256,256]{1,0:T(8,128)(2,1)S(1)} %get-tuple-element.66.weight, f32[1,256]{1,0:T(1,128)S(1)} %get-tuple-element.67.bias), custom_call_target="tpu_custom_call" | custom-call | flops 8000000000 | bytes 1048576 | tf_op jit(solution)/shard_map/pallas_call | solution.py:345
  54.5 5.6 %shard_map.131 = (bf16[32,256,256]{2,1,0:T(8,128)(2,1)S(1)}, bf16[256,256]{1,0:T(8,128)(2,1)S(1)}, f32[1,256]{1,0:T(1,128)S(1)}) custom-call(s32[4]{0:T(128)S(1)} %pad_add_fusion.here.refs_0_, bf16[2,64,16,128]{3,2,1,0:T(8,128)(2,1)S(1)} %pad_maximum_fusion.2.left_0, bf16[2,64,16,128]{3,2,1,0:T(8,128)(2,1)S(1)} %collective-permute-done.17.left_1, ...), custom_call_target="tpu_custom_call" | custom-call | flops 4000000000 | bytes 12582912 | tf_op jit(solution)/shard_map/pallas_call | solution.py:321
  60.5 1.7 %collective-permute-done.14.refs_4_ = bf16[80,4096]{1,0:T(8,128)(2,1)S(1)} collective-permute-done((bf16[80,4096]{1,0:T(8,128)(2,1)S(1)}, bf16[80,4096]{1,0:T(8,128)(2,1)S(1)}, u32[]{:S(2)}, u32[]{:S(2)}) %collective-permute-start.14) | collective-permute-done | bytes 655392 | tf_op jit(solution)/shard_map/ppermute | solution.py:28
  62.9 2.9 %collective-permute-start.18 = (bf16[64,4096]{1,0:T(8,128)(2,1)S(1)}, bf16[64,4096]{1,0:T(8,128)(2,1)S(1)}, u32[]{:S(2)}, u32[]{:S(2)}) collective-permute-start(bf16[64,4096]{1,0:T(8,128)(2,1)S(1)} %get-tuple-element.108), channel_id=1, source_target_pairs={{0,96},{1,97},{2,98},{3,99},{4,100},{5,101},{6,102},{7,103},{8,104... | collective-permute-start | bytes 1572872 | tf_op jit(solution)/shard_map/ppermute | solution.py:28
  66.0 3.2 %collective-permute-start.20 = (bf16[64,4096]{1,0:T(8,128)(2,1)S(1)}, bf16[64,4096]{1,0:T(8,128)(2,1)S(1)}, u32[]{:S(2)}, u32[]{:S(2)}) collective-permute-start(bf16[64,4096]{1,0:T(8,128)(2,1)S(1)} %get-tuple-element.106), channel_id=1, source_target_pairs={{0,24},{1,25},{2,26},{3,27},{4,28},{5,29},{6,30},{7,31},{8,0},{9,1... | collective-permute-start | bytes 1572872 | tf_op jit(solution)/shard_map/ppermute | solution.py:28
  70.1 8.2 %shard_map.132.refs_15_ = bf16[64,512,128]{2,1,0:T(8,128)(2,1)} custom-call(s32[4]{0:T(128)S(1)} %pad_add_fusion.here.refs_0_, bf16[64,4096]{1,0:T(8,128)(2,1)S(1)} %collective-permute-done.11.refs_1_, bf16[80,4096]{1,0:T(8,128)(2,1)S(1)} %collective-permute-done.12.refs_2_, bf16[64,4096]{1,0:T(8,128)(2,1)S(1)} %collective-permute-done.13.refs_3_, ...), custom_call_target="tpu_custom_call" | custom-call | flops 6400000000 | bytes 16777216 | tf_op jit(solution)/shard_map/pallas_call | solution.py:263
  78.3 3.3 %collective-permute-done.22.refs_7_ = bf16[32,8192]{1,0:T(8,128)(2,1)S(1)} collective-permute-done((bf16[32,8192]{1,0:T(8,128)(2,1)S(1)}, bf16[32,8192]{1,0:T(8,128)(2,1)S(1)}, u32[]{:S(2)}, u32[]{:S(2)}) %collective-permute-start.22) | collective-permute-done | bytes 524320 | tf_op jit(solution)/shard_map/ppermute | solution.py:28
  84.0 5.4 %shard_map.133.refs_14_ = bf16[64,512,128]{2,1,0:T(8,128)(2,1)} custom-call(s32[4]{0:T(128)S(1)} %pad_add_fusion.here.refs_0_, bf16[64,4096]{1,0:T(8,128)(2,1)S(1)} %collective-permute-done.11.refs_1_, bf16[80,4096]{1,0:T(8,128)(2,1)S(1)} %collective-permute-done.12.refs_2_, ...), custom_call_target="tpu_custom_call", output_to_operand_aliasing={{}: (15, {})} | custom-call | flops 3200000000 | bytes 8388608 | tf_op jit(solution)/shard_map/pallas_call | solution.py:263
  89.4 1.6 %collective-permute-done.25.refs_8_ = bf16[16,8192]{1,0:T(8,128)(2,1)S(1)} collective-permute-done((bf16[16,8192]{1,0:T(8,128)(2,1)S(1)}, bf16[16,8192]{1,0:T(8,128)(2,1)S(1)}, u32[]{:S(2)}, u32[]{:S(2)}) %collective-permute-start.25) | collective-permute-done | bytes 262176 | tf_op jit(solution)/shard_map/ppermute | solution.py:28
  91.1 5.4 %shard_map.134 = bf16[64,512,128]{2,1,0:T(8,128)(2,1)} custom-call(s32[4]{0:T(128)S(1)} %pad_add_fusion.here.refs_0_, bf16[64,4096]{1,0:T(8,128)(2,1)S(1)} %collective-permute-done.19.refs_6_.refs_1_, bf16[64,4096]{1,0:T(8,128)(2,1)S(1)} %collective-permute-done.20.refs_7_.refs_2_, ...), custom_call_target="tpu_custom_call", output_to_operand_aliasing={{}: (14, {})} | custom-call | flops 3200000000 | bytes 8388608 | tf_op jit(solution)/shard_map/pallas_call | solution.py:263
  (95 shorter events, 12.6 us)
Async XLA Ops:
  1.0 10.9 %collective-permute-start = (bf16[16,16,128]{2,1,0:T(8,128)(2,1)S(1)}, bf16[16,16,128]{2,1,0:T(8,128)(2,1)S(1)}, u32[]{:S(2)}, u32[]{:S(2)}) collective-permute-start(bf16[16,16,128]{2,1,0:T(8,128)(2,1)S(1)} %get-tuple-element.51), channel_id=1, source_target_pairs={{0,0},{1,32},{2,64},{3,96},{4,4},{5,36},{6,68},{7,100},{8,8},{9,40... | collective-permute-start | bytes 196616 | tf_op jit(solution)/shard_map/ppermute | solution.py:416
  1.6 10.2 %collective-permute-start.1 = (bf16[16,16,128]{2,1,0:T(8,128)(2,1)S(1)}, bf16[16,16,128]{2,1,0:T(8,128)(2,1)S(1)}, u32[]{:S(2)}, u32[]{:S(2)}) collective-permute-start(bf16[16,16,128]{2,1,0:T(8,128)(2,1)S(1)} %get-tuple-element.52), channel_id=1, source_target_pairs={{0,32},{1,0},{2,96},{3,64},{4,36},{5,4},{6,100},{7,68},{8,40},{9,8... | collective-permute-start | bytes 196616 | tf_op jit(solution)/shard_map/ppermute | solution.py:416
  5.0 9.0 %collective-permute-start.2 = (bf16[16,16,128]{2,1,0:T(8,128)(2,1)S(1)}, bf16[16,16,128]{2,1,0:T(8,128)(2,1)S(1)}, u32[]{:S(2)}, u32[]{:S(2)}) collective-permute-start(bf16[16,16,128]{2,1,0:T(8,128)(2,1)S(1)} %get-tuple-element.53), channel_id=1, source_target_pairs={{0,64},{1,96},{2,0},{3,32},{4,68},{5,100},{6,4},{7,36},{8,72},{9,1... | collective-permute-start | bytes 196616 | tf_op jit(solution)/shard_map/ppermute | solution.py:416
  16.2 10.4 %collective-permute-start.6 = (bf16[16,8192]{1,0:T(8,128)(2,1)S(1)}, bf16[16,8192]{1,0:T(8,128)(2,1)S(1)}, u32[]{:S(2)}, u32[]{:S(2)}) collective-permute-start(bf16[16,8192]{1,0:T(8,128)(2,1)S(1)} %shard_map.128.refs_7_), channel_id=1, source_target_pairs={{0,8},{1,9},{2,10},{3,11},{4,12},{5,13},{6,14},{7,15},{8,16},{9,17... | collective-permute-start | bytes 786440 | tf_op jit(solution)/shard_map/ppermute | solution.py:28
  17.8 10.4 %collective-permute-start.7 = (bf16[16,8192]{1,0:T(8,128)(2,1)S(1)}, bf16[16,8192]{1,0:T(8,128)(2,1)S(1)}, u32[]{:S(2)}, u32[]{:S(2)}) collective-permute-start(bf16[16,8192]{1,0:T(8,128)(2,1)S(1)} %shard_map.128.refs_7_), channel_id=1, source_target_pairs={{0,96},{1,97},{2,98},{3,99},{4,100},{5,101},{6,102},{7,103},{8,104... | collective-permute-start | bytes 786440 | tf_op jit(solution)/shard_map/ppermute | solution.py:28
  21.2 8.1 %collective-permute-start.4 = (bf16[16,8192]{1,0:T(8,128)(2,1)S(1)}, bf16[16,8192]{1,0:T(8,128)(2,1)S(1)}, u32[]{:S(2)}, u32[]{:S(2)}) collective-permute-start(bf16[16,8192]{1,0:T(8,128)(2,1)S(1)} %shard_map.128.refs_7_), channel_id=1, source_target_pairs={{0,24},{1,25},{2,26},{3,27},{4,28},{5,29},{6,30},{7,31},{8,0},{9,1... | collective-permute-start | bytes 786440 | tf_op jit(solution)/shard_map/ppermute | solution.py:28
  23.1 14.4 %collective-permute-start.10 = (bf16[16,8192]{1,0:T(8,128)(2,1)S(1)}, bf16[16,8192]{1,0:T(8,128)(2,1)S(1)}, u32[]{:S(2)}, u32[]{:S(2)}) collective-permute-start(bf16[16,8192]{1,0:T(8,128)(2,1)S(1)} %shard_map.128.refs_7_), channel_id=1, source_target_pairs={{0,4},{1,5},{2,6},{3,7},{4,0},{5,1},{6,2},{7,3},{8,12},{9,13},{10,... | collective-permute-start | bytes 786440 | tf_op jit(solution)/shard_map/ppermute | solution.py:28
  26.0 11.4 %collective-permute-start.9 = (bf16[16,8192]{1,0:T(8,128)(2,1)S(1)}, bf16[16,8192]{1,0:T(8,128)(2,1)S(1)}, u32[]{:S(2)}, u32[]{:S(2)}) collective-permute-start(bf16[16,8192]{1,0:T(8,128)(2,1)S(1)} %shard_map.128.refs_7_), channel_id=1, source_target_pairs={{0,32},{1,33},{2,34},{3,35},{4,36},{5,37},{6,38},{7,39},{8,40},{9,... | collective-permute-start | bytes 786440 | tf_op jit(solution)/shard_map/ppermute | solution.py:28
  26.6 10.7 %collective-permute-start.16 = (bf16[64,16,128]{2,1,0:T(8,128)(2,1)}, bf16[64,16,128]{2,1,0:T(8,128)(2,1)S(1)}, u32[]{:S(2)}, u32[]{:S(2)}) collective-permute-start(bf16[64,16,128]{2,1,0:T(8,128)(2,1)} %param.14), channel_id=1, source_target_pairs={{0,2},{1,3},{2,0},{3,1},{4,6},{5,7},{6,4},{7,5},{8,10},{9,11},{10,... | collective-permute-start | bytes 786440 | tf_op jit(solution)/shard_map/ppermute | solution.py:28
  28.2 9.3 %collective-permute-start.8 = (bf16[16,8192]{1,0:T(8,128)(2,1)S(1)}, bf16[16,8192]{1,0:T(8,128)(2,1)S(1)}, u32[]{:S(2)}, u32[]{:S(2)}) collective-permute-start(bf16[16,8192]{1,0:T(8,128)(2,1)S(1)} %collective-permute-done.7.refs_11_), channel_id=1, source_target_pairs={{0,96},{1,97},{2,98},{3,99},{4,100},{5,101},{6,102},{7,103},{8,104... | collective-permute-start | bytes 786440 | tf_op jit(solution)/shard_map/ppermute | solution.py:28
  29.4 8.1 %collective-permute-start.5 = (bf16[16,8192]{1,0:T(8,128)(2,1)S(1)}, bf16[16,8192]{1,0:T(8,128)(2,1)S(1)}, u32[]{:S(2)}, u32[]{:S(2)}) collective-permute-start(bf16[16,8192]{1,0:T(8,128)(2,1)S(1)} %collective-permute-done.4.refs_8_), channel_id=1, source_target_pairs={{0,24},{1,25},{2,26},{3,27},{4,28},{5,29},{6,30},{7,31},{8,0},{9,1... | collective-permute-start | bytes 786440 | tf_op jit(solution)/shard_map/ppermute | solution.py:28
  37.4 7.9 %collective-permute-start.17 = (bf16[2,64,16,128]{3,2,1,0:T(8,128)(2,1)S(1)}, bf16[2,64,16,128]{3,2,1,0:T(8,128)(2,1)S(1)}, u32[]{:S(2)}, u32[]{:S(2)}) collective-permute-start(bf16[2,64,16,128]{3,2,1,0:T(8,128)(2,1)S(1)} %pad_maximum_fusion.2.left_0), channel_id=1, source_target_pairs={{0,1},{1,0},{2,3},{3,2},{4,5},{5,4},{6,7},{7,6},{8,9},{9,8},{10,11... | collective-permute-start | bytes 1572872 | tf_op jit(solution)/shard_map/ppermute | solution.py:28
  37.6 22.5 %collective-permute-start.15 = (bf16[32,8192]{1,0:T(8,128)(2,1)S(1)}, bf16[32,8192]{1,0:T(8,128)(2,1)S(1)}, u32[]{:S(2)}, u32[]{:S(2)}) collective-permute-start(bf16[32,8192]{1,0:T(8,128)(2,1)S(1)} %maximum_maximum_fusion), channel_id=1, source_target_pairs={{0,4},{1,5},{2,6},{3,7},{4,0},{5,1},{6,2},{7,3},{8,12},{9,13},{10,... | collective-permute-start | bytes 1572872 | tf_op jit(solution)/shard_map/ppermute | solution.py:28
  40.7 19.4 %collective-permute-start.11 = (bf16[64,4096]{1,0:T(8,128)(2,1)S(1)}, bf16[64,4096]{1,0:T(8,128)(2,1)S(1)}, u32[]{:S(2)}, u32[]{:S(2)}) collective-permute-start(bf16[64,4096]{1,0:T(8,128)(2,1)S(1)} %pad_maximum_fusion), channel_id=1, source_target_pairs={{0,96},{1,97},{2,98},{3,99},{4,100},{5,101},{6,102},{7,103},{8,104... | collective-permute-start | bytes 1572872 | tf_op jit(solution)/shard_map/ppermute | solution.py:28
  41.7 18.4 %collective-permute-start.13 = (bf16[64,4096]{1,0:T(8,128)(2,1)S(1)}, bf16[64,4096]{1,0:T(8,128)(2,1)S(1)}, u32[]{:S(2)}, u32[]{:S(2)}) collective-permute-start(bf16[64,4096]{1,0:T(8,128)(2,1)S(1)} %pad_maximum_fusion.1), channel_id=1, source_target_pairs={{0,24},{1,25},{2,26},{3,27},{4,28},{5,29},{6,30},{7,31},{8,0},{9,1... | collective-permute-start | bytes 1572872 | tf_op jit(solution)/shard_map/ppermute | solution.py:28
  44.0 16.5 %collective-permute-start.12 = (bf16[80,4096]{1,0:T(8,128)(2,1)S(1)}, bf16[80,4096]{1,0:T(8,128)(2,1)S(1)}, u32[]{:S(2)}, u32[]{:S(2)}) collective-permute-start(bf16[80,4096]{1,0:T(8,128)(2,1)S(1)} %constant_dynamic-update-slice_fusion), channel_id=1, source_target_pairs={{0,32},{1,33},{2,34},{3,35},{4,36},{5,37},{6,38},{7,39},{8,40},{9,... | collective-permute-start | bytes 1966088 | tf_op jit(solution)/shard_map/ppermute | solution.py:28
  45.3 16.9 %collective-permute-start.14 = (bf16[80,4096]{1,0:T(8,128)(2,1)S(1)}, bf16[80,4096]{1,0:T(8,128)(2,1)S(1)}, u32[]{:S(2)}, u32[]{:S(2)}) collective-permute-start(bf16[80,4096]{1,0:T(8,128)(2,1)S(1)} %get-tuple-element.109), channel_id=1, source_target_pairs={{0,8},{1,9},{2,10},{3,11},{4,12},{5,13},{6,14},{7,15},{8,16},{9,17... | collective-permute-start | bytes 1966088 | tf_op jit(solution)/shard_map/ppermute | solution.py:28
  62.5 15.8 %collective-permute-start.19 = (bf16[64,4096]{1,0:T(8,128)(2,1)S(1)}, bf16[64,4096]{1,0:T(8,128)(2,1)S(1)}, u32[]{:S(2)}, u32[]{:S(2)}) collective-permute-start(bf16[64,4096]{1,0:T(8,128)(2,1)S(1)} %get-tuple-element.107), channel_id=1, source_target_pairs={{0,32},{1,33},{2,34},{3,35},{4,36},{5,37},{6,38},{7,39},{8,40},{9,... | collective-permute-start | bytes 1572872 | tf_op jit(solution)/shard_map/ppermute | solution.py:28
  62.9 15.4 %collective-permute-start.18 = (bf16[64,4096]{1,0:T(8,128)(2,1)S(1)}, bf16[64,4096]{1,0:T(8,128)(2,1)S(1)}, u32[]{:S(2)}, u32[]{:S(2)}) collective-permute-start(bf16[64,4096]{1,0:T(8,128)(2,1)S(1)} %get-tuple-element.108), channel_id=1, source_target_pairs={{0,96},{1,97},{2,98},{3,99},{4,100},{5,101},{6,102},{7,103},{8,104... | collective-permute-start | bytes 1572872 | tf_op jit(solution)/shard_map/ppermute | solution.py:28
  65.9 12.4 %collective-permute-start.21 = (bf16[64,4096]{1,0:T(8,128)(2,1)S(1)}, bf16[64,4096]{1,0:T(8,128)(2,1)S(1)}, u32[]{:S(2)}, u32[]{:S(2)}) collective-permute-start(bf16[64,4096]{1,0:T(8,128)(2,1)S(1)} %get-tuple-element.105), channel_id=1, source_target_pairs={{0,8},{1,9},{2,10},{3,11},{4,12},{5,13},{6,14},{7,15},{8,16},{9,17... | collective-permute-start | bytes 1572872 | tf_op jit(solution)/shard_map/ppermute | solution.py:28
  66.0 12.4 %collective-permute-start.20 = (bf16[64,4096]{1,0:T(8,128)(2,1)S(1)}, bf16[64,4096]{1,0:T(8,128)(2,1)S(1)}, u32[]{:S(2)}, u32[]{:S(2)}) collective-permute-start(bf16[64,4096]{1,0:T(8,128)(2,1)S(1)} %get-tuple-element.106), channel_id=1, source_target_pairs={{0,24},{1,25},{2,26},{3,27},{4,28},{5,29},{6,30},{7,31},{8,0},{9,1... | collective-permute-start | bytes 1572872 | tf_op jit(solution)/shard_map/ppermute | solution.py:28
  69.3 12.4 %collective-permute-start.22 = (bf16[32,8192]{1,0:T(8,128)(2,1)S(1)}, bf16[32,8192]{1,0:T(8,128)(2,1)S(1)}, u32[]{:S(2)}, u32[]{:S(2)}) collective-permute-start(bf16[32,8192]{1,0:T(8,128)(2,1)S(1)} %maximum_maximum_fusion.1), channel_id=1, source_target_pairs={{0,4},{1,5},{2,6},{3,7},{4,0},{5,1},{6,2},{7,3},{8,12},{9,13},{10,... | collective-permute-start | bytes 1572872 | tf_op jit(solution)/shard_map/ppermute | solution.py:28
  81.7 7.7 %collective-permute-start.23 = (bf16[32,4096]{1,0:T(8,128)(2,1)S(1)}, bf16[32,4096]{1,0:T(8,128)(2,1)S(1)}, u32[]{:S(2)}, u32[]{:S(2)}) collective-permute-start(bf16[32,4096]{1,0:T(8,128)(2,1)S(1)} %pad_maximum_fusion.9), channel_id=1, source_target_pairs={{0,96},{1,97},{2,98},{3,99},{4,100},{5,101},{6,102},{7,103},{8,104... | collective-permute-start | bytes 786440 | tf_op jit(solution)/shard_map/ppermute | solution.py:28
  82.8 8.2 %collective-permute-start.25 = (bf16[16,8192]{1,0:T(8,128)(2,1)S(1)}, bf16[16,8192]{1,0:T(8,128)(2,1)S(1)}, u32[]{:S(2)}, u32[]{:S(2)}) collective-permute-start(bf16[16,8192]{1,0:T(8,128)(2,1)S(1)} %pad_maximum_fusion.11), channel_id=1, source_target_pairs={{0,4},{1,5},{2,6},{3,7},{4,0},{5,1},{6,2},{7,3},{8,12},{9,13},{10,... | collective-permute-start | bytes 786440 | tf_op jit(solution)/shard_map/ppermute | solution.py:28
  (12 other events, 120.6 us)
